TPU v7x, 32 devices: a whole 2x2x4 slice. The times are simulated.
32 devices in a mesh: layer: 4 (over y, core), grid: 8 (over z, x).
Axes of the slice: x: 2, y: 2, z: 4, core: 2. Of those that a mesh axis runs over, the one named last changes fastest.
Arguments:
- l_panels: bfloat16 [4, 2, 8192, 512], P('layer', None, 'grid'), may hold values from -6 to 6
- u_panels: bfloat16 [4, 2, 512, 512], P('layer', None, 'grid'), may hold values from -0.046875 to 0.046875
- panel_fill: int32 [4, 2, 64, 4], P('layer', None, 'grid'), may hold values 0 or 1
- copy_fill: int32 [4, 64, 4], P('layer', 'grid'), may hold values 0 or 1
- sep_panels: bfloat16 [3, 8192, 256], P(None, 'grid'), may hold values from -0.25 to 0.25
- sep_owner: int32 [3], replicated, may hold values from 0 to 7
Outputs:
- schur: float32 [8192, 512], P('grid', 'layer')
All inputs are finite; a program needn't handle non-finite values. No bound on the sum of `panel_fill` or of `copy_fill` on one device may be relied on, other than what follows from the above.
Results may differ from a plain program's by a relative error of at most 0.0035.
Values may be sent and summed in bfloat16 or wider, within the bound.
No kernel may reach another device: no remote copies, remote signals or barrier semaphores. Data moves between devices by JAX's collectives and lax.ppermute only.
A program may use at most 64 MiB of HBM per device.

v0:
```python
import jax
import jax.numpy as jnp
from jax import lax
from jax.sharding import PartitionSpec as P

BLOCK = 128
WS = 256


def from_partner(x, axis, apart):
    return lax.ppermute(x, axis, [(i, i ^ 1 << apart) for i in range(lax.axis_size(axis))])


def spread(x, axis, root):
    mine = lax.axis_index(axis) == root
    return lax.psum(jnp.where(mine, x, jnp.zeros_like(x)), axis)


def local(l_panels, u_panels, panel_fill, copy_fill, sep_panels, sep_owner):
    panel_count = l_panels.shape[1]
    row_count = l_panels.shape[2]
    panel_width = l_panels.shape[3]
    columns = u_panels.shape[3]
    fill_panel = panel_fill[0].astype(jnp.bfloat16)
    masked = (
        l_panels[0].reshape(panel_count, row_count // BLOCK, BLOCK, panel_width // BLOCK, BLOCK)
        * fill_panel[:, :, None, :, None]
    ).reshape(panel_count, row_count, panel_width)
    running = jnp.zeros((row_count, columns), jnp.float32)
    piece = lax.all_gather(u_panels, "grid", axis=2, tiled=True)
    for k in range(panel_count):
        column_part = masked[k]
        running = running + jnp.dot(column_part, piece[0, k], preferred_element_type=jnp.float32)
    fill_copy = copy_fill[0].astype(jnp.float32)
    layer_copy = -(
        running.reshape(row_count // BLOCK, BLOCK, columns // BLOCK, BLOCK)
        * fill_copy[:, None, :, None]
    ).reshape(row_count, columns)
    layers = lax.axis_size("layer")
    level_count = layers.bit_length() - 1
    layer_index = lax.axis_index("layer")
    column_width = columns // layers
    combined = layer_copy
    for level_index in range(level_count):
        partner = from_partner(combined, "layer", level_index)
        combined = combined + partner
        node_index = layers - (layers >> level_index) + (layer_index >> level_index + 1)
        owner_index = sep_owner[node_index]
        pivot_rows = spread(combined[:WS].astype(jnp.bfloat16), "grid", owner_index)
        factor = lax.dynamic_index_in_dim(sep_panels, node_index, 0, keepdims=False)
        combined = combined - jnp.dot(factor, pivot_rows, preferred_element_type=jnp.float32)
    return lax.dynamic_slice_in_dim(combined, layer_index * column_width, column_width, 1)


def solution(mesh):
    return jax.shard_map(
        local,
        mesh=mesh,
        in_specs=(
            P("layer", None, "grid", None),
            P("layer", None, "grid", None),
            P("layer", None, "grid", None),
            P("layer", "grid", None),
            P(None, "grid", None),
            P(),
        ),
        out_specs=P("grid", "layer"),
        check_vma=False,
    )
```

profile of v0, /device:TPU:0, one launch (start us, length us, event | category | flops | bytes accessed | tf_op | source)
XLA Modules:
  0.0 269.6 jit_solution(16208585174442768612)
XLA Ops:
  6.5 0.0 copy-start
  6.5 0.0 all-gather.2.cloned.1.call-start
  6.5 0.7 all-gather.2.cloned.1.call-update
  7.3 0.0 copy-start.4
  7.3 0.0 copy-start.6
  7.3 0.0 all-reduce.3.cloned.1.call-start
  7.3 4.0 %reshape_squeeze.3 = bf16[2,8,128,4,128]{4,3,2,1,0:T(4,128)(2,1)} reshape(bf16[1,2,1024,512]{3,2,1,0:T(8,128)(2,1)} %param.6) | data formatting | bytes 4194304 | tf_op jit(solution)/shard_map/reshape;squeeze | solution.py:26
  11.3 0.0 copy-done.4
  11.3 0.1 copy.7
  11.4 0.0 copy-done.6
  11.4 0.1 copy.8
  11.5 2.6 broadcast_multiply_fusion
  14.1 1.9 fusion.15
  16.0 36.5 %all-gather.2.cloned.1.call-done = bf16[1,2,512,512]{3,2,1,0:T(8,128)(2,1)} async-done(((bf16[1,2,64,512]{3,2,1,0:T(8,128)(2,1)}), bf16[1,2,512,512]{3,2,1,0:T(8,128)(2,1)}) %all-gather.2.cloned.1.call-update) | async-done | bytes 1048592 | tf_op jit(solution)/shard_map/all_gather | solution.py:30
  52.5 0.0 copy-start.3
  52.5 2.1 fusion.3
  54.6 0.3 mul.24
  55.0 0.0 copy-done.3
  55.0 0.0 copy-start.5
  55.0 2.1 fusion
  57.0 0.0 collective-permute-start
  57.0 0.0 copy-done.5
  57.1 0.6 fusion.16
  58.3 3.3 %collective-permute-done = f32[1024,512]{1,0:T(8,128)} collective-permute-done((f32[1024,512]{1,0:T(8,128)}, f32[1024,512]{1,0:T(8,128)}, u32[]{:S(2)}, u32[]{:S(2)}) %collective-permute-start) | collective-permute-done | bytes 2097184 | tf_op jit(solution)/shard_map/ppermute | solution.py:11
  61.5 2.7 %add.31 = f32[1024,512]{1,0:T(8,128)S(1)} add(f32[1024,512]{1,0:T(8,128)} %fusion, f32[1024,512]{1,0:T(8,128)} %collective-permute-done) | non-fusion elementwise | flops 524288 | bytes 6291456 | tf_op jit(solution)/shard_map/add | solution.py:46
  64.3 0.0 copy-start.1
  64.3 1.3 copy-done.1
  65.6 0.7 fusion.11
  66.3 0.0 all-reduce.3.cloned.1.call-update
  66.3 0.0 all-reduce.5.cloned.1.call-start
  66.4 69.4 %all-reduce.3.cloned.1.call-done = bf16[256,512]{1,0:T(8,128)(2,1)} async-done(((bf16[256,512]{1,0:T(8,128)(2,1)}), bf16[256,512]{1,0:T(8,128)(2,1)}) %all-reduce.3.cloned.1.call-update) | async-done | bytes 262160 | tf_op jit(solution)/shard_map/psum | solution.py:16
  135.8 0.0 copy-done
  135.8 3.5 %convolution_subtract_fusion = f32[1024,512]{1,0:T(8,128)} fusion(f32[1024,512]{1,0:T(8,128)} %copy-done.1, bf16[256,512]{1,0:T(8,128)(2,1)} %all-reduce.3.cloned.1.call-done, bf16[3,1024,256]{2,1,0:T(8,128)(2,1)S(1)} %copy-done, s32[]{:T(128)S(6)} %select_n.26), kind=kOutput, calls=%fused_computation.2 | convolution fusion | flops 268959744 | bytes 4980740 | tf_op jit(solution)/shard_map/dot_general | solution.py:51
  139.3 1.5 collective-permute-start.1
  141.3 43.8 %collective-permute-done.1 = f32[1024,512]{1,0:T(8,128)} collective-permute-done((f32[1024,512]{1,0:T(8,128)}, f32[1024,512]{1,0:T(8,128)}, u32[]{:S(2)}, u32[]{:S(2)}) %collective-permute-start.1) | collective-permute-done | bytes 2097184 | tf_op jit(solution)/shard_map/ppermute | solution.py:11
  185.2 2.7 %add.33 = f32[1024,512]{1,0:T(8,128)S(1)} add(f32[1024,512]{1,0:T(8,128)} %convolution_subtract_fusion, f32[1024,512]{1,0:T(8,128)} %collective-permute-done.1) | non-fusion elementwise | flops 524288 | bytes 6291456 | tf_op jit(solution)/shard_map/add | solution.py:46
  187.9 0.0 copy-start.2
  187.9 1.3 copy-done.2
  189.2 0.7 fusion.12
  189.9 0.0 all-reduce.5.cloned.1.call-update
  190.0 69.8 %all-reduce.5.cloned.1.call-done = bf16[256,512]{1,0:T(8,128)(2,1)} async-done(((bf16[256,512]{1,0:T(8,128)(2,1)}), bf16[256,512]{1,0:T(8,128)(2,1)}) %all-reduce.5.cloned.1.call-update) | async-done | bytes 262160 | tf_op jit(solution)/shard_map/psum | solution.py:16
  259.7 1.4 fusion.6
  261.1 1.9 dynamic-slice_subtract_fusion
  (2 shorter events, 0.0 us)
Async XLA Ops:
  6.5 129.3 %copy-start = (bf16[3,1024,256]{2,1,0:T(8,128)(2,1)S(1)}, bf16[3,1024,256]{2,1,0:T(8,128)(2,1)}, u32[]{:S(2)}) copy-start(bf16[3,1024,256]{2,1,0:T(8,128)(2,1)} %param.10) | copy-start | bytes 4718596
  6.5 45.9 %all-gather.2.cloned.1.call-start = ((), (), s32[]{:S(2)}) async-start(), calls=%async_computation | async-start | bytes 1179648 | tf_op jit(solution)/shard_map/all_gather | solution.py:30
  7.3 4.0 %copy-start.4 = (s32[1,2,8,4]{2,3,1,0:T(4,128)S(1)}, s32[1,2,8,4]{2,3,1,0:T(4,128)}, u32[]{:S(2)}) copy-start(s32[1,2,8,4]{2,3,1,0:T(4,128)} %param.8) | copy-start | bytes 772
  7.3 4.1 %copy-start.6 = (s32[1,8,4]{1,2,0:T(4,128)S(1)}, s32[1,8,4]{1,2,0:T(4,128)}, u32[]{:S(2)}) copy-start(s32[1,8,4]{1,2,0:T(4,128)} %param.9) | copy-start | bytes 388
  7.3 128.5 %all-reduce.3.cloned.1.call-start = ((), (), s32[]{:S(2)}) async-start(), calls=%async_computation.1 | async-start | bytes 524288 | tf_op jit(solution)/shard_map/psum | solution.py:16
  52.5 2.5 copy-start.3
  55.0 2.1 copy-start.5
  57.0 4.5 %collective-permute-start = (f32[1024,512]{1,0:T(8,128)}, f32[1024,512]{1,0:T(8,128)}, u32[]{:S(2)}, u32[]{:S(2)}) collective-permute-start(f32[1024,512]{1,0:T(8,128)} %fusion), channel_id=1, source_target_pairs={{0,8},{8,0},{16,24},{24,16},{1,9},{9,1},{17,25},{25,17},{2,10},{10... | collective-permute-start | bytes 6291464 | tf_op jit(solution)/shard_map/ppermute | solution.py:11
  64.3 1.3 copy-start.1
  66.3 193.4 %all-reduce.5.cloned.1.call-start = ((), (), s32[]{:S(2)}) async-start(), calls=%async_computation.2 | async-start | bytes 524288 | tf_op jit(solution)/shard_map/psum | solution.py:16
  139.3 45.9 %collective-permute-start.1 = (f32[1024,512]{1,0:T(8,128)}, f32[1024,512]{1,0:T(8,128)}, u32[]{:S(2)}, u32[]{:S(2)}) collective-permute-start(f32[1024,512]{1,0:T(8,128)} %convolution_subtract_fusion), channel_id=1, source_target_pairs={{0,16},{8,24},{16,0},{24,8},{1,17},{9,25},{17,1},{25,9},{2,18},{10... | collective-permute-start | bytes 6291464 | tf_op jit(solution)/shard_map/ppermute | solution.py:11
  187.9 1.3 copy-start.2
Sparse Core Ops, SparseCore 0:
  9.5 42.8 all-gather.1
  66.4 69.3 all-reduce.2
  190.1 69.5 all-reduce.4
where the time goes:
time: 270 us
  waiting for transfers between devices  224 us (83%)
  between operations  14.4 us (5%)
  other arithmetic  11.4 us (4%)
  local copies, waits for them, and re-layouts  9.67 us (4%)
  matrix products  9.05 us (3%)
    psum x2, waiting for transfers between devices, spread(): return lax.psum(jnp.where(mine, x, jnp.zeros_like(x)), axis)  139 us
    ppermute x2, waiting for transfers between devices, from_partner(): lax.ppermute(x, axis, [(i, i ^ 1 << apart) for i in range(lax.axis_size(a...  47.1 us
    all_gather x1, waiting for transfers between devices, local(): piece = lax.all_gather(u_panels, 'grid', axis=2, tiled=True)  36.5 us
  transfers between devices with their start and end apart: 5, of which 5 were waited for; matrix products, arithmetic and copies ran while one was open for 3% of the time, Pallas kernels for 0%

commit v1 on v0

v1 whole, which is shorter than its diff:
```python
import jax
import jax.numpy as jnp
from jax import lax
from jax.experimental import pallas as pl
from jax.experimental.pallas import tpu as pltpu
from jax.sharding import PartitionSpec as P

BLOCK = 128
WS = 256
BOTH = ("layer", "grid")
VMEM = pl.BlockSpec(memory_space=pltpu.VMEM)
SMEM = pl.BlockSpec(memory_space=pltpu.SMEM)


def kernel_call(body, out_shape, in_specs, scratch=(), flops=0, nbytes=0):
    many = isinstance(out_shape, (tuple, list))
    return pl.pallas_call(
        body,
        out_shape=out_shape,
        in_specs=in_specs,
        out_specs=[VMEM] * len(out_shape) if many else VMEM,
        scratch_shapes=list(scratch),
        compiler_params=pltpu.CompilerParams(vmem_limit_bytes=40 << 20),
        cost_estimate=pl.CostEstimate(flops=flops, bytes_accessed=nbytes, transcendentals=0),
    )


def apart(x, axis, distance):
    return lax.ppermute(x, axis, [(i, i ^ distance) for i in range(lax.axis_size(axis))])


def gather_grid(x):
    count = lax.axis_size("grid")
    found = [x] + [None] * (count - 1)
    for k in range(2, count, 2):
        found[k] = apart(x, "grid", k)
    for k in range(0, count, 2):
        found[k + 1] = apart(found[k], "grid", 1)
    return found


def mask_panels(l_panels, panel_fill):
    _, panels, rows, width = l_panels.shape

    def body(l_ref, fill_ref, out_ref):
        for k in range(panels):
            for b in range(rows // BLOCK):
                for j in range(width // BLOCK):
                    r = slice(b * BLOCK, (b + 1) * BLOCK)
                    here = fill_ref[0, k, b, j] != 0
                    tile = l_ref[0, k, r, j * BLOCK : (j + 1) * BLOCK]
                    at = k * width + j * BLOCK
                    out_ref[r, at : at + BLOCK] = jnp.where(here, tile, jnp.zeros_like(tile))

    return kernel_call(
        body,
        jax.ShapeDtypeStruct((rows, panels * width), jnp.bfloat16),
        [VMEM, SMEM],
        nbytes=4 * panels * rows * width,
    )(l_panels, panel_fill)


def layer_copy(masked, pieces, copy_fill, place):
    rows, depth = masked.shape
    _, panels, share, columns = pieces[0].shape
    layers, grids = lax.axis_size("layer"), lax.axis_size("grid")
    width = columns // layers
    piece_rows = WS // grids
    step = min(rows, 256)

    def body(*refs):
        place_ref, fill_ref, l_ref = refs[:3]
        u_refs = refs[3 : 3 + grids]
        keep_ref, send_ref, pivot_ref, u_all = refs[3 + grids :]
        core, me = place_ref[0], place_ref[1]
        for k in range(grids):
            for p in range(panels):
                at = pl.multiple_of((p * grids + (me ^ k)) * share, share)
                u_all[pl.ds(at, share), :] = u_refs[k][0, p]
        for r in range(0, rows, step):
            part = jnp.dot(l_ref[r : r + step, :], u_all[...], preferred_element_type=jnp.float32)
            for b in range(0, step, BLOCK):
                here = slice(r + b, r + b + BLOCK)
                for j in range(layers):
                    tiles = []
                    for c in range(j * width, (j + 1) * width, BLOCK):
                        fill = fill_ref[0, (r + b) // BLOCK, c // BLOCK].astype(jnp.float32)
                        tiles.append(part[b : b + BLOCK, c : c + BLOCK] * -fill)
                    tile = tiles[0] if len(tiles) == 1 else jnp.concatenate(tiles, 1)

                    @pl.when(core == j % 2)
                    def _():
                        keep_ref[j // 2, here, :] = tile

                    @pl.when(core != j % 2)
                    def _():
                        send_ref[j // 2, here, :] = tile.astype(jnp.bfloat16)

                    if r + b < WS:
                        low = tile.astype(jnp.bfloat16)
                        for g in range(BLOCK // piece_rows):
                            at = (r + b) // piece_rows + g
                            pivot_ref[j, at] = low[g * piece_rows : (g + 1) * piece_rows]

    return kernel_call(
        body,
        (
            jax.ShapeDtypeStruct((layers // 2, rows, width), jnp.float32),
            jax.ShapeDtypeStruct((layers // 2, rows, width), jnp.bfloat16),
            jax.ShapeDtypeStruct((layers, grids, piece_rows, width), jnp.bfloat16),
        ),
        [SMEM, SMEM, VMEM] + [VMEM] * grids,
        scratch=[pltpu.VMEM((depth, columns), jnp.bfloat16)],
        flops=2 * rows * depth * columns,
        nbytes=2 * rows * depth + 2 * depth * columns + 6 * rows * columns,
    )(place, copy_fill, masked, *pieces)


def tree(layers):
    nodes, level = [], 0
    while 2 << level <= layers:
        size = 2 << level
        for j in range(layers // size):
            low = j * size
            below = [n for n, first, span, _ in nodes if low <= first < low + size]
            nodes.append((layers - (layers >> level) + j, low, size, below))
        level += 1
    return nodes


def pick_pivots(candidates, sep_owner, grids):
    layers, _, piece_rows, width = candidates.shape
    nodes = tree(layers)

    def body(owner_ref, c_ref, out_ref):
        for node, low, size, _ in nodes:
            owner = owner_ref[node]
            total = c_ref[low, owner].astype(jnp.float32)
            for i in range(low + 1, low + size):
                total = total + c_ref[i, owner].astype(jnp.float32)
            total = total.astype(jnp.bfloat16)
            for g in range(grids):
                out_ref[g, node] = total

    return kernel_call(
        body,
        jax.ShapeDtypeStruct((grids, len(nodes), piece_rows, width), jnp.bfloat16),
        [SMEM, VMEM],
        nbytes=4 * candidates.size,
    )(sep_owner, candidates)


def eliminate(own, other, pivots, below_rows, sep_panels):
    rows, width = own.shape
    grids, count, piece_rows, _ = pivots.shape
    nodes = tree(count + 1)
    inner = [n for n in nodes if n[3]]
    step = min(rows, 256)

    def body(own_ref, other_ref, p_ref, below_ref, sep_ref, out_ref, all_p):
        for node, _, _, below in nodes:
            at = node * WS
            for g in range(grids):
                all_p[at + g * piece_rows : at + (g + 1) * piece_rows, :] = p_ref[g, node]
            if below:
                which = [n[0] for n in inner].index(node)
                pivot = all_p[at : at + WS, :].astype(jnp.float32)
                for m in below:
                    pivot = pivot - jnp.dot(
                        below_ref[which, m], all_p[m * WS : (m + 1) * WS, :], preferred_element_type=jnp.float32
                    )
                all_p[at : at + WS, :] = pivot.astype(jnp.bfloat16)
        for r in range(0, rows, step):
            here = slice(r, r + step)
            total = own_ref[here, :] + other_ref[here, :].astype(jnp.float32)
            for node in range(count):
                total = total - jnp.dot(
                    sep_ref[node, here, :], all_p[node * WS : (node + 1) * WS, :], preferred_element_type=jnp.float32
                )
            out_ref[here, :] = total

    return kernel_call(
        body,
        jax.ShapeDtypeStruct((rows, width), jnp.float32),
        [VMEM] * 5,
        scratch=[pltpu.VMEM((count * WS, width), jnp.bfloat16)],
        flops=2 * rows * count * WS * width,
        nbytes=10 * rows * width + 2 * sep_panels.size,
    )(own, other, pivots, below_rows, sep_panels)


def rows_below(sep_panels, sep_owner):
    layers, grids = lax.axis_size("layer"), lax.axis_size("grid")
    inner = [n for n in tree(layers) if n[3]]
    wide = max(max(n[3]) for n in inner) + 1
    shares = layers if WS % (layers * grids * 8) == 0 else 1
    part = WS // shares
    mine = sep_panels[:wide, :WS]
    if shares > 1:
        mine = lax.dynamic_slice_in_dim(mine, lax.axis_index("layer") * part, part, 1)
    piece = part // grids
    mine = mine.reshape(wide, grids, piece, WS).swapaxes(0, 1)
    got = lax.all_to_all(mine, "grid", 0, 0)
    picked = jnp.stack([lax.dynamic_index_in_dim(got, sep_owner[n[0]], 0, keepdims=False) for n in inner])
    axis = BOTH if shares > 1 else "grid"
    spread = jnp.broadcast_to(picked[None], (shares * grids,) + picked.shape)
    full = lax.all_to_all(spread, axis, 0, 0)
    full = jnp.moveaxis(full, 0, 2)
    return full.reshape(len(inner), wide, WS, WS)


def local(l_panels, u_panels, panel_fill, copy_fill, sep_panels, sep_owner):
    layers, grids = lax.axis_size("layer"), lax.axis_size("grid")
    layer, me = lax.axis_index("layer"), lax.axis_index("grid")
    place = jnp.stack([layer % 2, me]).astype(jnp.int32)

    pieces = gather_grid(u_panels)
    masked = mask_panels(l_panels, panel_fill)
    below = rows_below(sep_panels, sep_owner)

    keep, send, candidates = layer_copy(masked, pieces, copy_fill, place)
    shape = candidates.shape
    candidates = lax.all_to_all(candidates.reshape((layers * grids,) + shape[2:]), BOTH, 0, 0).reshape(shape)
    pivots = lax.all_to_all(pick_pivots(candidates, sep_owner, grids), "grid", 0, 0)

    other = apart(send, "layer", 1)
    bit = 1
    while keep.shape[0] > 1:
        bit *= 2
        half = keep.shape[0] // 2
        total = keep + other.astype(jnp.float32)
        total = total.reshape((half, 2) + total.shape[1:])
        side = (layer // bit) % 2
        keep = lax.dynamic_index_in_dim(total, side, 1, keepdims=False)
        send = lax.dynamic_index_in_dim(total, 1 - side, 1, keepdims=False).astype(jnp.bfloat16)
        other = apart(send, "layer", bit)
    return eliminate(keep[0], other[0], pivots, below, sep_panels)


def solution(mesh):
    return jax.shard_map(
        local,
        mesh=mesh,
        in_specs=(
            P("layer", None, "grid", None),
            P("layer", None, "grid", None),
            P("layer", None, "grid", None),
            P("layer", "grid", None),
            P(None, "grid", None),
            P(),
        ),
        out_specs=P("grid", "layer"),
        check_vma=False,
    )
```

time: 270 us -> 75.6 us (0.28)
  waiting for transfers between devices: 224 us -> 27.5 us
  starting transfers between devices: 1.56 us -> 29.6 us
  between operations: 14.4 us -> 2.08 us
  other arithmetic: 11.4 us -> 0.16 us
  matrix products: 9.05 us -> 0 us
  Pallas kernels: 0 us -> 7.52 us
    psum x2 -> x0, waiting for transfers between devices: 139 us -> none  [spread(): return lax.psum(jnp.where(mine, x, jnp.zeros_like(x)), axis)]
    ppermute x2 -> x9, waiting for transfers between devices: 47.1 us -> 6.22 us  [apart(): lax.ppermute(x, axis, [(i, i ^ distance) for i in range(lax.axis_size(axi...]
    all_gather x1 -> x0, waiting for transfers between devices: 36.5 us -> none  [local(): piece = lax.all_gather(u_panels, 'grid', axis=2, tiled=True)]
    all_to_all x0 -> x4, waiting for transfers between devices: none -> 21.3 us  [the longest x1 7.81 us: local(): lax.all_to_all(candidates.reshape((layers * grids,) + shape[2:]), BOTH, 0...]
    all_to_all x0 -> x4, starting transfers between devices: none -> 16.5 us  [the longest x1 6.04 us: local(): lax.all_to_all(candidates.reshape((layers * grids,) + shape[2:]), BOTH, 0...]
    ppermute x2 -> x9, starting transfers between devices: 1.48 us -> 13.1 us  [apart(): lax.ppermute(x, axis, [(i, i ^ distance) for i in range(lax.axis_size(axi...]
    dot_general x4 -> x0, matrix products: 9.05 us -> none  [the longest x2 4.84 us: local(): jnp.dot(factor, pivot_rows, preferred_element_type=jnp.float32)]
    pallas_call x0 -> x4, Pallas kernels: none -> 7.52 us  [the longest x1 3.48 us: layer_copy(): kernel_call(body, (jax.ShapeDtypeStruct((layers // 2, rows, width), jnp.f...]
  transfers between devices with their start and end apart: 5 -> 13, of which waited for: 5 -> 4; matrix products, arithmetic and copies ran while one was open for 3% -> 8% of each run, Pallas kernels for 0% -> 8%
where the time goes in v1:
time: 75.6 us; the launch traced here: 75 us
  starting transfers between devices  29.6 us (39%)
  waiting for transfers between devices  27.5 us (36%)
  local copies, waits for them, and re-layouts  8.19 us (11%)
  Pallas kernels  7.52 us (10%)
  between operations  2.08 us (3%)
    ppermute x9, starting transfers between devices, apart(): lax.ppermute(x, axis, [(i, i ^ distance) for i in range(lax.axis_size(axi...  13.1 us
    all_to_all x1, waiting for transfers between devices, local(): lax.all_to_all(candidates.reshape((layers * grids,) + shape[2:]), BOTH, 0...  7.81 us
    all_to_all x1, waiting for transfers between devices, local(): lax.all_to_all(pick_pivots(candidates, sep_owner, grids), 'grid', 0, 0)  6.96 us
    all_to_all x1, waiting for transfers between devices, rows_below(): full = lax.all_to_all(spread, axis, 0, 0)  6.52 us
    ppermute x9, waiting for transfers between devices, apart(): lax.ppermute(x, axis, [(i, i ^ distance) for i in range(lax.axis_size(axi...  6.22 us
    all_to_all x1, starting transfers between devices, local(): lax.all_to_all(candidates.reshape((layers * grids,) + shape[2:]), BOTH, 0...  6.04 us
    all_to_all x1, starting transfers between devices, rows_below(): got = lax.all_to_all(mine, 'grid', 0, 0)  4.49 us
    unnamed x12, local copies, waits for them, and re-layouts  4.12 us
  transfers between devices with their start and end apart: 13, of which 4 were waited for; matrix products, arithmetic and copies ran while one was open for 8% of the time, Pallas kernels for 8%

profile of v1, /device:TPU:0, one launch (start us, length us, event | category | flops | bytes accessed | tf_op | source)
XLA Modules:
  0.0 75.0 jit_solution(16635444293213813192)
XLA Ops:
  0.0 3.0 %collective-permute-start.1 = (bf16[1,2,64,512]{3,2,1,0:T(8,128)(2,1)}, bf16[1,2,64,512]{3,2,1,0:T(8,128)(2,1)S(1)}, u32[]{:S(2)}, u32[]{:S(2)}) collective-permute-start(bf16[1,2,64,512]{3,2,1,0:T(8,128)(2,1)} %refs_3_.1), channel_id=1, source_target_pairs={{0,2},{1,3},{2,0},{3,1},{4,6},{5,7},{6,4},{7,5},{8,10},{9,11},{10,... | collective-permute-start | bytes 393224 | tf_op jit(solution)/shard_map/ppermute | solution.py:29
  3.0 2.6 %collective-permute-start.3 = (bf16[1,2,64,512]{3,2,1,0:T(8,128)(2,1)}, bf16[1,2,64,512]{3,2,1,0:T(8,128)(2,1)S(1)}, u32[]{:S(2)}, u32[]{:S(2)}) collective-permute-start(bf16[1,2,64,512]{3,2,1,0:T(8,128)(2,1)} %refs_3_.1), channel_id=1, source_target_pairs={{0,4},{1,5},{2,6},{3,7},{4,0},{5,1},{6,2},{7,3},{8,12},{9,13},{10,... | collective-permute-start | bytes 393224 | tf_op jit(solution)/shard_map/ppermute | solution.py:29
  5.6 0.0 collective-permute-start.5
  5.6 1.7 %collective-permute-start = (bf16[1,2,64,512]{3,2,1,0:T(8,128)(2,1)}, bf16[1,2,64,512]{3,2,1,0:T(8,128)(2,1)S(1)}, u32[]{:S(2)}, u32[]{:S(2)}) collective-permute-start(bf16[1,2,64,512]{3,2,1,0:T(8,128)(2,1)} %refs_3_.1), channel_id=1, source_target_pairs={{0,1},{1,0},{2,3},{3,2},{4,5},{5,4},{6,7},{7,6},{8,9},{9,8},{10,11... | collective-permute-start | bytes 393224 | tf_op jit(solution)/shard_map/ppermute | solution.py:29
  7.3 1.0 %slice.6 = bf16[2,256,256]{2,1,0:T(8,128)(2,1)S(1)} slice(bf16[3,1024,256]{2,1,0:T(8,128)(2,1)} %sep_ref.1), slice={[0:2], [0:256], [0:256]} | slice | bytes 524288 | tf_op jit(solution)/shard_map/slice | solution.py:198
  8.3 0.0 collective-permute-done.1.refs_5_
  8.3 1.7 %collective-permute-start.2 = (bf16[1,2,64,512]{3,2,1,0:T(8,128)(2,1)S(1)}, bf16[1,2,64,512]{3,2,1,0:T(8,128)(2,1)S(1)}, u32[]{:S(2)}, u32[]{:S(2)}) collective-permute-start(bf16[1,2,64,512]{3,2,1,0:T(8,128)(2,1)S(1)} %collective-permute-done.1.refs_5_), channel_id=1, source_target_pairs={{0,1},{1,0},{2,3},{3,2},{4,5},{5,4},{6,7},{7,6},{8,9},{9,8},{10,11... | collective-permute-start | bytes 393224 | tf_op jit(solution)/shard_map/ppermute | solution.py:29
  10.0 6.2 %collective-permute-done.3.refs_7_ = bf16[1,2,64,512]{3,2,1,0:T(8,128)(2,1)S(1)} collective-permute-done((bf16[1,2,64,512]{3,2,1,0:T(8,128)(2,1)}, bf16[1,2,64,512]{3,2,1,0:T(8,128)(2,1)S(1)}, u32[]{:S(2)}, u32[]{:S(2)}) %collective-permute-start.3) | collective-permute-done | bytes 131104 | tf_op jit(solution)/shard_map/ppermute | solution.py:29
  16.2 1.5 %collective-permute-start.4 = (bf16[1,2,64,512]{3,2,1,0:T(8,128)(2,1)S(1)}, bf16[1,2,64,512]{3,2,1,0:T(8,128)(2,1)S(1)}, u32[]{:S(2)}, u32[]{:S(2)}) collective-permute-start(bf16[1,2,64,512]{3,2,1,0:T(8,128)(2,1)S(1)} %collective-permute-done.3.refs_7_), channel_id=1, source_target_pairs={{0,1},{1,0},{2,3},{3,2},{4,5},{5,4},{6,7},{7,6},{8,9},{9,8},{10,11... | collective-permute-start | bytes 393224 | tf_op jit(solution)/shard_map/ppermute | solution.py:29
  17.7 0.0 collective-permute-done.5.refs_9_
  17.7 0.5 collective-permute-start.6
  18.2 0.6 copy.14
  18.8 4.5 %all-to-all-start.2 = ((bf16[8,2,8,256]{3,2,1,0:T(8,128)(2,1)}), bf16[8,2,8,256]{3,2,1,0:T(8,128)(2,1)S(1)}, u32[]{:S(2)}, u32[]{:S(2)}) async-start(bf16[8,2,8,256]{3,2,1,0:T(8,128)(2,1)} %copy.14), calls=%async_computation.2 | async-start | bytes 131072 | tf_op jit(solution)/shard_map/all_to_all | solution.py:203
  23.3 0.1 pad_add_fusion.refs_0_
  23.4 0.8 %copy.12.fill_ref = s32[1,2,8,4]{3,2,1,0:T(8,128)S(1)} copy(s32[1,2,8,4]{2,3,1,0:T(4,128)} %param.8) | data formatting | bytes 512 | tf_op args[2]
  24.2 0.8 %copy.13.refs_1_ = s32[1,8,4]{2,1,0:T(8,128)S(1)} copy(s32[1,8,4]{1,2,0:T(4,128)} %param.9) | data formatting | bytes 256 | tf_op args[3]
  24.9 0.0 copy-start.1
  24.9 1.6 %copy-done.1 = bf16[1,2,1024,512]{3,2,1,0:T(8,128)(2,1)S(1)} copy-done((bf16[1,2,1024,512]{3,2,1,0:T(8,128)(2,1)S(1)}, bf16[1,2,1024,512]{3,2,1,0:T(8,128)(2,1)}, u32[]{:S(2)}) %copy-start.1) | copy-done | bytes 2097176
  26.5 0.0 copy-start.3
  26.5 1.3 %shard_map.64.refs_2_ = bf16[1024,1024]{1,0:T(8,128)(2,1)S(1)} custom-call(bf16[1,2,1024,512]{3,2,1,0:T(8,128)(2,1)S(1)} %copy-done.1, s32[1,2,8,4]{3,2,1,0:T(8,128)S(1)} %copy.12.fill_ref), custom_call_target="tpu_custom_call" | custom-call | bytes 4194304 | tf_op jit(solution)/shard_map/pallas_call | solution.py:55
  27.8 0.0 copy-start.2
  27.8 0.0 collective-permute-done.refs_4_
  27.8 0.0 collective-permute-done.2.refs_6_
  27.8 0.0 collective-permute-done.4.refs_8_
  27.9 0.0 collective-permute-done.6.refs_10_
  27.9 0.0 copy-done.3
  27.9 3.5 %shard_map.65 = (f32[2,1024,128]{2,1,0:T(8,128)S(1)}, bf16[2,1024,128]{2,1,0:T(8,128)(2,1)S(1)}, bf16[4,8,32,128]{3,2,1,0:T(8,128)(2,1)}) custom-call(s32[2]{0:T(128)S(1)} %pad_add_fusion.refs_0_, s32[1,8,4]{2,1,0:T(8,128)S(1)} %copy.13.refs_1_, bf16[1024,1024]{1,0:T(8,128)(2,1)S(1)} %shard_map.64.refs_2_, bf16[1,2,64,512]{3,2,1,0:T(8,128)(2,1)S(1)} %copy-done.3, ...), custom_call_target="tpu_custom_call" | custom-call | flops 1073741824 | bytes 6291456 | tf_op jit(solution)/shard_map/pallas_call | solution.py:105
  31.4 0.0 all-to-all-done.2
  31.4 6.0 %all-to-all-start = ((bf16[32,32,128]{2,1,0:T(8,128)(2,1)}), bf16[32,32,128]{2,1,0:T(8,128)(2,1)S(1)}, u32[]{:S(2)}, u32[]{:S(2)}) async-start(bf16[32,32,128]{2,1,0:T(8,128)(2,1)} %bitcast.4), calls=%async_computation | async-start | bytes 524288 | tf_op jit(solution)/shard_map/all_to_all | solution.py:223
  37.4 0.3 collective-permute-start.7
  37.7 0.0 copy-done.2
  37.7 0.6 slice.7
  40.2 7.8 %all-to-all-done = bf16[32,32,128]{2,1,0:T(8,128)(2,1)S(1)} async-done(((bf16[32,32,128]{2,1,0:T(8,128)(2,1)}), bf16[32,32,128]{2,1,0:T(8,128)(2,1)S(1)}, u32[]{:S(2)}, u32[]{:S(2)}) %all-to-all-start) | async-done | bytes 262176 | tf_op jit(solution)/shard_map/all_to_all | solution.py:223
  48.1 0.7 broadcast_in_dim.8
  48.8 2.6 %all-to-all-start.3 = ((bf16[32,1,2,8,256]{4,3,2,1,0:T(8,128)(2,1)}), bf16[32,1,2,8,256]{4,3,2,1,0:T(8,128)(2,1)S(1)}, u32[]{:S(2)}, u32[]{:S(2)}) async-start(bf16[32,1,2,8,256]{4,3,2,1,0:T(8,128)(2,1)} %broadcast_in_dim.8), calls=%async_computation.3 | async-start | bytes 524288 | tf_op jit(solution)/shard_map/all_to_all | solution.py:207
  51.4 1.2 %shard_map.66 = bf16[8,3,32,128]{3,2,1,0:T(8,128)(2,1)} custom-call(s32[3]{0:T(128)S(1)} %copy-done.2, bf16[4,8,32,128]{3,2,1,0:T(8,128)(2,1)S(1)} %bitcast.19), custom_call_target="tpu_custom_call" | custom-call | bytes 524288 | tf_op jit(solution)/shard_map/pallas_call | solution.py:145
  52.6 0.0 collective-permute-done.7
  52.7 0.1 convert_add_fusion
  52.7 0.0 copy-start.4
  52.8 1.0 %copy-done.4 = f32[2,1024,128]{2,1,0:T(8,128)} copy-done((f32[2,1024,128]{2,1,0:T(8,128)}, f32[2,1024,128]{2,1,0:T(8,128)S(1)}, u32[]{:S(2)}) %copy-start.4) | copy-done | bytes 1048600
  53.8 1.7 %collective-permute-start.8 = (bf16[1,1024,128]{2,1,0:T(8,128)(2,1)S(1)}, bf16[1,1024,128]{2,1,0:T(8,128)(2,1)S(1)}, u32[]{:S(2)}, u32[]{:S(2)}) collective-permute-start(bf16[1,1024,128]{2,1,0:T(8,128)(2,1)S(1)} %dynamic-slice_convert_fusion), channel_id=1, source_target_pairs={{0,16},{8,24},{16,0},{24,8},{1,17},{9,25},{17,1},{25,9},{2,18},{10... | collective-permute-start | bytes 786440 | tf_op jit(solution)/shard_map/ppermute | solution.py:29
  55.5 6.5 %all-to-all-done.3 = bf16[32,1,2,8,256]{4,3,2,1,0:T(8,128)(2,1)S(1)} async-done(((bf16[32,1,2,8,256]{4,3,2,1,0:T(8,128)(2,1)}), bf16[32,1,2,8,256]{4,3,2,1,0:T(8,128)(2,1)S(1)}, u32[]{:S(2)}, u32[]{:S(2)}) %all-to-all-start.3) | async-done | bytes 262176 | tf_op jit(solution)/shard_map/all_to_all | solution.py:207
  62.0 3.4 %all-to-all-start.1 = ((bf16[8,3,32,128]{3,2,1,0:T(8,128)(2,1)}), bf16[8,3,32,128]{3,2,1,0:T(8,128)(2,1)S(1)}, u32[]{:S(2)}, u32[]{:S(2)}) async-start(bf16[8,3,32,128]{3,2,1,0:T(8,128)(2,1)} %shard_map.66), calls=%async_computation.1 | async-start | bytes 393216 | tf_op jit(solution)/shard_map/all_to_all | solution.py:224
  65.4 1.1 %dynamic-slice_bitcast_fusion.own_ref = f32[1024,128]{1,0:T(8,128)S(1)} fusion(f32[2,1024,128]{2,1,0:T(8,128)} %copy-done.4, s32[]{:T(128)S(6)} %select_n.32), kind=kLoop, calls=%fused_computation.2 | loop fusion | bytes 1048580 | tf_op jit(solution)/shard_map/squeeze | solution.py:237
  66.5 0.0 collective-permute-done.8
  66.5 7.0 %all-to-all-done.1.p_ref = bf16[8,3,32,128]{3,2,1,0:T(8,128)(2,1)S(1)} async-done(((bf16[8,3,32,128]{3,2,1,0:T(8,128)(2,1)}), bf16[8,3,32,128]{3,2,1,0:T(8,128)(2,1)S(1)}, u32[]{:S(2)}, u32[]{:S(2)}) %all-to-all-start.1) | async-done | bytes 196640 | tf_op jit(solution)/shard_map/all_to_all | solution.py:224
  73.5 0.0 copy-done
  73.5 1.5 %shard_map.67 = f32[1024,128]{1,0:T(8,128)} custom-call(f32[1024,128]{1,0:T(8,128)S(1)} %dynamic-slice_bitcast_fusion.own_ref, bf16[1024,128]{1,0:T(8,128)(2,1)S(1)} %bitcast.20, bf16[8,3,32,128]{3,2,1,0:T(8,128)(2,1)S(1)} %all-to-all-done.1.p_ref, bf16[1,2,256,256]{3,2,1,0:T(8,128)(2,1)S(1)} %copy_bitcast_fusion.below_ref, bf16[3,1024,256]{2,1,0:T(8,128)(2,1)S(1)} %copy-done), custom_call_target="tpu_custom_call" | custom-call | flops 201326592 | bytes 2883584 | tf_op jit(solution)/shard_map/pallas_call | solution.py:182
  (5 shorter events, 0.1 us)
Async XLA Ops:
  0.0 8.3 %collective-permute-start.1 = (bf16[1,2,64,512]{3,2,1,0:T(8,128)(2,1)}, bf16[1,2,64,512]{3,2,1,0:T(8,128)(2,1)S(1)}, u32[]{:S(2)}, u32[]{:S(2)}) collective-permute-start(bf16[1,2,64,512]{3,2,1,0:T(8,128)(2,1)} %refs_3_.1), channel_id=1, source_target_pairs={{0,2},{1,3},{2,0},{3,1},{4,6},{5,7},{6,4},{7,5},{8,10},{9,11},{10,... | collective-permute-start | bytes 393224 | tf_op jit(solution)/shard_map/ppermute | solution.py:29
  3.0 13.2 %collective-permute-start.3 = (bf16[1,2,64,512]{3,2,1,0:T(8,128)(2,1)}, bf16[1,2,64,512]{3,2,1,0:T(8,128)(2,1)S(1)}, u32[]{:S(2)}, u32[]{:S(2)}) collective-permute-start(bf16[1,2,64,512]{3,2,1,0:T(8,128)(2,1)} %refs_3_.1), channel_id=1, source_target_pairs={{0,4},{1,5},{2,6},{3,7},{4,0},{5,1},{6,2},{7,3},{8,12},{9,13},{10,... | collective-permute-start | bytes 393224 | tf_op jit(solution)/shard_map/ppermute | solution.py:29
  5.6 12.1 %collective-permute-start.5 = (bf16[1,2,64,512]{3,2,1,0:T(8,128)(2,1)}, bf16[1,2,64,512]{3,2,1,0:T(8,128)(2,1)S(1)}, u32[]{:S(2)}, u32[]{:S(2)}) collective-permute-start(bf16[1,2,64,512]{3,2,1,0:T(8,128)(2,1)} %refs_3_.1), channel_id=1, source_target_pairs={{0,6},{1,7},{2,4},{3,5},{4,2},{5,3},{6,0},{7,1},{8,14},{9,15},{10,... | collective-permute-start | bytes 393224 | tf_op jit(solution)/shard_map/ppermute | solution.py:29
  5.6 22.2 %collective-permute-start = (bf16[1,2,64,512]{3,2,1,0:T(8,128)(2,1)}, bf16[1,2,64,512]{3,2,1,0:T(8,128)(2,1)S(1)}, u32[]{:S(2)}, u32[]{:S(2)}) collective-permute-start(bf16[1,2,64,512]{3,2,1,0:T(8,128)(2,1)} %refs_3_.1), channel_id=1, source_target_pairs={{0,1},{1,0},{2,3},{3,2},{4,5},{5,4},{6,7},{7,6},{8,9},{9,8},{10,11... | collective-permute-start | bytes 393224 | tf_op jit(solution)/shard_map/ppermute | solution.py:29
  8.3 19.5 %collective-permute-start.2 = (bf16[1,2,64,512]{3,2,1,0:T(8,128)(2,1)S(1)}, bf16[1,2,64,512]{3,2,1,0:T(8,128)(2,1)S(1)}, u32[]{:S(2)}, u32[]{:S(2)}) collective-permute-start(bf16[1,2,64,512]{3,2,1,0:T(8,128)(2,1)S(1)} %collective-permute-done.1.refs_5_), channel_id=1, source_target_pairs={{0,1},{1,0},{2,3},{3,2},{4,5},{5,4},{6,7},{7,6},{8,9},{9,8},{10,11... | collective-permute-start | bytes 393224 | tf_op jit(solution)/shard_map/ppermute | solution.py:29
  16.2 11.7 %collective-permute-start.4 = (bf16[1,2,64,512]{3,2,1,0:T(8,128)(2,1)S(1)}, bf16[1,2,64,512]{3,2,1,0:T(8,128)(2,1)S(1)}, u32[]{:S(2)}, u32[]{:S(2)}) collective-permute-start(bf16[1,2,64,512]{3,2,1,0:T(8,128)(2,1)S(1)} %collective-permute-done.3.refs_7_), channel_id=1, source_target_pairs={{0,1},{1,0},{2,3},{3,2},{4,5},{5,4},{6,7},{7,6},{8,9},{9,8},{10,11... | collective-permute-start | bytes 393224 | tf_op jit(solution)/shard_map/ppermute | solution.py:29
  17.7 10.2 %collective-permute-start.6 = (bf16[1,2,64,512]{3,2,1,0:T(8,128)(2,1)S(1)}, bf16[1,2,64,512]{3,2,1,0:T(8,128)(2,1)S(1)}, u32[]{:S(2)}, u32[]{:S(2)}) collective-permute-start(bf16[1,2,64,512]{3,2,1,0:T(8,128)(2,1)S(1)} %collective-permute-done.5.refs_9_), channel_id=1, source_target_pairs={{0,1},{1,0},{2,3},{3,2},{4,5},{5,4},{6,7},{7,6},{8,9},{9,8},{10,11... | collective-permute-start | bytes 393224 | tf_op jit(solution)/shard_map/ppermute | solution.py:29
  18.8 12.5 %all-to-all-start.2 = ((bf16[8,2,8,256]{3,2,1,0:T(8,128)(2,1)}), bf16[8,2,8,256]{3,2,1,0:T(8,128)(2,1)S(1)}, u32[]{:S(2)}, u32[]{:S(2)}) async-start(bf16[8,2,8,256]{3,2,1,0:T(8,128)(2,1)} %copy.14), calls=%async_computation.2 | async-start | bytes 131072 | tf_op jit(solution)/shard_map/all_to_all | solution.py:203
  24.9 1.6 %copy-start.1 = (bf16[1,2,1024,512]{3,2,1,0:T(8,128)(2,1)S(1)}, bf16[1,2,1024,512]{3,2,1,0:T(8,128)(2,1)}, u32[]{:S(2)}) copy-start(bf16[1,2,1024,512]{3,2,1,0:T(8,128)(2,1)} %l_ref.1) | copy-start | bytes 6291460
  26.5 1.3 %copy-start.3 = (bf16[1,2,64,512]{3,2,1,0:T(8,128)(2,1)S(1)}, bf16[1,2,64,512]{3,2,1,0:T(8,128)(2,1)}, u32[]{:S(2)}) copy-start(bf16[1,2,64,512]{3,2,1,0:T(8,128)(2,1)} %refs_3_.1) | copy-start | bytes 393220
  27.8 9.9 %copy-start.2 = (s32[3]{0:T(128)S(1)}, s32[3]{0:T(128)}, u32[]{:S(2)}) copy-start(s32[3]{0:T(128)} %owner_ref.1) | copy-start | bytes 40
  31.4 16.7 %all-to-all-start = ((bf16[32,32,128]{2,1,0:T(8,128)(2,1)}), bf16[32,32,128]{2,1,0:T(8,128)(2,1)S(1)}, u32[]{:S(2)}, u32[]{:S(2)}) async-start(bf16[32,32,128]{2,1,0:T(8,128)(2,1)} %bitcast.4), calls=%async_computation | async-start | bytes 524288 | tf_op jit(solution)/shard_map/all_to_all | solution.py:223
  37.4 15.2 %collective-permute-start.7 = (bf16[2,1024,128]{2,1,0:T(8,128)(2,1)S(1)}, bf16[2,1024,128]{2,1,0:T(8,128)(2,1)S(1)}, u32[]{:S(2)}, u32[]{:S(2)}) collective-permute-start(bf16[2,1024,128]{2,1,0:T(8,128)(2,1)S(1)} %get-tuple-element.9), channel_id=1, source_target_pairs={{0,8},{8,0},{16,24},{24,16},{1,9},{9,1},{17,25},{25,17},{2,10},{10... | collective-permute-start | bytes 1572872 | tf_op jit(solution)/shard_map/ppermute | solution.py:29
  48.8 13.2 %all-to-all-start.3 = ((bf16[32,1,2,8,256]{4,3,2,1,0:T(8,128)(2,1)}), bf16[32,1,2,8,256]{4,3,2,1,0:T(8,128)(2,1)S(1)}, u32[]{:S(2)}, u32[]{:S(2)}) async-start(bf16[32,1,2,8,256]{4,3,2,1,0:T(8,128)(2,1)} %broadcast_in_dim.8), calls=%async_computation.3 | async-start | bytes 524288 | tf_op jit(solution)/shard_map/all_to_all | solution.py:207
  52.6 20.8 %copy-start = (bf16[3,1024,256]{2,1,0:T(8,128)(2,1)S(1)}, bf16[3,1024,256]{2,1,0:T(8,128)(2,1)}, u32[]{:S(2)}) copy-start(bf16[3,1024,256]{2,1,0:T(8,128)(2,1)} %sep_ref.1) | copy-start | bytes 4718596
  52.7 1.0 %copy-start.4 = (f32[2,1024,128]{2,1,0:T(8,128)}, f32[2,1024,128]{2,1,0:T(8,128)S(1)}, u32[]{:S(2)}) copy-start(f32[2,1024,128]{2,1,0:T(8,128)S(1)} %convert_add_fusion) | copy-start | bytes 3145732
  53.8 12.8 %collective-permute-start.8 = (bf16[1,1024,128]{2,1,0:T(8,128)(2,1)S(1)}, bf16[1,1024,128]{2,1,0:T(8,128)(2,1)S(1)}, u32[]{:S(2)}, u32[]{:S(2)}) collective-permute-start(bf16[1,1024,128]{2,1,0:T(8,128)(2,1)S(1)} %dynamic-slice_convert_fusion), channel_id=1, source_target_pairs={{0,16},{8,24},{16,0},{24,8},{1,17},{9,25},{17,1},{25,9},{2,18},{10... | collective-permute-start | bytes 786440 | tf_op jit(solution)/shard_map/ppermute | solution.py:29
  62.0 11.5 %all-to-all-start.1 = ((bf16[8,3,32,128]{3,2,1,0:T(8,128)(2,1)}), bf16[8,3,32,128]{3,2,1,0:T(8,128)(2,1)S(1)}, u32[]{:S(2)}, u32[]{:S(2)}) async-start(bf16[8,3,32,128]{3,2,1,0:T(8,128)(2,1)} %shard_map.66), calls=%async_computation.1 | async-start | bytes 393216 | tf_op jit(solution)/shard_map/all_to_all | solution.py:224

commit v2 on v1

v2 whole, which is shorter than its diff:
```python
import jax
import jax.numpy as jnp
from jax import lax
from jax.experimental import pallas as pl
from jax.experimental.pallas import tpu as pltpu
from jax.sharding import PartitionSpec as P

BLOCK = 128
WS = 256
VMEM_LIMIT = 40 << 20
EARLY_LIMIT = 60 << 20
BOTH = ("layer", "grid")
VMEM = pl.BlockSpec(memory_space=pltpu.VMEM)
HBM = pl.BlockSpec(memory_space=pltpu.HBM)
ANY = pl.BlockSpec(memory_space=pl.ANY)
SMEM = pl.BlockSpec(memory_space=pltpu.SMEM)


def kernel_call(body, out_shape, in_specs, scratch=(), flops=0, nbytes=0, limit=VMEM_LIMIT):
    many = isinstance(out_shape, (tuple, list))
    return pl.pallas_call(
        body,
        out_shape=out_shape,
        in_specs=in_specs,
        out_specs=[VMEM] * len(out_shape) if many else VMEM,
        scratch_shapes=list(scratch),
        compiler_params=pltpu.CompilerParams(vmem_limit_bytes=limit),
        cost_estimate=pl.CostEstimate(flops=flops, bytes_accessed=nbytes, transcendentals=0),
    )


def apart(x, axis, distance):
    return lax.ppermute(x, axis, [(i, i ^ distance) for i in range(lax.axis_size(axis))])


def bits(count):
    return [1 << i for i in range(count.bit_length() - 1)]


def gather_grid(x):
    count = lax.axis_size("grid")
    found = [x] + [None] * (count - 1)
    for k in range(2, count, 2):
        found[k] = apart(x, "grid", k)
    for k in range(0, count, 2):
        found[k + 1] = apart(found[k], "grid", 1)
    return found


def pick_below(sep_panels, sep_owner, place, after):
    layers = lax.axis_size("layer")
    inner = [n for n in tree(layers) if n[3]]
    wide = max(max(n[3]) for n in inner) + 1
    part = WS // layers

    def body(place_ref, owner_ref, sep_ref, _, out_ref, held, sem):
        start = pl.multiple_of(place_ref[0] * part, part)
        copy = pltpu.make_async_copy(sep_ref.at[:wide, pl.ds(start, part)], held, sem)
        copy.start()
        copy.wait()
        for i, n in enumerate(inner):
            mine = owner_ref[n[0]] == place_ref[1]
            out_ref[i] = jnp.where(mine, held[...], jnp.zeros(held.shape, held.dtype))

    return kernel_call(
        body,
        jax.ShapeDtypeStruct((len(inner), wide, part, WS), jnp.bfloat16),
        [SMEM, SMEM, HBM, ANY],
        scratch=[pltpu.VMEM((wide, part, WS), jnp.bfloat16), pltpu.SemaphoreType.DMA],
        nbytes=4 * wide * part * WS,
        limit=EARLY_LIMIT,
    )(place, sep_owner, sep_panels, after)


def mask_panels(l_panels, panel_fill, place, after):
    _, panels, rows, width = l_panels.shape
    share = width // lax.axis_size("grid")
    step = min(rows, 256)

    def body(place_ref, fill_ref, l_ref, _, out_ref, l_all, sems):
        first = place_ref[1] * share // BLOCK
        copies = [
            pltpu.make_async_copy(l_ref.at[0, :, r : r + step], l_all.at[:, r : r + step], sems.at[r // step])
            for r in range(0, rows, step)
        ]
        for copy in copies:
            copy.start()
        for r in range(0, rows, step):
            copies[r // step].wait()
            for k in range(panels):
                for j in range(width // BLOCK):
                    at = pl.multiple_of(((j ^ first) * panels + k) * BLOCK, BLOCK)
                    for b in range(r, r + step, BLOCK):
                        here = fill_ref[0, k, j, b // BLOCK] != 0
                        tile = l_all[k, b : b + BLOCK, j * BLOCK : (j + 1) * BLOCK]
                        out_ref[b : b + BLOCK, pl.ds(at, BLOCK)] = jnp.where(here, tile, jnp.zeros_like(tile))

    return kernel_call(
        body,
        jax.ShapeDtypeStruct((rows, panels * width), jnp.bfloat16),
        [SMEM, SMEM, HBM, ANY],
        scratch=[pltpu.VMEM((panels, rows, width), jnp.bfloat16), pltpu.SemaphoreType.DMA((rows // step,))],
        nbytes=4 * panels * rows * width,
    )(place, panel_fill, l_panels, after)


def load_panels(u_refs, first, grids, u_all, sems, me):
    _, panels, share, _ = u_refs[0].shape
    copies = []
    for i, ref in enumerate(u_refs):
        block, inside = i * share // BLOCK, (me ^ (first + i)) * share % BLOCK
        for p in range(panels):
            at = pl.multiple_of((block * panels + p) * BLOCK + inside, share)
            copies.append(pltpu.make_async_copy(ref.at[0, p], u_all.at[pl.ds(at, share), :], sems.at[i, p]))
            copies[-1].start()
    return copies


def block_fill(part, fill_ref, row, low, high):
    lines = []
    for b in range(0, part.shape[0], BLOCK):
        tiles = []
        for c in range(low, high, BLOCK):
            fill = fill_ref[0, c // BLOCK, (row + b) // BLOCK].astype(jnp.float32)
            tiles.append(part[b : b + BLOCK, c : c + BLOCK] * -fill)
        lines.append(tiles[0] if len(tiles) == 1 else jnp.concatenate(tiles, 1))
    return lines[0] if len(lines) == 1 else jnp.concatenate(lines, 0)


def first_part(masked, pieces, grids, place, after):
    rows, _ = masked.shape
    _, panels, share, columns = pieces[0].shape
    depth = panels * share * len(pieces)
    step = min(rows, 256)

    def body(place_ref, l_ref, *refs):
        u_refs, (out_ref, u_all, sems) = refs[: len(pieces)], refs[len(pieces) + 1 :]
        for copy in load_panels(u_refs, 0, grids, u_all, sems, place_ref[1]):
            copy.wait()
        for r in range(0, rows, step):
            here = slice(r, r + step)
            out_ref[here, :] = jnp.dot(l_ref[here, :depth], u_all[...], preferred_element_type=jnp.float32)

    return kernel_call(
        body,
        jax.ShapeDtypeStruct((rows, columns), jnp.float32),
        [SMEM, VMEM] + [HBM] * len(pieces) + [ANY],
        scratch=[pltpu.VMEM((depth, columns), jnp.bfloat16), pltpu.SemaphoreType.DMA((len(pieces), panels))],
        flops=2 * rows * depth * columns,
        nbytes=2 * rows * depth + 2 * depth * columns + 4 * rows * columns,
    )(place, masked, *pieces, after)


def layer_copy(begun, masked, pieces, grids, copy_fill, place, after):
    rows, columns = begun.shape
    _, panels, share, _ = pieces[0].shape
    layers = lax.axis_size("layer")
    width = columns // layers
    piece_rows = WS // grids
    step = min(rows, 256)
    depth = panels * share * len(pieces)
    done = masked.shape[1] - depth

    def body(place_ref, fill_ref, begun_ref, l_ref, *refs):
        u_refs, (keep_ref, send_ref, pivot_ref, u_all, sems) = refs[: len(pieces)], refs[len(pieces) + 1 :]
        core = place_ref[0] % 2
        for copy in load_panels(u_refs, grids - len(pieces), grids, u_all, sems, place_ref[1]):
            copy.wait()
        for r in range(0, rows, step):
            here = slice(r, r + step)
            part = begun_ref[here, :] + jnp.dot(l_ref[here, done:], u_all[...], preferred_element_type=jnp.float32)
            for j in range(layers):
                tile = block_fill(part, fill_ref, r, j * width, (j + 1) * width)

                @pl.when(core == j % 2)
                def _():
                    keep_ref[j // 2, here, :] = tile

                @pl.when(core != j % 2)
                def _():
                    send_ref[j // 2, here, :] = tile.astype(jnp.bfloat16)

                if r < WS:
                    low = tile.astype(jnp.bfloat16)
                    for g in range(step // piece_rows):
                        pivot_ref[j, r // piece_rows + g] = low[g * piece_rows : (g + 1) * piece_rows]

    return kernel_call(
        body,
        (
            jax.ShapeDtypeStruct((layers // 2, rows, width), jnp.float32),
            jax.ShapeDtypeStruct((layers // 2, rows, width), jnp.bfloat16),
            jax.ShapeDtypeStruct((layers, grids, piece_rows, width), jnp.bfloat16),
        ),
        [SMEM, SMEM, VMEM, VMEM] + [HBM] * len(pieces) + [ANY],
        scratch=[pltpu.VMEM((depth, columns), jnp.bfloat16), pltpu.SemaphoreType.DMA((len(pieces), panels))],
        flops=2 * rows * depth * columns,
        nbytes=2 * rows * depth + 2 * depth * columns + 8 * rows * columns,
    )(place, copy_fill, begun, masked, *pieces, after)


def tree(layers):
    nodes, level = [], 0
    while 2 << level <= layers:
        size = 2 << level
        for j in range(layers // size):
            low = j * size
            below = [n for n, first, span, _ in nodes if low <= first < low + size]
            nodes.append((layers - (layers >> level) + j, low, size, below))
        level += 1
    return nodes


def pick_pivots(candidates, sep_owner, grids, after):
    layers, _, piece_rows, width = candidates.shape
    nodes = tree(layers)

    def body(owner_ref, c_ref, *refs):
        out_ref = refs[-1]
        for node, low, size, _ in nodes:
            owner = owner_ref[node]
            total = c_ref[low, owner].astype(jnp.float32)
            for i in range(low + 1, low + size):
                total = total + c_ref[i, owner].astype(jnp.float32)
            total = total.astype(jnp.bfloat16)
            for g in range(grids):
                out_ref[g, node] = total

    return kernel_call(
        body,
        jax.ShapeDtypeStruct((grids, len(nodes), piece_rows, width), jnp.bfloat16),
        [SMEM, VMEM] + [ANY] * len(after),
        nbytes=4 * candidates.size,
    )(sep_owner, candidates, *after)


def eliminate(own, other, pivots, below, sep_panels, place):
    rows, width = own.shape
    grids, count, piece_rows, _ = pivots.shape
    nodes = tree(count + 1)
    inner = [n for n in nodes if n[3]]
    _, wide, part, _ = below[0].shape
    step = min(rows, 256)

    def body(place_ref, own_ref, other_ref, p_ref, sep_ref, *refs):
        below_refs = refs[: len(below)]
        out_ref, all_p, all_below = refs[len(below) :]
        layer = place_ref[0]
        for k, ref in enumerate(below_refs):
            at = pl.multiple_of((layer ^ k if len(below) > 1 else 0) * part, part)
            for i in range(len(inner)):
                for m in inner[i][3]:
                    all_below[i, m, pl.ds(at, part), :] = ref[i, m]
        for node, _, _, under in nodes:
            at = node * WS
            for g in range(grids):
                all_p[at + g * piece_rows : at + (g + 1) * piece_rows, :] = p_ref[g, node]
            if under:
                which = [n[0] for n in inner].index(node)
                pivot = all_p[at : at + WS, :].astype(jnp.float32)
                for m in under:
                    pivot = pivot - jnp.dot(
                        all_below[which, m], all_p[m * WS : (m + 1) * WS, :], preferred_element_type=jnp.float32
                    )
                all_p[at : at + WS, :] = pivot.astype(jnp.bfloat16)
        for r in range(0, rows, step):
            here = slice(r, r + step)
            total = own_ref[here, :] + other_ref[here, :].astype(jnp.float32)
            for node in range(count):
                total = total - jnp.dot(
                    sep_ref[node, here, :], all_p[node * WS : (node + 1) * WS, :], preferred_element_type=jnp.float32
                )
            out_ref[here, :] = total

    return kernel_call(
        body,
        jax.ShapeDtypeStruct((rows, width), jnp.float32),
        [SMEM] + [VMEM] * (4 + len(below)),
        scratch=[
            pltpu.VMEM((count * WS, width), jnp.bfloat16),
            pltpu.VMEM((len(inner), wide, WS, WS), jnp.bfloat16),
        ],
        flops=2 * rows * count * WS * width,
        nbytes=10 * rows * width + 2 * sep_panels.size,
    )(place, own, other, pivots, sep_panels, *below)


def parts_below(part):
    found = [part]
    while len(found) < lax.axis_size("layer"):
        found += [apart(x, "layer", len(found)) for x in found]
    return found


def local(l_panels, u_panels, panel_fill, copy_fill, sep_panels, sep_owner):
    layers, grids = lax.axis_size("layer"), lax.axis_size("grid")
    layer, me = lax.axis_index("layer"), lax.axis_index("grid")
    place = jnp.stack([layer, me]).astype(jnp.int32)

    pieces = gather_grid(u_panels)
    below = pick_below(sep_panels, sep_owner, place, pieces[1])
    masked = mask_panels(l_panels, jnp.swapaxes(panel_fill, 2, 3), place, below)
    for bit in bits(grids)[:2]:
        below = below + apart(below, "grid", bit)

    last = grids * BLOCK // l_panels.shape[3]
    begun = first_part(masked, pieces[:-last], grids, place, below)
    for bit in bits(grids)[2:]:
        below = below + apart(below, "grid", bit)
    keep, send, candidates = layer_copy(
        begun, masked, pieces[-last:], grids, jnp.swapaxes(copy_fill, 1, 2), place, below
    )
    below = parts_below(below)
    shape = candidates.shape
    candidates = lax.all_to_all(candidates.reshape((layers * grids,) + shape[2:]), BOTH, 0, 0).reshape(shape)

    other = apart(send, "layer", 1)
    pivots = None
    bit = 1
    while keep.shape[0] > 1:
        bit *= 2
        half = keep.shape[0] // 2
        total = keep + other.astype(jnp.float32)
        total = total.reshape((half, 2) + total.shape[1:])
        side = (layer // bit) % 2
        keep = lax.dynamic_index_in_dim(total, side, 1, keepdims=False)
        send = lax.dynamic_index_in_dim(total, 1 - side, 1, keepdims=False).astype(jnp.bfloat16)
        if pivots is None:
            pivots = lax.all_to_all(pick_pivots(candidates, sep_owner, grids, [send] + below), "grid", 0, 0)
        other = apart(send, "layer", bit)
    return eliminate(keep[0], other[0], pivots, below, sep_panels, place)


def solution(mesh):
    return jax.shard_map(
        local,
        mesh=mesh,
        in_specs=(
            P("layer", None, "grid", None),
            P("layer", None, "grid", None),
            P("layer", None, "grid", None),
            P("layer", "grid", None),
            P(None, "grid", None),
            P(),
        ),
        out_specs=P("grid", "layer"),
        check_vma=False,
    )
```

time: 75.6 us -> 64.1 us (0.85)
  waiting for transfers between devices: 27.5 us -> 16.1 us
  Pallas kernels: 7.52 us -> 12.4 us
  starting transfers between devices: 29.6 us -> 25.7 us
  other arithmetic: 0.16 us -> 2.55 us
  between operations: 2.08 us -> 0.19 us
  local copies, waits for them, and re-layouts: 8.19 us -> 6.66 us
    all_to_all x3 -> x1, waiting for transfers between devices: 13.5 us -> 0.06 us  [local(): lax.all_to_all(pick_pivots(candidates, sep_owner, grids, [send] + below),...]
    ppermute x9 -> x15, waiting for transfers between devices: 6.22 us -> 13.6 us  [apart(): lax.ppermute(x, axis, [(i, i ^ distance) for i in range(lax.axis_size(axi...]
    all_to_all x3 -> x1, starting transfers between devices: 10.5 us -> 3.39 us  [local(): lax.all_to_all(pick_pivots(candidates, sep_owner, grids, [send] + below),...]
    ppermute x9 -> x15, starting transfers between devices: 13.1 us -> 18.5 us  [apart(): lax.ppermute(x, axis, [(i, i ^ distance) for i in range(lax.axis_size(axi...]
    pallas_call x1 -> x3, Pallas kernels: 1.52 us -> 6.92 us  [the longest x1 2.71 us: first_part(): kernel_call(body, jax.ShapeDtypeStruct((rows, columns), jnp.float32), [SM...]
    all_to_all x1, waiting for transfers between devices: 7.81 us -> 2.47 us  [local(): lax.all_to_all(candidates.reshape((layers * grids,) + shape[2:]), BOTH, 0...]
    all_to_all x1, starting transfers between devices: 6.04 us -> 3.83 us  [local(): lax.all_to_all(candidates.reshape((layers * grids,) + shape[2:]), BOTH, 0...]
    slice x2 -> x0, local copies, waits for them, and re-layouts: 1.58 us -> none  [the longest x1 0.97 us: rows_below(): mine = sep_panels[:wide, :WS]]
  transfers between devices with their start and end apart: 13 -> 17, of which waited for: 4 -> 6; matrix products, arithmetic and copies ran while one was open for 8% -> 8% of each run, Pallas kernels for 8% -> 10%
where the time goes in v2:
time: 64.1 us; the launch traced here: 63.6 us
  starting transfers between devices  25.7 us (40%)
  waiting for transfers between devices  16.1 us (25%)
  Pallas kernels  12.4 us (19%)
  local copies, waits for them, and re-layouts  6.66 us (10%)
  other arithmetic  2.55 us (4%)
    ppermute x15, starting transfers between devices, apart(): lax.ppermute(x, axis, [(i, i ^ distance) for i in range(lax.axis_size(axi...  18.5 us
    ppermute x15, waiting for transfers between devices, apart(): lax.ppermute(x, axis, [(i, i ^ distance) for i in range(lax.axis_size(axi...  13.6 us
    unnamed x22, local copies, waits for them, and re-layouts  4.39 us
    all_to_all x1, starting transfers between devices, local(): lax.all_to_all(candidates.reshape((layers * grids,) + shape[2:]), BOTH, 0...  3.83 us
    all_to_all x1, starting transfers between devices, local(): lax.all_to_all(pick_pivots(candidates, sep_owner, grids, [send] + below),...  3.39 us
    pallas_call x1, Pallas kernels, layer_copy(): kernel_call(body, (jax.ShapeDtypeStruct((layers // 2, rows, width), jnp.f...  2.79 us
    pallas_call x1, Pallas kernels, first_part(): kernel_call(body, jax.ShapeDtypeStruct((rows, columns), jnp.float32), [SM...  2.71 us
    all_to_all x1, waiting for transfers between devices, local(): lax.all_to_all(candidates.reshape((layers * grids,) + shape[2:]), BOTH, 0...  2.47 us
  transfers between devices with their start and end apart: 17, of which 6 were waited for; matrix products, arithmetic and copies ran while one was open for 8% of the time, Pallas kernels for 10%

profile of v2, /device:TPU:0, one launch (start us, length us, event | category | flops | bytes accessed | tf_op | source)
XLA Modules:
  0.0 63.6 jit_solution(12810755916579962339)
XLA Ops:
  0.0 2.9 %collective-permute-start = (bf16[1,2,64,512]{3,2,1,0:T(8,128)(2,1)}, bf16[1,2,64,512]{3,2,1,0:T(8,128)(2,1)S(1)}, u32[]{:S(2)}, u32[]{:S(2)}) collective-permute-start(bf16[1,2,64,512]{3,2,1,0:T(8,128)(2,1)} %refs_0_.1), channel_id=1, source_target_pairs={{0,1},{1,0},{2,3},{3,2},{4,5},{5,4},{6,7},{7,6},{8,9},{9,8},{10,11... | collective-permute-start | bytes 393224 | tf_op jit(solution)/shard_map/ppermute | solution.py:33
  2.9 1.6 %collective-permute-start.1 = (bf16[1,2,64,512]{3,2,1,0:T(8,128)(2,1)}, bf16[1,2,64,512]{3,2,1,0:T(8,128)(2,1)S(1)}, u32[]{:S(2)}, u32[]{:S(2)}) collective-permute-start(bf16[1,2,64,512]{3,2,1,0:T(8,128)(2,1)} %refs_0_.1), channel_id=1, source_target_pairs={{0,2},{1,3},{2,0},{3,1},{4,6},{5,7},{6,4},{7,5},{8,10},{9,11},{10,... | collective-permute-start | bytes 393224 | tf_op jit(solution)/shard_map/ppermute | solution.py:33
  4.5 2.6 %collective-permute-start.3 = (bf16[1,2,64,512]{3,2,1,0:T(8,128)(2,1)}, bf16[1,2,64,512]{3,2,1,0:T(8,128)(2,1)S(1)}, u32[]{:S(2)}, u32[]{:S(2)}) collective-permute-start(bf16[1,2,64,512]{3,2,1,0:T(8,128)(2,1)} %refs_0_.1), channel_id=1, source_target_pairs={{0,4},{1,5},{2,6},{3,7},{4,0},{5,1},{6,2},{7,3},{8,12},{9,13},{10,... | collective-permute-start | bytes 393224 | tf_op jit(solution)/shard_map/ppermute | solution.py:33
  7.1 0.2 collective-permute-start.7
  7.3 0.6 pad_add_fusion.place_ref
  7.9 0.0 collective-permute-done._.refs_1_
  7.9 0.7 %copy-done.3 = bf16[1,2,64,512]{3,2,1,0:T(8,128)(2,1)} copy-done((bf16[1,2,64,512]{3,2,1,0:T(8,128)(2,1)}, bf16[1,2,64,512]{3,2,1,0:T(8,128)(2,1)S(1)}, u32[]{:S(2)}) %copy-start.3) | copy-done | bytes 131096
  8.6 2.2 %shard_map.64._ = bf16[1,2,64,256]{3,2,1,0:T(8,128)(2,1)} custom-call(s32[2]{0:T(128)} %pad_add_fusion.place_ref, s32[3]{0:T(128)} %owner_ref.3, bf16[3,1024,256]{2,1,0:T(8,128)(2,1)} %sep_ref.3, bf16[1,2,64,512]{3,2,1,0:T(8,128)(2,1)} %copy-done.3), custom_call_target="tpu_custom_call" | custom-call | bytes 131072 | tf_op jit(solution)/shard_map/pallas_call | solution.py:65
  10.7 0.5 collective-permute-start.5
  11.3 0.0 collective-permute-done.1.refs_2_
  11.3 1.5 %collective-permute-start.2 = (bf16[1,2,64,512]{3,2,1,0:T(8,128)(2,1)S(1)}, bf16[1,2,64,512]{3,2,1,0:T(8,128)(2,1)S(1)}, u32[]{:S(2)}, u32[]{:S(2)}) collective-permute-start(bf16[1,2,64,512]{3,2,1,0:T(8,128)(2,1)S(1)} %collective-permute-done.1.refs_2_), channel_id=1, source_target_pairs={{0,1},{1,0},{2,3},{3,2},{4,5},{5,4},{6,7},{7,6},{8,9},{9,8},{10,11... | collective-permute-start | bytes 393224 | tf_op jit(solution)/shard_map/ppermute | solution.py:33
  12.8 4.6 %collective-permute-done.3.refs_4_ = bf16[1,2,64,512]{3,2,1,0:T(8,128)(2,1)S(1)} collective-permute-done((bf16[1,2,64,512]{3,2,1,0:T(8,128)(2,1)}, bf16[1,2,64,512]{3,2,1,0:T(8,128)(2,1)S(1)}, u32[]{:S(2)}, u32[]{:S(2)}) %collective-permute-start.3) | collective-permute-done | bytes 131104 | tf_op jit(solution)/shard_map/ppermute | solution.py:33
  17.4 0.5 collective-permute-start.4
  17.9 0.9 %add.25 = bf16[1,2,64,256]{3,2,1,0:T(8,128)(2,1)S(1)} add(bf16[1,2,64,256]{3,2,1,0:T(8,128)(2,1)} %shard_map.64._, bf16[1,2,64,256]{3,2,1,0:T(8,128)(2,1)S(1)} %collective-permute-done.5) | non-fusion elementwise | flops 32768 | bytes 196608 | tf_op jit(solution)/shard_map/add | solution.py:304
  18.8 0.1 collective-permute-start.6
  18.9 1.6 %collective-permute-start.8 = (bf16[1,2,64,512]{3,2,1,0:T(8,128)(2,1)S(1)}, bf16[1,2,64,512]{3,2,1,0:T(8,128)(2,1)S(1)}, u32[]{:S(2)}, u32[]{:S(2)}) collective-permute-start(bf16[1,2,64,512]{3,2,1,0:T(8,128)(2,1)S(1)} %collective-permute-done.7.refs_0_), channel_id=1, source_target_pairs={{0,1},{1,0},{2,3},{3,2},{4,5},{5,4},{6,7},{7,6},{8,9},{9,8},{10,11... | collective-permute-start | bytes 393224 | tf_op jit(solution)/shard_map/ppermute | solution.py:33
  20.4 1.6 %copy-done.1 = bf16[1,2,1024,512]{3,2,1,0:T(8,128)(2,1)S(1)} copy-done((bf16[1,2,1024,512]{3,2,1,0:T(8,128)(2,1)S(1)}, bf16[1,2,1024,512]{3,2,1,0:T(8,128)(2,1)}, u32[]{:S(2)}) %copy-start.1) | copy-done | bytes 2097176
  22.0 0.8 %copy-done.2 = bf16[1,2,64,256]{3,2,1,0:T(8,128)(2,1)S(1)} copy-done((bf16[1,2,64,256]{3,2,1,0:T(8,128)(2,1)S(1)}, bf16[1,2,64,256]{3,2,1,0:T(8,128)(2,1)}, u32[]{:S(2)}) %copy-start.2) | copy-done | bytes 65560
  22.9 0.6 copy-done.6
  23.5 0.7 %copy-done.8 = s32[1,2,8,4]{2,3,1,0:T(4,128)S(1)} copy-done((s32[1,2,8,4]{2,3,1,0:T(4,128)S(1)}, s32[1,2,8,4]{2,3,1,0:T(4,128)}, u32[]{:S(2)}) %copy-start.8) | copy-done | bytes 280
  24.2 1.4 %shard_map.65.l_ref = bf16[1024,1024]{1,0:T(8,128)(2,1)S(1)} custom-call(s32[2]{0:T(128)S(1)} %copy-done.6, s32[1,2,4,8]{3,2,1,0:T(4,128)S(1)} %bitcast.11, bf16[1,2,1024,512]{3,2,1,0:T(8,128)(2,1)S(1)} %copy-done.1, bf16[1,2,64,256]{3,2,1,0:T(8,128)(2,1)S(1)} %copy-done.2), custom_call_target="tpu_custom_call" | custom-call | bytes 4194304 | tf_op jit(solution)/shard_map/pallas_call | solution.py:98
  25.6 0.0 collective-permute-done.6
  25.6 0.0 copy-start.10
  25.7 3.0 %collective-permute-start.9 = (bf16[1,2,64,256]{3,2,1,0:T(8,128)(2,1)S(1)}, bf16[1,2,64,256]{3,2,1,0:T(8,128)(2,1)S(1)}, u32[]{:S(2)}, u32[]{:S(2)}) collective-permute-start(bf16[1,2,64,256]{3,2,1,0:T(8,128)(2,1)S(1)} %add.26.refs_6_), channel_id=1, source_target_pairs={{0,4},{1,5},{2,6},{3,7},{4,0},{5,1},{6,2},{7,3},{8,12},{9,13},{10,... | collective-permute-start | bytes 196616 | tf_op jit(solution)/shard_map/ppermute | solution.py:33
  28.6 0.0 collective-permute-done.2.refs_3_
  28.6 2.7 %shard_map.66.begun_ref = f32[1024,512]{1,0:T(8,128)S(1)} custom-call(s32[2]{0:T(128)S(1)} %copy-done.6, bf16[1024,1024]{1,0:T(8,128)(2,1)S(1)} %shard_map.65.l_ref, bf16[1,2,64,512]{3,2,1,0:T(8,128)(2,1)S(1)} %copy-done.5, bf16[1,2,64,512]{3,2,1,0:T(8,128)(2,1)S(1)} %copy-done.4, bf16[1,2,64,512]{3,2,1,0:T(8,128)(2,1)S(1)} %collective-permute-done.1.refs_2_, ...), custom_call_target="tpu_custom_call" | custom-call | flops 805306368 | bytes 4456448 | tf_op jit(solution)/shard_map/pallas_call | solution.py:144
  31.4 0.0 collective-permute-done.9
  31.4 0.0 collective-permute-done.8.refs_1_
  31.4 2.8 %shard_map.67 = (f32[2,1024,128]{2,1,0:T(8,128)S(1)}, bf16[2,1024,128]{2,1,0:T(8,128)(2,1)S(1)}, bf16[4,8,32,128]{3,2,1,0:T(8,128)(2,1)}) custom-call(s32[2]{0:T(128)S(1)} %copy-done.7, s32[1,4,8]{2,1,0:T(4,128)S(1)} %bitcast.12, f32[1024,512]{1,0:T(8,128)S(1)} %shard_map.66.begun_ref, bf16[1024,1024]{1,0:T(8,128)(2,1)S(1)} %shard_map.65.l_ref, ...), custom_call_target="tpu_custom_call" | custom-call | flops 268435456 | bytes 4980736 | tf_op jit(solution)/shard_map/pallas_call | solution.py:188
  34.2 0.0 copy-start.9
  34.2 0.1 collective-permute-start.10
  34.3 3.8 %all-to-all-start = ((bf16[32,32,128]{2,1,0:T(8,128)(2,1)}), bf16[32,32,128]{2,1,0:T(8,128)(2,1)S(1)}, u32[]{:S(2)}, u32[]{:S(2)}) async-start(bf16[32,32,128]{2,1,0:T(8,128)(2,1)} %bitcast.6), calls=%async_computation | async-start | bytes 524288 | tf_op jit(solution)/shard_map/all_to_all | solution.py:315
  38.2 0.3 collective-permute-start.12
  38.5 1.7 %collective-permute-start.13 = (bf16[1,2,64,256]{3,2,1,0:T(8,128)(2,1)S(1)}, bf16[1,2,64,256]{3,2,1,0:T(8,128)(2,1)S(1)}, u32[]{:S(2)}, u32[]{:S(2)}) collective-permute-start(bf16[1,2,64,256]{3,2,1,0:T(8,128)(2,1)S(1)} %add.27.refs_2_.refs_1_.refs_0_), channel_id=1, source_target_pairs={{0,16},{8,24},{16,0},{24,8},{1,17},{9,25},{17,1},{25,9},{2,18},{10... | collective-permute-start | bytes 196616 | tf_op jit(solution)/shard_map/ppermute | solution.py:33
  40.2 0.0 collective-permute-done.12.refs_2_.refs_1_
  40.2 1.1 %collective-permute-start.14 = (bf16[1,2,64,256]{3,2,1,0:T(8,128)(2,1)S(1)}, bf16[1,2,64,256]{3,2,1,0:T(8,128)(2,1)S(1)}, u32[]{:S(2)}, u32[]{:S(2)}) collective-permute-start(bf16[1,2,64,256]{3,2,1,0:T(8,128)(2,1)S(1)} %collective-permute-done.12.refs_2_.refs_1_), channel_id=1, source_target_pairs={{0,16},{8,24},{16,0},{24,8},{1,17},{9,25},{17,1},{25,9},{2,18},{10... | collective-permute-start | bytes 196616 | tf_op jit(solution)/shard_map/ppermute | solution.py:33
  41.2 1.1 %convert_add_fusion = f32[2,1024,128]{2,1,0:T(8,128)} fusion(f32[2,1024,128]{2,1,0:T(8,128)S(1)} %get-tuple-element.8, bf16[2,1024,128]{2,1,0:T(8,128)(2,1)S(1)} %collective-permute-done.10), kind=kLoop, calls=%fused_computation | loop fusion | flops 524288 | bytes 2621440 | tf_op jit(solution)/shard_map/add | solution.py:323
  42.3 1.2 %dynamic-slice_convert_fusion.refs_0_ = bf16[1,1024,128]{2,1,0:T(8,128)(2,1)S(1)} fusion(f32[2,1024,128]{2,1,0:T(8,128)} %convert_add_fusion, s32[]{:T(128)S(6)} %select_n.21), kind=kLoop, calls=%fused_computation.1 | loop fusion | bytes 524292 | tf_op jit(solution)/shard_map/convert_element_type | solution.py:327
  43.5 1.3 %collective-permute-done.13.refs_3_.refs_2_ = bf16[1,2,64,256]{3,2,1,0:T(8,128)(2,1)S(1)} collective-permute-done((bf16[1,2,64,256]{3,2,1,0:T(8,128)(2,1)S(1)}, bf16[1,2,64,256]{3,2,1,0:T(8,128)(2,1)S(1)}, u32[]{:S(2)}, u32[]{:S(2)}) %collective-permute-start.13) | collective-permute-done | bytes 65568 | tf_op jit(solution)/shard_map/ppermute | solution.py:33
  44.8 1.5 %collective-permute-done.14.refs_4_.refs_3_ = bf16[1,2,64,256]{3,2,1,0:T(8,128)(2,1)S(1)} collective-permute-done((bf16[1,2,64,256]{3,2,1,0:T(8,128)(2,1)S(1)}, bf16[1,2,64,256]{3,2,1,0:T(8,128)(2,1)S(1)}, u32[]{:S(2)}, u32[]{:S(2)}) %collective-permute-start.14) | collective-permute-done | bytes 65568 | tf_op jit(solution)/shard_map/ppermute | solution.py:33
  46.3 2.5 %all-to-all-done = bf16[32,32,128]{2,1,0:T(8,128)(2,1)S(1)} async-done(((bf16[32,32,128]{2,1,0:T(8,128)(2,1)}), bf16[32,32,128]{2,1,0:T(8,128)(2,1)S(1)}, u32[]{:S(2)}, u32[]{:S(2)}) %all-to-all-start) | async-done | bytes 262176 | tf_op jit(solution)/shard_map/all_to_all | solution.py:315
  48.8 1.2 %shard_map.68 = bf16[8,3,32,128]{3,2,1,0:T(8,128)(2,1)} custom-call(s32[3]{0:T(128)S(1)} %copy-done.9, bf16[4,8,32,128]{3,2,1,0:T(8,128)(2,1)S(1)} %bitcast.9, bf16[1,1024,128]{2,1,0:T(8,128)(2,1)S(1)} %dynamic-slice_convert_fusion.refs_0_, bf16[1,2,64,256]{3,2,1,0:T(8,128)(2,1)S(1)} %add.27.refs_2_.refs_1_.refs_0_, ...), custom_call_target="tpu_custom_call" | custom-call | bytes 524288 | tf_op jit(solution)/shard_map/pallas_call | solution.py:229
  50.0 3.4 %all-to-all-start.1 = ((bf16[8,3,32,128]{3,2,1,0:T(8,128)(2,1)}), bf16[8,3,32,128]{3,2,1,0:T(8,128)(2,1)S(1)}, u32[]{:S(2)}, u32[]{:S(2)}) async-start(bf16[8,3,32,128]{3,2,1,0:T(8,128)(2,1)} %shard_map.68), calls=%async_computation.1 | async-start | bytes 393216 | tf_op jit(solution)/shard_map/all_to_all | solution.py:329
  53.4 0.8 %collective-permute-start.11 = (bf16[1,1024,128]{2,1,0:T(8,128)(2,1)S(1)}, bf16[1,1024,128]{2,1,0:T(8,128)(2,1)S(1)}, u32[]{:S(2)}, u32[]{:S(2)}) collective-permute-start(bf16[1,1024,128]{2,1,0:T(8,128)(2,1)S(1)} %dynamic-slice_convert_fusion.refs_0_), channel_id=1, source_target_pairs={{0,16},{8,24},{16,0},{24,8},{1,17},{9,25},{17,1},{25,9},{2,18},{10... | collective-permute-start | bytes 786440 | tf_op jit(solution)/shard_map/ppermute | solution.py:33
  54.2 1.1 %dynamic-slice_bitcast_fusion.own_ref = f32[1024,128]{1,0:T(8,128)S(1)} fusion(f32[2,1024,128]{2,1,0:T(8,128)} %convert_add_fusion, s32[]{:T(128)S(6)} %select_n.20), kind=kLoop, calls=%fused_computation.2 | loop fusion | bytes 1048580 | tf_op jit(solution)/shard_map/squeeze | solution.py:331
  55.3 6.2 %collective-permute-done.11 = bf16[1,1024,128]{2,1,0:T(8,128)(2,1)S(1)} collective-permute-done((bf16[1,1024,128]{2,1,0:T(8,128)(2,1)S(1)}, bf16[1,1024,128]{2,1,0:T(8,128)(2,1)S(1)}, u32[]{:S(2)}, u32[]{:S(2)}) %collective-permute-start.11) | collective-permute-done | bytes 262176 | tf_op jit(solution)/shard_map/ppermute | solution.py:33
  61.5 0.1 all-to-all-done.1.p_ref
  61.5 2.1 %shard_map.69 = f32[1024,128]{1,0:T(8,128)} custom-call(s32[2]{0:T(128)S(1)} %copy-done.7, f32[1024,128]{1,0:T(8,128)S(1)} %dynamic-slice_bitcast_fusion.own_ref, bf16[1024,128]{1,0:T(8,128)(2,1)S(1)} %bitcast.10, bf16[8,3,32,128]{3,2,1,0:T(8,128)(2,1)S(1)} %all-to-all-done.1.p_ref, bf16[3,1024,256]{2,1,0:T(8,128)(2,1)S(1)} %copy-done, ...), custom_call_target="tpu_custom_call" | custom-call | flops 201326592 | bytes 2883584 | tf_op jit(solution)/shard_map/pallas_call | solution.py:275
  (21 shorter events, 0.1 us)
Async XLA Ops:
  0.0 7.9 %collective-permute-start = (bf16[1,2,64,512]{3,2,1,0:T(8,128)(2,1)}, bf16[1,2,64,512]{3,2,1,0:T(8,128)(2,1)S(1)}, u32[]{:S(2)}, u32[]{:S(2)}) collective-permute-start(bf16[1,2,64,512]{3,2,1,0:T(8,128)(2,1)} %refs_0_.1), channel_id=1, source_target_pairs={{0,1},{1,0},{2,3},{3,2},{4,5},{5,4},{6,7},{7,6},{8,9},{9,8},{10,11... | collective-permute-start | bytes 393224 | tf_op jit(solution)/shard_map/ppermute | solution.py:33
  2.9 8.3 %collective-permute-start.1 = (bf16[1,2,64,512]{3,2,1,0:T(8,128)(2,1)}, bf16[1,2,64,512]{3,2,1,0:T(8,128)(2,1)S(1)}, u32[]{:S(2)}, u32[]{:S(2)}) collective-permute-start(bf16[1,2,64,512]{3,2,1,0:T(8,128)(2,1)} %refs_0_.1), channel_id=1, source_target_pairs={{0,2},{1,3},{2,0},{3,1},{4,6},{5,7},{6,4},{7,5},{8,10},{9,11},{10,... | collective-permute-start | bytes 393224 | tf_op jit(solution)/shard_map/ppermute | solution.py:33
  4.5 12.9 %collective-permute-start.3 = (bf16[1,2,64,512]{3,2,1,0:T(8,128)(2,1)}, bf16[1,2,64,512]{3,2,1,0:T(8,128)(2,1)S(1)}, u32[]{:S(2)}, u32[]{:S(2)}) collective-permute-start(bf16[1,2,64,512]{3,2,1,0:T(8,128)(2,1)} %refs_0_.1), channel_id=1, source_target_pairs={{0,4},{1,5},{2,6},{3,7},{4,0},{5,1},{6,2},{7,3},{8,12},{9,13},{10,... | collective-permute-start | bytes 393224 | tf_op jit(solution)/shard_map/ppermute | solution.py:33
  7.1 11.8 %collective-permute-start.7 = (bf16[1,2,64,512]{3,2,1,0:T(8,128)(2,1)}, bf16[1,2,64,512]{3,2,1,0:T(8,128)(2,1)S(1)}, u32[]{:S(2)}, u32[]{:S(2)}) collective-permute-start(bf16[1,2,64,512]{3,2,1,0:T(8,128)(2,1)} %refs_0_.1), channel_id=1, source_target_pairs={{0,6},{1,7},{2,4},{3,5},{4,2},{5,3},{6,0},{7,1},{8,14},{9,15},{10,... | collective-permute-start | bytes 393224 | tf_op jit(solution)/shard_map/ppermute | solution.py:33
  7.9 0.7 %copy-start.3 = (bf16[1,2,64,512]{3,2,1,0:T(8,128)(2,1)}, bf16[1,2,64,512]{3,2,1,0:T(8,128)(2,1)S(1)}, u32[]{:S(2)}) copy-start(bf16[1,2,64,512]{3,2,1,0:T(8,128)(2,1)S(1)} %collective-permute-done._.refs_1_) | copy-start | bytes 393220
  10.7 7.2 %collective-permute-start.5 = (bf16[1,2,64,256]{3,2,1,0:T(8,128)(2,1)}, bf16[1,2,64,256]{3,2,1,0:T(8,128)(2,1)S(1)}, u32[]{:S(2)}, u32[]{:S(2)}) collective-permute-start(bf16[1,2,64,256]{3,2,1,0:T(8,128)(2,1)} %shard_map.64._), channel_id=1, source_target_pairs={{0,1},{1,0},{2,3},{3,2},{4,5},{5,4},{6,7},{7,6},{8,9},{9,8},{10,11... | collective-permute-start | bytes 196616 | tf_op jit(solution)/shard_map/ppermute | solution.py:33
  11.3 17.3 %collective-permute-start.2 = (bf16[1,2,64,512]{3,2,1,0:T(8,128)(2,1)S(1)}, bf16[1,2,64,512]{3,2,1,0:T(8,128)(2,1)S(1)}, u32[]{:S(2)}, u32[]{:S(2)}) collective-permute-start(bf16[1,2,64,512]{3,2,1,0:T(8,128)(2,1)S(1)} %collective-permute-done.1.refs_2_), channel_id=1, source_target_pairs={{0,1},{1,0},{2,3},{3,2},{4,5},{5,4},{6,7},{7,6},{8,9},{9,8},{10,11... | collective-permute-start | bytes 393224 | tf_op jit(solution)/shard_map/ppermute | solution.py:33
  17.4 11.2 %collective-permute-start.4 = (bf16[1,2,64,512]{3,2,1,0:T(8,128)(2,1)S(1)}, bf16[1,2,64,512]{3,2,1,0:T(8,128)(2,1)S(1)}, u32[]{:S(2)}, u32[]{:S(2)}) collective-permute-start(bf16[1,2,64,512]{3,2,1,0:T(8,128)(2,1)S(1)} %collective-permute-done.3.refs_4_), channel_id=1, source_target_pairs={{0,1},{1,0},{2,3},{3,2},{4,5},{5,4},{6,7},{7,6},{8,9},{9,8},{10,11... | collective-permute-start | bytes 393224 | tf_op jit(solution)/shard_map/ppermute | solution.py:33
  18.8 6.8 %collective-permute-start.6 = (bf16[1,2,64,256]{3,2,1,0:T(8,128)(2,1)S(1)}, bf16[1,2,64,256]{3,2,1,0:T(8,128)(2,1)S(1)}, u32[]{:S(2)}, u32[]{:S(2)}) collective-permute-start(bf16[1,2,64,256]{3,2,1,0:T(8,128)(2,1)S(1)} %add.25), channel_id=1, source_target_pairs={{0,2},{1,3},{2,0},{3,1},{4,6},{5,7},{6,4},{7,5},{8,10},{9,11},{10,... | collective-permute-start | bytes 196616 | tf_op jit(solution)/shard_map/ppermute | solution.py:33
  18.9 12.5 %collective-permute-start.8 = (bf16[1,2,64,512]{3,2,1,0:T(8,128)(2,1)S(1)}, bf16[1,2,64,512]{3,2,1,0:T(8,128)(2,1)S(1)}, u32[]{:S(2)}, u32[]{:S(2)}) collective-permute-start(bf16[1,2,64,512]{3,2,1,0:T(8,128)(2,1)S(1)} %collective-permute-done.7.refs_0_), channel_id=1, source_target_pairs={{0,1},{1,0},{2,3},{3,2},{4,5},{5,4},{6,7},{7,6},{8,9},{9,8},{10,11... | collective-permute-start | bytes 393224 | tf_op jit(solution)/shard_map/ppermute | solution.py:33
  20.4 1.6 %copy-start.1 = (bf16[1,2,1024,512]{3,2,1,0:T(8,128)(2,1)S(1)}, bf16[1,2,1024,512]{3,2,1,0:T(8,128)(2,1)}, u32[]{:S(2)}) copy-start(bf16[1,2,1024,512]{3,2,1,0:T(8,128)(2,1)} %l_ref.1) | copy-start | bytes 6291460
  22.0 0.8 %copy-start.2 = (bf16[1,2,64,256]{3,2,1,0:T(8,128)(2,1)S(1)}, bf16[1,2,64,256]{3,2,1,0:T(8,128)(2,1)}, u32[]{:S(2)}) copy-start(bf16[1,2,64,256]{3,2,1,0:T(8,128)(2,1)} %shard_map.64._) | copy-start | bytes 196612
  22.9 0.6 copy-start.6
  23.5 0.7 %copy-start.8 = (s32[1,2,8,4]{2,3,1,0:T(4,128)S(1)}, s32[1,2,8,4]{2,3,1,0:T(4,128)}, u32[]{:S(2)}) copy-start(s32[1,2,8,4]{2,3,1,0:T(4,128)} %param.8) | copy-start | bytes 772
  24.2 4.5 %copy-start.4 = (bf16[1,2,64,512]{3,2,1,0:T(8,128)(2,1)S(1)}, bf16[1,2,64,512]{3,2,1,0:T(8,128)(2,1)}, u32[]{:S(2)}) copy-start(bf16[1,2,64,512]{3,2,1,0:T(8,128)(2,1)} %copy-done.3) | copy-start | bytes 393220
  24.2 4.5 %copy-start.5 = (bf16[1,2,64,512]{3,2,1,0:T(8,128)(2,1)S(1)}, bf16[1,2,64,512]{3,2,1,0:T(8,128)(2,1)}, u32[]{:S(2)}) copy-start(bf16[1,2,64,512]{3,2,1,0:T(8,128)(2,1)} %refs_0_.1) | copy-start | bytes 393220
  25.6 5.8 %copy-start.7 = (s32[2]{0:T(128)S(1)}, s32[2]{0:T(128)}, u32[]{:S(2)}) copy-start(s32[2]{0:T(128)} %pad_add_fusion.place_ref) | copy-start | bytes 28
  25.6 5.8 %copy-start.10 = (s32[1,8,4]{1,2,0:T(4,128)S(1)}, s32[1,8,4]{1,2,0:T(4,128)}, u32[]{:S(2)}) copy-start(s32[1,8,4]{1,2,0:T(4,128)} %param.9) | copy-start | bytes 388
  25.7 5.7 %collective-permute-start.9 = (bf16[1,2,64,256]{3,2,1,0:T(8,128)(2,1)S(1)}, bf16[1,2,64,256]{3,2,1,0:T(8,128)(2,1)S(1)}, u32[]{:S(2)}, u32[]{:S(2)}) collective-permute-start(bf16[1,2,64,256]{3,2,1,0:T(8,128)(2,1)S(1)} %add.26.refs_6_), channel_id=1, source_target_pairs={{0,4},{1,5},{2,6},{3,7},{4,0},{5,1},{6,2},{7,3},{8,12},{9,13},{10,... | collective-permute-start | bytes 196616 | tf_op jit(solution)/shard_map/ppermute | solution.py:33
  34.2 14.6 %copy-start.9 = (s32[3]{0:T(128)S(1)}, s32[3]{0:T(128)}, u32[]{:S(2)}) copy-start(s32[3]{0:T(128)} %owner_ref.3) | copy-start | bytes 40
  34.2 7.0 %collective-permute-start.10 = (bf16[2,1024,128]{2,1,0:T(8,128)(2,1)S(1)}, bf16[2,1024,128]{2,1,0:T(8,128)(2,1)S(1)}, u32[]{:S(2)}, u32[]{:S(2)}) collective-permute-start(bf16[2,1024,128]{2,1,0:T(8,128)(2,1)S(1)} %get-tuple-element.9), channel_id=1, source_target_pairs={{0,8},{8,0},{16,24},{24,16},{1,9},{9,1},{17,25},{25,17},{2,10},{10... | collective-permute-start | bytes 1572872 | tf_op jit(solution)/shard_map/ppermute | solution.py:33
  34.3 14.5 %all-to-all-start = ((bf16[32,32,128]{2,1,0:T(8,128)(2,1)}), bf16[32,32,128]{2,1,0:T(8,128)(2,1)S(1)}, u32[]{:S(2)}, u32[]{:S(2)}) async-start(bf16[32,32,128]{2,1,0:T(8,128)(2,1)} %bitcast.6), calls=%async_computation | async-start | bytes 524288 | tf_op jit(solution)/shard_map/all_to_all | solution.py:315
  38.2 2.0 %collective-permute-start.12 = (bf16[1,2,64,256]{3,2,1,0:T(8,128)(2,1)S(1)}, bf16[1,2,64,256]{3,2,1,0:T(8,128)(2,1)S(1)}, u32[]{:S(2)}, u32[]{:S(2)}) collective-permute-start(bf16[1,2,64,256]{3,2,1,0:T(8,128)(2,1)S(1)} %add.27.refs_2_.refs_1_.refs_0_), channel_id=1, source_target_pairs={{0,8},{8,0},{16,24},{24,16},{1,9},{9,1},{17,25},{25,17},{2,10},{10... | collective-permute-start | bytes 196616 | tf_op jit(solution)/shard_map/ppermute | solution.py:33
  38.5 6.3 %collective-permute-start.13 = (bf16[1,2,64,256]{3,2,1,0:T(8,128)(2,1)S(1)}, bf16[1,2,64,256]{3,2,1,0:T(8,128)(2,1)S(1)}, u32[]{:S(2)}, u32[]{:S(2)}) collective-permute-start(bf16[1,2,64,256]{3,2,1,0:T(8,128)(2,1)S(1)} %add.27.refs_2_.refs_1_.refs_0_), channel_id=1, source_target_pairs={{0,16},{8,24},{16,0},{24,8},{1,17},{9,25},{17,1},{25,9},{2,18},{10... | collective-permute-start | bytes 196616 | tf_op jit(solution)/shard_map/ppermute | solution.py:33
  40.2 6.2 %collective-permute-start.14 = (bf16[1,2,64,256]{3,2,1,0:T(8,128)(2,1)S(1)}, bf16[1,2,64,256]{3,2,1,0:T(8,128)(2,1)S(1)}, u32[]{:S(2)}, u32[]{:S(2)}) collective-permute-start(bf16[1,2,64,256]{3,2,1,0:T(8,128)(2,1)S(1)} %collective-permute-done.12.refs_2_.refs_1_), channel_id=1, source_target_pairs={{0,16},{8,24},{16,0},{24,8},{1,17},{9,25},{17,1},{25,9},{2,18},{10... | collective-permute-start | bytes 196616 | tf_op jit(solution)/shard_map/ppermute | solution.py:33
  42.3 19.2 %copy-start = (bf16[3,1024,256]{2,1,0:T(8,128)(2,1)S(1)}, bf16[3,1024,256]{2,1,0:T(8,128)(2,1)}, u32[]{:S(2)}) copy-start(bf16[3,1024,256]{2,1,0:T(8,128)(2,1)} %sep_ref.3) | copy-start | bytes 4718596
  50.0 11.5 %all-to-all-start.1 = ((bf16[8,3,32,128]{3,2,1,0:T(8,128)(2,1)}), bf16[8,3,32,128]{3,2,1,0:T(8,128)(2,1)S(1)}, u32[]{:S(2)}, u32[]{:S(2)}) async-start(bf16[8,3,32,128]{3,2,1,0:T(8,128)(2,1)} %shard_map.68), calls=%async_computation.1 | async-start | bytes 393216 | tf_op jit(solution)/shard_map/all_to_all | solution.py:329
  53.4 8.0 %collective-permute-start.11 = (bf16[1,1024,128]{2,1,0:T(8,128)(2,1)S(1)}, bf16[1,1024,128]{2,1,0:T(8,128)(2,1)S(1)}, u32[]{:S(2)}, u32[]{:S(2)}) collective-permute-start(bf16[1,1024,128]{2,1,0:T(8,128)(2,1)S(1)} %dynamic-slice_convert_fusion.refs_0_), channel_id=1, source_target_pairs={{0,16},{8,24},{16,0},{24,8},{1,17},{9,25},{17,1},{25,9},{2,18},{10... | collective-permute-start | bytes 786440 | tf_op jit(solution)/shard_map/ppermute | solution.py:33

commit v3 on v2

v3 whole, which is shorter than its diff:
```python
import jax
import jax.numpy as jnp
from jax import lax
from jax.experimental import pallas as pl
from jax.experimental.pallas import tpu as pltpu
from jax.sharding import PartitionSpec as P

BLOCK = 128
WS = 256
VMEM_LIMIT = 40 << 20
EARLY_LIMIT = 60 << 20
BOTH = ("layer", "grid")
VMEM = pl.BlockSpec(memory_space=pltpu.VMEM)
HBM = pl.BlockSpec(memory_space=pltpu.HBM)
ANY = pl.BlockSpec(memory_space=pl.ANY)
SMEM = pl.BlockSpec(memory_space=pltpu.SMEM)


def kernel_call(body, out_shape, in_specs, scratch=(), flops=0, nbytes=0, limit=VMEM_LIMIT):
    many = isinstance(out_shape, (tuple, list))
    return pl.pallas_call(
        body,
        out_shape=out_shape,
        in_specs=in_specs,
        out_specs=[VMEM] * len(out_shape) if many else VMEM,
        scratch_shapes=list(scratch),
        compiler_params=pltpu.CompilerParams(vmem_limit_bytes=limit),
        cost_estimate=pl.CostEstimate(flops=flops, bytes_accessed=nbytes, transcendentals=0),
    )


def apart(x, axis, distance):
    return lax.ppermute(x, axis, [(i, i ^ distance) for i in range(lax.axis_size(axis))])


def masks(count):
    top = count.bit_length() - 1
    return [3 << i - 1 for i in range(top - 1, 1, -1)] + [1 << i for i in (1, 0) if i < top]


def together(*xs):
    return lax.optimization_barrier(xs)


def pick_below(sep_panels, sep_owner):
    inner = [n for n in tree(lax.axis_size("layer")) if n[3]]
    wide = max(max(n[3]) for n in inner) + 1
    part = WS // lax.axis_size("layer")

    def body(owner_ref, sep_ref, out_ref, held, sem):
        start = pl.multiple_of(lax.axis_index("layer") * part, part)
        copy = pltpu.make_async_copy(sep_ref.at[:wide, pl.ds(start, part)], held, sem)
        copy.start()
        copy.wait()
        for i, n in enumerate(inner):
            mine = owner_ref[n[0]] == lax.axis_index("grid")
            out_ref[i] = jnp.where(mine, held[...], jnp.zeros(held.shape, held.dtype))

    return kernel_call(
        body,
        jax.ShapeDtypeStruct((len(inner), wide, part, WS), jnp.bfloat16),
        [SMEM, HBM],
        scratch=[pltpu.VMEM((wide, part, WS), jnp.bfloat16), pltpu.SemaphoreType.DMA],
        nbytes=4 * wide * part * WS,
        limit=EARLY_LIMIT,
    )(sep_owner, sep_panels)


def mask_panels(l_panels, panel_fill, order):
    _, panels, rows, width = l_panels.shape
    share = width // lax.axis_size("grid")
    step = min(rows, 256)

    def body(fill_ref, l_ref, out_ref, l_all, sems):
        first = lax.axis_index("grid") * share // BLOCK
        copies = [
            pltpu.make_async_copy(l_ref.at[0, :, r : r + step], l_all.at[:, r : r + step], sems.at[r // step])
            for r in range(0, rows, step)
        ]
        for copy in copies:
            copy.start()
        for r in range(0, rows, step):
            copies[r // step].wait()
            for i, block in enumerate(order):
                j = first ^ block
                for k in range(panels):
                    at = (i * panels + k) * BLOCK
                    for b in range(r, r + step, BLOCK):
                        here = fill_ref[0, k, j, b // BLOCK] != 0
                        tile = l_all[k, b : b + BLOCK, pl.ds(pl.multiple_of(j * BLOCK, BLOCK), BLOCK)]
                        out_ref[b : b + BLOCK, at : at + BLOCK] = jnp.where(here, tile, jnp.zeros_like(tile))

    return kernel_call(
        body,
        jax.ShapeDtypeStruct((rows, panels * width), jnp.bfloat16),
        [SMEM, HBM],
        scratch=[pltpu.VMEM((panels, rows, width), jnp.bfloat16), pltpu.SemaphoreType.DMA((rows // step,))],
        nbytes=4 * panels * rows * width,
    )(panel_fill, pltpu.with_memory_space_constraint(l_panels, pltpu.HBM))


def load_panels(u_refs, pieces, order, u_all, sems, me):
    _, panels, share, _ = u_refs[0].shape
    copies = []
    for i, (k, ref) in enumerate(zip(pieces, u_refs)):
        block, inside = order.index(k * share // BLOCK), (me ^ k) * share % BLOCK
        for p in range(panels):
            at = pl.multiple_of((block * panels + p) * BLOCK + inside, share)
            copies.append(pltpu.make_async_copy(ref.at[0, p], u_all.at[pl.ds(at, share), :], sems.at[i, p]))
            copies[-1].start()
    return copies


def first_part(masked, pieces, order):
    rows, _ = masked.shape
    _, panels, share, columns = pieces[0].shape
    depth = panels * share * len(pieces)
    step = min(rows, 256)

    def body(l_ref, *refs):
        u_refs, (out_ref, u_all, sems) = refs[: len(pieces)], refs[len(pieces) :]
        for copy in load_panels(u_refs, list(pieces), order, u_all, sems, lax.axis_index("grid")):
            copy.wait()
        for r in range(0, rows, step):
            here = slice(r, r + step)
            out_ref[here, :] = jnp.dot(l_ref[here, :depth], u_all[...], preferred_element_type=jnp.float32)

    return kernel_call(
        body,
        jax.ShapeDtypeStruct((rows, columns), jnp.float32),
        [VMEM] + [HBM] * len(pieces),
        scratch=[pltpu.VMEM((depth, columns), jnp.bfloat16), pltpu.SemaphoreType.DMA((len(pieces), panels))],
        flops=2 * rows * depth * columns,
        nbytes=2 * rows * depth + 2 * depth * columns + 4 * rows * columns,
    )(masked, *pieces.values())


def layer_copy(begun, masked, pieces, order, grids, copy_fill):
    rows, columns = begun.shape
    panels, share = next(iter(pieces.values())).shape[1:3]
    layers = lax.axis_size("layer")
    width = columns // layers
    piece_rows = WS // grids
    step = min(rows, 256)
    depth = panels * share * len(pieces)
    done = masked.shape[1] - depth

    def body(fill_ref, begun_ref, l_ref, *refs):
        u_refs, (keep_ref, send_ref, pivot_ref, u_all, sums, sems) = refs[: len(pieces)], refs[len(pieces) :]
        core = lax.rem(lax.axis_index("layer"), 2)
        for copy in load_panels(u_refs, list(pieces), order[-(depth // panels // BLOCK) :], u_all, sems, lax.axis_index("grid")):
            copy.wait()

        def filled(slot, j, row, count):
            start = pl.multiple_of(j * width, width)
            lines = []
            for b in range(row, row + count, BLOCK):
                tiles = []
                for c in range(0, width, BLOCK):
                    fill = fill_ref[0, j * (width // BLOCK) + c // BLOCK, b // BLOCK].astype(jnp.float32)
                    tiles.append(sums[slot, b - row : b - row + BLOCK, pl.ds(start + c, BLOCK)] * -fill)
                lines.append(tiles[0] if len(tiles) == 1 else jnp.concatenate(tiles, 1))
            return lines[0] if len(lines) == 1 else jnp.concatenate(lines, 0)

        for r in range(0, rows, step):
            here, slot = slice(r, r + step), r // step % 2
            sums[slot] = begun_ref[here, :] + jnp.dot(
                l_ref[here, done:], u_all[...], preferred_element_type=jnp.float32
            )
            if r < WS:
                for j in range(layers):
                    low = filled(slot, j, r, step).astype(jnp.bfloat16)
                    for g in range(step // piece_rows):
                        pivot_ref[j, r // piece_rows + g] = low[g * piece_rows : (g + 1) * piece_rows]
            for i in range(layers // 2):
                keep_ref[i, here, :] = filled(slot, 2 * i + core, r, step)
                send_ref[i, here, :] = filled(slot, 2 * i + 1 - core, r, step).astype(jnp.bfloat16)

    return kernel_call(
        body,
        (
            jax.ShapeDtypeStruct((layers // 2, rows, width), jnp.float32),
            jax.ShapeDtypeStruct((layers // 2, rows, width), jnp.bfloat16),
            jax.ShapeDtypeStruct((layers, grids, piece_rows, width), jnp.bfloat16),
        ),
        [SMEM, VMEM, VMEM] + [HBM] * len(pieces),
        scratch=[
            pltpu.VMEM((depth, columns), jnp.bfloat16),
            pltpu.VMEM((2, step, columns), jnp.float32),
            pltpu.SemaphoreType.DMA((len(pieces), panels)),
        ],
        flops=2 * rows * depth * columns,
        nbytes=2 * rows * depth + 2 * depth * columns + 8 * rows * columns,
    )(copy_fill, begun, masked, *pieces.values())


def tree(layers):
    nodes, level = [], 0
    while 2 << level <= layers:
        size = 2 << level
        for j in range(layers // size):
            low = j * size
            below = [n for n, first, span, _ in nodes if low <= first < low + size]
            nodes.append((layers - (layers >> level) + j, low, size, below))
        level += 1
    return nodes


def pick_pivots(candidates, sep_owner, grids, after):
    layers, _, piece_rows, width = candidates.shape
    nodes = tree(layers)

    def body(owner_ref, c_ref, *refs):
        out_ref = refs[-1]
        for node, low, size, _ in nodes:
            owner = owner_ref[node]
            total = c_ref[low, owner].astype(jnp.float32)
            for i in range(low + 1, low + size):
                total = total + c_ref[i, owner].astype(jnp.float32)
            total = total.astype(jnp.bfloat16)
            for g in range(grids):
                out_ref[g, node] = total

    return kernel_call(
        body,
        jax.ShapeDtypeStruct((grids, len(nodes), piece_rows, width), jnp.bfloat16),
        [SMEM, VMEM] + [ANY] * len(after),
        nbytes=4 * candidates.size,
    )(sep_owner, candidates, *after)


def eliminate(own, other, pivots, below, sep_panels):
    rows, width = own.shape
    grids, count, piece_rows, _ = pivots.shape
    nodes = tree(count + 1)
    inner = [n for n in nodes if n[3]]
    _, wide, part, _ = below[0].shape
    step = min(rows, 256)

    def body(own_ref, other_ref, p_ref, sep_ref, *refs):
        below_refs = refs[: len(below)]
        out_ref, all_p, all_below = refs[len(below) :]
        layer = lax.axis_index("layer")
        for k, ref in enumerate(below_refs):
            at = pl.multiple_of((layer ^ k) * part, part)
            for i in range(len(inner)):
                for m in inner[i][3]:
                    all_below[i, m, pl.ds(at, part), :] = ref[i, m]
        for node, _, _, under in nodes:
            at = node * WS
            for g in range(grids):
                all_p[at + g * piece_rows : at + (g + 1) * piece_rows, :] = p_ref[g, node]
            if under:
                which = [n[0] for n in inner].index(node)
                pivot = all_p[at : at + WS, :].astype(jnp.float32)
                for m in under:
                    pivot = pivot - jnp.dot(
                        all_below[which, m], all_p[m * WS : (m + 1) * WS, :], preferred_element_type=jnp.float32
                    )
                all_p[at : at + WS, :] = pivot.astype(jnp.bfloat16)
        for r in range(0, rows, step):
            here = slice(r, r + step)
            total = own_ref[here, :] + other_ref[here, :].astype(jnp.float32)
            for node in range(count):
                total = total - jnp.dot(
                    sep_ref[node, here, :], all_p[node * WS : (node + 1) * WS, :], preferred_element_type=jnp.float32
                )
            out_ref[here, :] = total

    return kernel_call(
        body,
        jax.ShapeDtypeStruct((rows, width), jnp.float32),
        [VMEM] * (4 + len(below)),
        scratch=[
            pltpu.VMEM((count * WS, width), jnp.bfloat16),
            pltpu.VMEM((len(inner), wide, WS, WS), jnp.bfloat16),
        ],
        flops=2 * rows * count * WS * width,
        nbytes=10 * rows * width + 2 * sep_panels.size,
    )(own, other, pivots, sep_panels, *below)


def local(l_panels, u_panels, panel_fill, copy_fill, sep_panels, sep_owner):
    layers, grids = lax.axis_size("layer"), lax.axis_size("grid")
    layer, me = lax.axis_index("layer"), lax.axis_index("grid")

    hops = masks(grids)
    far, near = hops[0], hops[-1]
    pieces = {0: u_panels}
    below = pick_below(sep_panels, sep_owner)
    beside = apart(u_panels, "grid", near)
    for hop in hops[:-1]:
        for k, piece in list(pieces.items()):
            if k == far:
                piece, below = together(piece, below)
            pieces[k ^ hop] = apart(piece, "grid", hop)
    blocks = [k * u_panels.shape[2] // BLOCK for k in pieces]
    order = list(dict.fromkeys(blocks))
    masked = mask_panels(l_panels, jnp.swapaxes(panel_fill, 2, 3), order)
    beside, below = together(beside, below)
    below = below + apart(below, "grid", far)
    last = list(pieces)[-1]
    pieces[near] = beside
    for k in list(pieces)[1:-1]:
        if k == far:
            pieces[k], masked = together(pieces[k], masked)
        if k == last:
            pieces[k], below = together(pieces[k], below)
        pieces[k ^ near] = apart(pieces[k], "grid", near)
    for hop in hops[1:-1]:
        below = below + apart(below, "grid", hop)
    last ^= near
    pieces[last], below = together(pieces[last], below)

    half = len(order) // 2
    early = {k: piece for k, piece in pieces.items() if k * piece.shape[2] // BLOCK in order[:half]}
    late = {k: piece for k, piece in pieces.items() if k not in early}
    begun = first_part(masked, early, order)
    keep, send, candidates = layer_copy(begun, masked, late, order, grids, jnp.swapaxes(copy_fill, 1, 2))
    shape = candidates.shape
    candidates = lax.all_to_all(candidates.reshape((layers * grids,) + shape[2:]), BOTH, 0, 0).reshape(shape)

    below = [below + apart(below, "grid", hops[-1])]
    while len(below) < layers:
        below += [apart(part, "layer", len(below)) for part in below]
    other = apart(send, "layer", 1)
    pivots = None
    bit = 1
    while keep.shape[0] > 1:
        bit *= 2
        half = keep.shape[0] // 2
        total = keep + other.astype(jnp.float32)
        total = total.reshape((half, 2) + total.shape[1:])
        side = (layer // bit) % 2
        keep = lax.dynamic_index_in_dim(total, side, 1, keepdims=False)
        send = lax.dynamic_index_in_dim(total, 1 - side, 1, keepdims=False).astype(jnp.bfloat16)
        if pivots is None:
            pivots = lax.all_to_all(pick_pivots(candidates, sep_owner, grids, [send] + below), "grid", 0, 0)
        other = apart(send, "layer", bit)
    return eliminate(keep[0], other[0], pivots, below, sep_panels)


def solution(mesh):
    return jax.shard_map(
        local,
        mesh=mesh,
        in_specs=(
            P("layer", None, "grid", None),
            P("layer", None, "grid", None),
            P("layer", None, "grid", None),
            P("layer", "grid", None),
            P(None, "grid", None),
            P(),
        ),
        out_specs=P("grid", "layer"),
        check_vma=False,
    )
```

time: 64.1 us -> 60.3 us (0.941)
  local copies, waits for them, and re-layouts: 6.66 us -> 1.83 us
  starting transfers between devices: 25.7 us -> 28.2 us
  other arithmetic: 2.55 us -> 0.14 us
  waiting for transfers between devices: 16.1 us -> 17.7 us
    unnamed x22 -> x14, local copies, waits for them, and re-layouts: 4.39 us -> 0.72 us
    ppermute x15, starting transfers between devices: 18.5 us -> 21.3 us  [apart(): lax.ppermute(x, axis, [(i, i ^ distance) for i in range(lax.axis_size(axi...]
    pallas_call x2, Pallas kernels: 4.76 us -> 3.01 us  [the longest x1 1.52 us: eliminate(): kernel_call(body, jax.ShapeDtypeStruct((rows, width), jnp.float32), [VMEM...]
    ppermute x15, waiting for transfers between devices: 13.6 us -> 15.2 us  [apart(): lax.ppermute(x, axis, [(i, i ^ distance) for i in range(lax.axis_size(axi...]
    convert_element_type x1, local copies, waits for them, and re-layouts: 1.19 us -> 0.04 us  [local(): lax.dynamic_index_in_dim(total, 1 - side, 1, keepdims=False)]
    add x1, other arithmetic: 1.07 us -> 0.09 us  [local(): total = keep + other.astype(jnp.float32)]
    pallas_call x1, Pallas kernels: 1.43 us -> 2.33 us  [mask_panels(): kernel_call(body, jax.ShapeDtypeStruct((rows, panels * width), jnp.bfloat...]
    add x3, other arithmetic: 0.9 us -> 0.06 us  [the longest x1 0.02 us: local(): below = [below + apart(below, 'grid', hops[-1])]]
  transfers between devices with their start and end apart: 17 -> 17, of which waited for: 6 -> 10; matrix products, arithmetic and copies ran while one was open for 8% -> 2% of each run, Pallas kernels for 10% -> 10%
where the time goes in v3:
time: 60.3 us; the launch traced here: 59.9 us
  starting transfers between devices  28.2 us (47%)
  waiting for transfers between devices  17.7 us (29%)
  Pallas kernels  11.9 us (20%)
  local copies, waits for them, and re-layouts  1.83 us (3%)
    ppermute x15, starting transfers between devices, apart(): lax.ppermute(x, axis, [(i, i ^ distance) for i in range(lax.axis_size(axi...  21.3 us
    ppermute x15, waiting for transfers between devices, apart(): lax.ppermute(x, axis, [(i, i ^ distance) for i in range(lax.axis_size(axi...  15.2 us
    all_to_all x1, starting transfers between devices, local(): lax.all_to_all(candidates.reshape((layers * grids,) + shape[2:]), BOTH, 0...  3.49 us
    all_to_all x1, starting transfers between devices, local(): lax.all_to_all(pick_pivots(candidates, sep_owner, grids, [send] + below),...  3.39 us
    pallas_call x1, Pallas kernels, layer_copy(): kernel_call(body, (jax.ShapeDtypeStruct((layers // 2, rows, width), jnp.f...  3.17 us
    all_to_all x1, waiting for transfers between devices, local(): lax.all_to_all(candidates.reshape((layers * grids,) + shape[2:]), BOTH, 0...  2.43 us
    pallas_call x1, Pallas kernels, mask_panels(): kernel_call(body, jax.ShapeDtypeStruct((rows, panels * width), jnp.bfloat...  2.33 us
    pallas_call x1, Pallas kernels, pick_below(): kernel_call(body, jax.ShapeDtypeStruct((len(inner), wide, part, WS), jnp....  2.15 us
  transfers between devices with their start and end apart: 17, of which 10 were waited for; matrix products, arithmetic and copies ran while one was open for 2% of the time, Pallas kernels for 10%

profile of v3, /device:TPU:0, one launch (start us, length us, event | category | flops | bytes accessed | tf_op | source)
XLA Modules:
  0.0 59.9 jit_solution(6977649941914221271)
XLA Ops:
  0.0 5.0 %collective-permute-start = (bf16[1,2,64,512]{3,2,1,0:T(8,128)(2,1)}, bf16[1,2,64,512]{3,2,1,0:T(8,128)(2,1)S(1)}, u32[]{:S(2)}, u32[]{:S(2)}) collective-permute-start(bf16[1,2,64,512]{3,2,1,0:T(8,128)(2,1)} %refs_0_.1), channel_id=1, source_target_pairs={{0,6},{1,7},{2,4},{3,5},{4,2},{5,3},{6,0},{7,1},{8,14},{9,15},{10,... | collective-permute-start | bytes 393224 | tf_op jit(solution)/shard_map/ppermute | solution.py:33
  5.0 1.5 %collective-permute-start.1 = (bf16[1,2,64,512]{3,2,1,0:T(8,128)(2,1)}, bf16[1,2,64,512]{3,2,1,0:T(8,128)(2,1)S(1)}, u32[]{:S(2)}, u32[]{:S(2)}) collective-permute-start(bf16[1,2,64,512]{3,2,1,0:T(8,128)(2,1)} %refs_0_.1), channel_id=1, source_target_pairs={{0,1},{1,0},{2,3},{3,2},{4,5},{5,4},{6,7},{7,6},{8,9},{9,8},{10,11... | collective-permute-start | bytes 393224 | tf_op jit(solution)/shard_map/ppermute | solution.py:33
  6.5 2.2 %shard_map.65 = bf16[1,2,64,256]{3,2,1,0:T(8,128)(2,1)} custom-call(s32[3]{0:T(128)} %owner_ref.3, bf16[3,1024,256]{2,1,0:T(8,128)(2,1)} %sep_ref.3), custom_call_target="tpu_custom_call" | custom-call | bytes 131072 | tf_op jit(solution)/shard_map/pallas_call | solution.py:59
  8.7 0.2 collective-permute-done.refs_1_
  8.9 2.4 %collective-permute-start.4 = (bf16[1,2,64,512]{3,2,1,0:T(8,128)(2,1)S(1)}, bf16[1,2,64,512]{3,2,1,0:T(8,128)(2,1)S(1)}, u32[]{:S(2)}, u32[]{:S(2)}) collective-permute-start(bf16[1,2,64,512]{3,2,1,0:T(8,128)(2,1)S(1)} %collective-permute-done.refs_1_), channel_id=1, source_target_pairs={{0,2},{1,3},{2,0},{3,1},{4,6},{5,7},{6,4},{7,5},{8,10},{9,11},{10,... | collective-permute-start | bytes 393224 | tf_op jit(solution)/shard_map/ppermute | solution.py:33
  11.3 0.0 collective-permute-start.3
  11.3 0.0 collective-permute-done.1.refs_2_
  11.3 3.1 %collective-permute-start.5 = (bf16[1,2,64,256]{3,2,1,0:T(8,128)(2,1)}, bf16[1,2,64,256]{3,2,1,0:T(8,128)(2,1)S(1)}, u32[]{:S(2)}, u32[]{:S(2)}) collective-permute-start(bf16[1,2,64,256]{3,2,1,0:T(8,128)(2,1)} %shard_map.65), channel_id=1, source_target_pairs={{0,6},{1,7},{2,4},{3,5},{4,2},{5,3},{6,0},{7,1},{8,14},{9,15},{10,... | collective-permute-start | bytes 196616 | tf_op jit(solution)/shard_map/ppermute | solution.py:33
  14.4 0.7 %copy-done.2 = s32[1,2,8,4]{2,3,1,0:T(4,128)S(1)} copy-done((s32[1,2,8,4]{2,3,1,0:T(4,128)S(1)}, s32[1,2,8,4]{2,3,1,0:T(4,128)}, u32[]{:S(2)}) %copy-start.2) | copy-done | bytes 280
  15.1 2.3 %shard_map.64.l_ref = bf16[1024,1024]{1,0:T(8,128)(2,1)S(1)} custom-call(s32[1,2,4,8]{3,2,1,0:T(4,128)S(1)} %bitcast.9, bf16[1,2,1024,512]{3,2,1,0:T(8,128)(2,1)} %l_ref.1), custom_call_target="tpu_custom_call" | custom-call | bytes 4194304 | tf_op jit(solution)/shard_map/pallas_call | solution.py:93
  17.5 1.6 %collective-permute-start.2 = (bf16[1,2,64,512]{3,2,1,0:T(8,128)(2,1)S(1)}, bf16[1,2,64,512]{3,2,1,0:T(8,128)(2,1)S(1)}, u32[]{:S(2)}, u32[]{:S(2)}) collective-permute-start(bf16[1,2,64,512]{3,2,1,0:T(8,128)(2,1)S(1)} %collective-permute-done.refs_1_), channel_id=1, source_target_pairs={{0,1},{1,0},{2,3},{3,2},{4,5},{5,4},{6,7},{7,6},{8,9},{9,8},{10,11... | collective-permute-start | bytes 393224 | tf_op jit(solution)/shard_map/ppermute | solution.py:33
  19.0 0.5 collective-permute-done.5
  19.5 0.0 copy-done.6
  19.5 0.0 copy-start.4
  19.5 0.0 collective-permute-done.4.refs_1_
  19.5 1.6 %collective-permute-start.7 = (bf16[1,2,64,512]{3,2,1,0:T(8,128)(2,1)S(1)}, bf16[1,2,64,512]{3,2,1,0:T(8,128)(2,1)S(1)}, u32[]{:S(2)}, u32[]{:S(2)}) collective-permute-start(bf16[1,2,64,512]{3,2,1,0:T(8,128)(2,1)S(1)} %collective-permute-done.4.refs_1_), channel_id=1, source_target_pairs={{0,1},{1,0},{2,3},{3,2},{4,5},{5,4},{6,7},{7,6},{8,9},{9,8},{10,11... | collective-permute-start | bytes 393224 | tf_op jit(solution)/shard_map/ppermute | solution.py:33
  21.1 0.0 collective-permute-done.3.refs_0_
  21.1 0.5 collective-permute-start.6
  21.6 0.0 collective-permute-start.8
  21.6 2.2 %collective-permute-done.2.refs_3_ = bf16[1,2,64,512]{3,2,1,0:T(8,128)(2,1)S(1)} collective-permute-done((bf16[1,2,64,512]{3,2,1,0:T(8,128)(2,1)S(1)}, bf16[1,2,64,512]{3,2,1,0:T(8,128)(2,1)S(1)}, u32[]{:S(2)}, u32[]{:S(2)}) %collective-permute-start.2) | collective-permute-done | bytes 131104 | tf_op jit(solution)/shard_map/ppermute | solution.py:33
  23.8 0.0 copy-done.1
  23.9 1.5 %shard_map.66.begun_ref = f32[1024,512]{1,0:T(8,128)S(1)} custom-call(bf16[1024,1024]{1,0:T(8,128)(2,1)S(1)} %shard_map.64.l_ref, bf16[1,2,64,512]{3,2,1,0:T(8,128)(2,1)S(1)} %copy-done.1, bf16[1,2,64,512]{3,2,1,0:T(8,128)(2,1)S(1)} %collective-permute-done.refs_1_, bf16[1,2,64,512]{3,2,1,0:T(8,128)(2,1)S(1)} %collective-permute-done.1.refs_2_, ...), custom_call_target="tpu_custom_call" | custom-call | flops 536870912 | bytes 3670016 | tf_op jit(solution)/shard_map/pallas_call | solution.py:128
  25.3 0.6 collective-permute-done.8
  25.9 0.0 collective-permute-done.7.refs_3_
  25.9 0.7 %collective-permute-done.6.refs_2_ = bf16[1,2,64,512]{3,2,1,0:T(8,128)(2,1)S(1)} collective-permute-done((bf16[1,2,64,512]{3,2,1,0:T(8,128)(2,1)S(1)}, bf16[1,2,64,512]{3,2,1,0:T(8,128)(2,1)S(1)}, u32[]{:S(2)}, u32[]{:S(2)}) %collective-permute-start.6) | collective-permute-done | bytes 131104 | tf_op jit(solution)/shard_map/ppermute | solution.py:33
  26.7 3.2 %shard_map.67 = (f32[2,1024,128]{2,1,0:T(8,128)S(1)}, bf16[2,1024,128]{2,1,0:T(8,128)(2,1)S(1)}, bf16[4,8,32,128]{3,2,1,0:T(8,128)(2,1)}) custom-call(s32[1,4,8]{2,1,0:T(4,128)S(1)} %bitcast.10, f32[1024,512]{1,0:T(8,128)S(1)} %shard_map.66.begun_ref, bf16[1024,1024]{1,0:T(8,128)(2,1)S(1)} %shard_map.64.l_ref, ...), custom_call_target="tpu_custom_call" | custom-call | flops 536870912 | bytes 5767168 | tf_op jit(solution)/shard_map/pallas_call | solution.py:179
  29.8 0.0 copy-start.3
  29.9 0.1 collective-permute-start.9
  29.9 1.6 %collective-permute-start.11 = (bf16[1,2,64,256]{3,2,1,0:T(8,128)(2,1)S(1)}, bf16[1,2,64,256]{3,2,1,0:T(8,128)(2,1)S(1)}, u32[]{:S(2)}, u32[]{:S(2)}) collective-permute-start(bf16[1,2,64,256]{3,2,1,0:T(8,128)(2,1)S(1)} %add.26), channel_id=1, source_target_pairs={{0,1},{1,0},{2,3},{3,2},{4,5},{5,4},{6,7},{7,6},{8,9},{9,8},{10,11... | collective-permute-start | bytes 196616 | tf_op jit(solution)/shard_map/ppermute | solution.py:33
  31.5 3.5 %all-to-all-start = ((bf16[32,32,128]{2,1,0:T(8,128)(2,1)}), bf16[32,32,128]{2,1,0:T(8,128)(2,1)S(1)}, u32[]{:S(2)}, u32[]{:S(2)}) async-start(bf16[32,32,128]{2,1,0:T(8,128)(2,1)} %bitcast.4), calls=%async_computation | async-start | bytes 524288 | tf_op jit(solution)/shard_map/all_to_all | solution.py:321
  35.0 0.0 collective-permute-done.11
  35.0 0.3 collective-permute-start.12
  35.3 1.7 %collective-permute-start.13 = (bf16[1,2,64,256]{3,2,1,0:T(8,128)(2,1)S(1)}, bf16[1,2,64,256]{3,2,1,0:T(8,128)(2,1)S(1)}, u32[]{:S(2)}, u32[]{:S(2)}) collective-permute-start(bf16[1,2,64,256]{3,2,1,0:T(8,128)(2,1)S(1)} %add.31.refs_1_.refs_0_), channel_id=1, source_target_pairs={{0,16},{8,24},{16,0},{24,8},{1,17},{9,25},{17,1},{25,9},{2,18},{10... | collective-permute-start | bytes 196616 | tf_op jit(solution)/shard_map/ppermute | solution.py:33
  37.0 0.0 collective-permute-done.12.refs_2_.refs_1_
  37.0 1.1 %collective-permute-start.14 = (bf16[1,2,64,256]{3,2,1,0:T(8,128)(2,1)S(1)}, bf16[1,2,64,256]{3,2,1,0:T(8,128)(2,1)S(1)}, u32[]{:S(2)}, u32[]{:S(2)}) collective-permute-start(bf16[1,2,64,256]{3,2,1,0:T(8,128)(2,1)S(1)} %collective-permute-done.12.refs_2_.refs_1_), channel_id=1, source_target_pairs={{0,16},{8,24},{16,0},{24,8},{1,17},{9,25},{17,1},{25,9},{2,18},{10... | collective-permute-start | bytes 196616 | tf_op jit(solution)/shard_map/ppermute | solution.py:33
  38.1 0.0 collective-permute-done.9
  38.1 0.1 convert_add_fusion
  38.2 0.0 copy-start
  38.3 3.4 %collective-permute-done.13.refs_3_.refs_2_ = bf16[1,2,64,256]{3,2,1,0:T(8,128)(2,1)S(1)} collective-permute-done((bf16[1,2,64,256]{3,2,1,0:T(8,128)(2,1)S(1)}, bf16[1,2,64,256]{3,2,1,0:T(8,128)(2,1)S(1)}, u32[]{:S(2)}, u32[]{:S(2)}) %collective-permute-start.13) | collective-permute-done | bytes 65568 | tf_op jit(solution)/shard_map/ppermute | solution.py:33
  41.6 1.6 %collective-permute-done.14.refs_4_.refs_3_ = bf16[1,2,64,256]{3,2,1,0:T(8,128)(2,1)S(1)} collective-permute-done((bf16[1,2,64,256]{3,2,1,0:T(8,128)(2,1)S(1)}, bf16[1,2,64,256]{3,2,1,0:T(8,128)(2,1)S(1)}, u32[]{:S(2)}, u32[]{:S(2)}) %collective-permute-start.14) | collective-permute-done | bytes 65568 | tf_op jit(solution)/shard_map/ppermute | solution.py:33
  43.2 2.4 %all-to-all-done = bf16[32,32,128]{2,1,0:T(8,128)(2,1)S(1)} async-done(((bf16[32,32,128]{2,1,0:T(8,128)(2,1)}), bf16[32,32,128]{2,1,0:T(8,128)(2,1)S(1)}, u32[]{:S(2)}, u32[]{:S(2)}) %all-to-all-start) | async-done | bytes 262176 | tf_op jit(solution)/shard_map/all_to_all | solution.py:321
  45.6 1.2 %shard_map.68 = bf16[8,3,32,128]{3,2,1,0:T(8,128)(2,1)} custom-call(s32[3]{0:T(128)S(1)} %copy-done.3, bf16[4,8,32,128]{3,2,1,0:T(8,128)(2,1)S(1)} %bitcast.7, bf16[1,1024,128]{2,1,0:T(8,128)(2,1)S(1)} %dynamic-slice_convert_fusion.refs_0_, bf16[1,2,64,256]{3,2,1,0:T(8,128)(2,1)S(1)} %add.31.refs_1_.refs_0_, ...), custom_call_target="tpu_custom_call" | custom-call | bytes 524288 | tf_op jit(solution)/shard_map/pallas_call | solution.py:224
  46.9 3.4 %all-to-all-start.1 = ((bf16[8,3,32,128]{3,2,1,0:T(8,128)(2,1)}), bf16[8,3,32,128]{3,2,1,0:T(8,128)(2,1)S(1)}, u32[]{:S(2)}, u32[]{:S(2)}) async-start(bf16[8,3,32,128]{3,2,1,0:T(8,128)(2,1)} %shard_map.68), calls=%async_computation.1 | async-start | bytes 393216 | tf_op jit(solution)/shard_map/all_to_all | solution.py:338
  50.3 0.8 %collective-permute-start.10 = (bf16[1,1024,128]{2,1,0:T(8,128)(2,1)S(1)}, bf16[1,1024,128]{2,1,0:T(8,128)(2,1)S(1)}, u32[]{:S(2)}, u32[]{:S(2)}) collective-permute-start(bf16[1,1024,128]{2,1,0:T(8,128)(2,1)S(1)} %dynamic-slice_convert_fusion.refs_0_), channel_id=1, source_target_pairs={{0,16},{8,24},{16,0},{24,8},{1,17},{9,25},{17,1},{25,9},{2,18},{10... | collective-permute-start | bytes 786440 | tf_op jit(solution)/shard_map/ppermute | solution.py:33
  51.1 1.1 %dynamic-slice_bitcast_fusion.own_ref = f32[1024,128]{1,0:T(8,128)S(1)} fusion(f32[2,1024,128]{2,1,0:T(8,128)} %copy-done.5, s32[]{:T(128)S(6)} %select_n.20), kind=kLoop, calls=%fused_computation.2 | loop fusion | bytes 1048580 | tf_op jit(solution)/shard_map/squeeze | solution.py:340
  52.2 6.1 %collective-permute-done.10 = bf16[1,1024,128]{2,1,0:T(8,128)(2,1)S(1)} collective-permute-done((bf16[1,1024,128]{2,1,0:T(8,128)(2,1)S(1)}, bf16[1,1024,128]{2,1,0:T(8,128)(2,1)S(1)}, u32[]{:S(2)}, u32[]{:S(2)}) %collective-permute-start.10) | collective-permute-done | bytes 262176 | tf_op jit(solution)/shard_map/ppermute | solution.py:33
  58.3 0.1 all-to-all-done.1.p_ref
  58.4 1.5 %shard_map.69 = f32[1024,128]{1,0:T(8,128)} custom-call(f32[1024,128]{1,0:T(8,128)S(1)} %dynamic-slice_bitcast_fusion.own_ref, bf16[1024,128]{1,0:T(8,128)(2,1)S(1)} %bitcast.8, bf16[8,3,32,128]{3,2,1,0:T(8,128)(2,1)S(1)} %all-to-all-done.1.p_ref, bf16[3,1024,256]{2,1,0:T(8,128)(2,1)S(1)} %copy-done, bf16[1,2,64,256]{3,2,1,0:T(8,128)(2,1)S(1)} %add.31.refs_1_.refs_0_, ...), custom_call_target="tpu_custom_call" | custom-call | flops 201326592 | bytes 2883584 | tf_op jit(solution)/shard_map/pallas_call | solution.py:270
  (12 shorter events, 0.1 us)
Async XLA Ops:
  0.0 8.9 %collective-permute-start = (bf16[1,2,64,512]{3,2,1,0:T(8,128)(2,1)}, bf16[1,2,64,512]{3,2,1,0:T(8,128)(2,1)S(1)}, u32[]{:S(2)}, u32[]{:S(2)}) collective-permute-start(bf16[1,2,64,512]{3,2,1,0:T(8,128)(2,1)} %refs_0_.1), channel_id=1, source_target_pairs={{0,6},{1,7},{2,4},{3,5},{4,2},{5,3},{6,0},{7,1},{8,14},{9,15},{10,... | collective-permute-start | bytes 393224 | tf_op jit(solution)/shard_map/ppermute | solution.py:33
  5.0 6.3 %collective-permute-start.1 = (bf16[1,2,64,512]{3,2,1,0:T(8,128)(2,1)}, bf16[1,2,64,512]{3,2,1,0:T(8,128)(2,1)S(1)}, u32[]{:S(2)}, u32[]{:S(2)}) collective-permute-start(bf16[1,2,64,512]{3,2,1,0:T(8,128)(2,1)} %refs_0_.1), channel_id=1, source_target_pairs={{0,1},{1,0},{2,3},{3,2},{4,5},{5,4},{6,7},{7,6},{8,9},{9,8},{10,11... | collective-permute-start | bytes 393224 | tf_op jit(solution)/shard_map/ppermute | solution.py:33
  8.9 10.7 %collective-permute-start.4 = (bf16[1,2,64,512]{3,2,1,0:T(8,128)(2,1)S(1)}, bf16[1,2,64,512]{3,2,1,0:T(8,128)(2,1)S(1)}, u32[]{:S(2)}, u32[]{:S(2)}) collective-permute-start(bf16[1,2,64,512]{3,2,1,0:T(8,128)(2,1)S(1)} %collective-permute-done.refs_1_), channel_id=1, source_target_pairs={{0,2},{1,3},{2,0},{3,1},{4,6},{5,7},{6,4},{7,5},{8,10},{9,11},{10,... | collective-permute-start | bytes 393224 | tf_op jit(solution)/shard_map/ppermute | solution.py:33
  11.3 9.8 %collective-permute-start.3 = (bf16[1,2,64,512]{3,2,1,0:T(8,128)(2,1)}, bf16[1,2,64,512]{3,2,1,0:T(8,128)(2,1)S(1)}, u32[]{:S(2)}, u32[]{:S(2)}) collective-permute-start(bf16[1,2,64,512]{3,2,1,0:T(8,128)(2,1)} %refs_0_.1), channel_id=1, source_target_pairs={{0,2},{1,3},{2,0},{3,1},{4,6},{5,7},{6,4},{7,5},{8,10},{9,11},{10,... | collective-permute-start | bytes 393224 | tf_op jit(solution)/shard_map/ppermute | solution.py:33
  11.3 8.2 %collective-permute-start.5 = (bf16[1,2,64,256]{3,2,1,0:T(8,128)(2,1)}, bf16[1,2,64,256]{3,2,1,0:T(8,128)(2,1)S(1)}, u32[]{:S(2)}, u32[]{:S(2)}) collective-permute-start(bf16[1,2,64,256]{3,2,1,0:T(8,128)(2,1)} %shard_map.65), channel_id=1, source_target_pairs={{0,6},{1,7},{2,4},{3,5},{4,2},{5,3},{6,0},{7,1},{8,14},{9,15},{10,... | collective-permute-start | bytes 196616 | tf_op jit(solution)/shard_map/ppermute | solution.py:33
  14.4 0.7 %copy-start.2 = (s32[1,2,8,4]{2,3,1,0:T(4,128)S(1)}, s32[1,2,8,4]{2,3,1,0:T(4,128)}, u32[]{:S(2)}) copy-start(s32[1,2,8,4]{2,3,1,0:T(4,128)} %param.8) | copy-start | bytes 772
  15.1 4.4 %copy-start.6 = (bf16[1,2,64,256]{3,2,1,0:T(8,128)(2,1)S(1)}, bf16[1,2,64,256]{3,2,1,0:T(8,128)(2,1)}, u32[]{:S(2)}) copy-start(bf16[1,2,64,256]{3,2,1,0:T(8,128)(2,1)} %shard_map.65) | copy-start | bytes 196612
  15.1 8.7 %copy-start.1 = (bf16[1,2,64,512]{3,2,1,0:T(8,128)(2,1)S(1)}, bf16[1,2,64,512]{3,2,1,0:T(8,128)(2,1)}, u32[]{:S(2)}) copy-start(bf16[1,2,64,512]{3,2,1,0:T(8,128)(2,1)} %refs_0_.1) | copy-start | bytes 393220
  17.5 6.4 %collective-permute-start.2 = (bf16[1,2,64,512]{3,2,1,0:T(8,128)(2,1)S(1)}, bf16[1,2,64,512]{3,2,1,0:T(8,128)(2,1)S(1)}, u32[]{:S(2)}, u32[]{:S(2)}) collective-permute-start(bf16[1,2,64,512]{3,2,1,0:T(8,128)(2,1)S(1)} %collective-permute-done.refs_1_), channel_id=1, source_target_pairs={{0,1},{1,0},{2,3},{3,2},{4,5},{5,4},{6,7},{7,6},{8,9},{9,8},{10,11... | collective-permute-start | bytes 393224 | tf_op jit(solution)/shard_map/ppermute | solution.py:33
  19.5 7.1 %copy-start.4 = (s32[1,8,4]{1,2,0:T(4,128)S(1)}, s32[1,8,4]{1,2,0:T(4,128)}, u32[]{:S(2)}) copy-start(s32[1,8,4]{1,2,0:T(4,128)} %param.9) | copy-start | bytes 388
  19.5 6.4 %collective-permute-start.7 = (bf16[1,2,64,512]{3,2,1,0:T(8,128)(2,1)S(1)}, bf16[1,2,64,512]{3,2,1,0:T(8,128)(2,1)S(1)}, u32[]{:S(2)}, u32[]{:S(2)}) collective-permute-start(bf16[1,2,64,512]{3,2,1,0:T(8,128)(2,1)S(1)} %collective-permute-done.4.refs_1_), channel_id=1, source_target_pairs={{0,1},{1,0},{2,3},{3,2},{4,5},{5,4},{6,7},{7,6},{8,9},{9,8},{10,11... | collective-permute-start | bytes 393224 | tf_op jit(solution)/shard_map/ppermute | solution.py:33
  21.1 5.6 %collective-permute-start.6 = (bf16[1,2,64,512]{3,2,1,0:T(8,128)(2,1)S(1)}, bf16[1,2,64,512]{3,2,1,0:T(8,128)(2,1)S(1)}, u32[]{:S(2)}, u32[]{:S(2)}) collective-permute-start(bf16[1,2,64,512]{3,2,1,0:T(8,128)(2,1)S(1)} %collective-permute-done.3.refs_0_), channel_id=1, source_target_pairs={{0,1},{1,0},{2,3},{3,2},{4,5},{5,4},{6,7},{7,6},{8,9},{9,8},{10,11... | collective-permute-start | bytes 393224 | tf_op jit(solution)/shard_map/ppermute | solution.py:33
  21.6 4.3 %collective-permute-start.8 = (bf16[1,2,64,256]{3,2,1,0:T(8,128)(2,1)S(1)}, bf16[1,2,64,256]{3,2,1,0:T(8,128)(2,1)S(1)}, u32[]{:S(2)}, u32[]{:S(2)}) collective-permute-start(bf16[1,2,64,256]{3,2,1,0:T(8,128)(2,1)S(1)} %add.25), channel_id=1, source_target_pairs={{0,2},{1,3},{2,0},{3,1},{4,6},{5,7},{6,4},{7,5},{8,10},{9,11},{10,... | collective-permute-start | bytes 196616 | tf_op jit(solution)/shard_map/ppermute | solution.py:33
  29.8 15.8 %copy-start.3 = (s32[3]{0:T(128)S(1)}, s32[3]{0:T(128)}, u32[]{:S(2)}) copy-start(s32[3]{0:T(128)} %owner_ref.3) | copy-start | bytes 40
  29.9 8.3 %collective-permute-start.9 = (bf16[2,1024,128]{2,1,0:T(8,128)(2,1)S(1)}, bf16[2,1024,128]{2,1,0:T(8,128)(2,1)S(1)}, u32[]{:S(2)}, u32[]{:S(2)}) collective-permute-start(bf16[2,1024,128]{2,1,0:T(8,128)(2,1)S(1)} %get-tuple-element.28), channel_id=1, source_target_pairs={{0,8},{8,0},{16,24},{24,16},{1,9},{9,1},{17,25},{25,17},{2,10},{10... | collective-permute-start | bytes 1572872 | tf_op jit(solution)/shard_map/ppermute | solution.py:33
  29.9 5.1 %collective-permute-start.11 = (bf16[1,2,64,256]{3,2,1,0:T(8,128)(2,1)S(1)}, bf16[1,2,64,256]{3,2,1,0:T(8,128)(2,1)S(1)}, u32[]{:S(2)}, u32[]{:S(2)}) collective-permute-start(bf16[1,2,64,256]{3,2,1,0:T(8,128)(2,1)S(1)} %add.26), channel_id=1, source_target_pairs={{0,1},{1,0},{2,3},{3,2},{4,5},{5,4},{6,7},{7,6},{8,9},{9,8},{10,11... | collective-permute-start | bytes 196616 | tf_op jit(solution)/shard_map/ppermute | solution.py:33
  31.5 14.1 %all-to-all-start = ((bf16[32,32,128]{2,1,0:T(8,128)(2,1)}), bf16[32,32,128]{2,1,0:T(8,128)(2,1)S(1)}, u32[]{:S(2)}, u32[]{:S(2)}) async-start(bf16[32,32,128]{2,1,0:T(8,128)(2,1)} %bitcast.4), calls=%async_computation | async-start | bytes 524288 | tf_op jit(solution)/shard_map/all_to_all | solution.py:321
  35.0 2.0 %collective-permute-start.12 = (bf16[1,2,64,256]{3,2,1,0:T(8,128)(2,1)S(1)}, bf16[1,2,64,256]{3,2,1,0:T(8,128)(2,1)S(1)}, u32[]{:S(2)}, u32[]{:S(2)}) collective-permute-start(bf16[1,2,64,256]{3,2,1,0:T(8,128)(2,1)S(1)} %add.31.refs_1_.refs_0_), channel_id=1, source_target_pairs={{0,8},{8,0},{16,24},{24,16},{1,9},{9,1},{17,25},{25,17},{2,10},{10... | collective-permute-start | bytes 196616 | tf_op jit(solution)/shard_map/ppermute | solution.py:33
  35.3 6.3 %collective-permute-start.13 = (bf16[1,2,64,256]{3,2,1,0:T(8,128)(2,1)S(1)}, bf16[1,2,64,256]{3,2,1,0:T(8,128)(2,1)S(1)}, u32[]{:S(2)}, u32[]{:S(2)}) collective-permute-start(bf16[1,2,64,256]{3,2,1,0:T(8,128)(2,1)S(1)} %add.31.refs_1_.refs_0_), channel_id=1, source_target_pairs={{0,16},{8,24},{16,0},{24,8},{1,17},{9,25},{17,1},{25,9},{2,18},{10... | collective-permute-start | bytes 196616 | tf_op jit(solution)/shard_map/ppermute | solution.py:33
  37.0 6.2 %collective-permute-start.14 = (bf16[1,2,64,256]{3,2,1,0:T(8,128)(2,1)S(1)}, bf16[1,2,64,256]{3,2,1,0:T(8,128)(2,1)S(1)}, u32[]{:S(2)}, u32[]{:S(2)}) collective-permute-start(bf16[1,2,64,256]{3,2,1,0:T(8,128)(2,1)S(1)} %collective-permute-done.12.refs_2_.refs_1_), channel_id=1, source_target_pairs={{0,16},{8,24},{16,0},{24,8},{1,17},{9,25},{17,1},{25,9},{2,18},{10... | collective-permute-start | bytes 196616 | tf_op jit(solution)/shard_map/ppermute | solution.py:33
  38.2 3.4 %copy-start.5 = (f32[2,1024,128]{2,1,0:T(8,128)}, f32[2,1024,128]{2,1,0:T(8,128)S(1)}, u32[]{:S(2)}) copy-start(f32[2,1024,128]{2,1,0:T(8,128)S(1)} %convert_add_fusion) | copy-start | bytes 3145732
  38.2 20.1 %copy-start = (bf16[3,1024,256]{2,1,0:T(8,128)(2,1)S(1)}, bf16[3,1024,256]{2,1,0:T(8,128)(2,1)}, u32[]{:S(2)}) copy-start(bf16[3,1024,256]{2,1,0:T(8,128)(2,1)} %sep_ref.3) | copy-start | bytes 4718596
  46.9 11.5 %all-to-all-start.1 = ((bf16[8,3,32,128]{3,2,1,0:T(8,128)(2,1)}), bf16[8,3,32,128]{3,2,1,0:T(8,128)(2,1)S(1)}, u32[]{:S(2)}, u32[]{:S(2)}) async-start(bf16[8,3,32,128]{3,2,1,0:T(8,128)(2,1)} %shard_map.68), calls=%async_computation.1 | async-start | bytes 393216 | tf_op jit(solution)/shard_map/all_to_all | solution.py:338
  50.3 8.0 %collective-permute-start.10 = (bf16[1,1024,128]{2,1,0:T(8,128)(2,1)S(1)}, bf16[1,1024,128]{2,1,0:T(8,128)(2,1)S(1)}, u32[]{:S(2)}, u32[]{:S(2)}) collective-permute-start(bf16[1,1024,128]{2,1,0:T(8,128)(2,1)S(1)} %dynamic-slice_convert_fusion.refs_0_), channel_id=1, source_target_pairs={{0,16},{8,24},{16,0},{24,8},{1,17},{9,25},{17,1},{25,9},{2,18},{10... | collective-permute-start | bytes 786440 | tf_op jit(solution)/shard_map/ppermute | solution.py:33

commit v4 on v3

--- a/solution.py
+++ b/solution.py
@@ -45,22 +45,31 @@
 def pick_below(sep_panels, sep_owner):
     inner = [n for n in tree(lax.axis_size("layer")) if n[3]]
     wide = max(max(n[3]) for n in inner) + 1
-    part = WS // lax.axis_size("layer")
-
-    def body(owner_ref, sep_ref, out_ref, held, sem):
-        start = pl.multiple_of(lax.axis_index("layer") * part, part)
-        copy = pltpu.make_async_copy(sep_ref.at[:wide, pl.ds(start, part)], held, sem)
-        copy.start()
-        copy.wait()
+    part = WS // 2
+
+    def body(owner_ref, sep_ref, out_ref, held, owner, sems):
+        start = pl.multiple_of(lax.rem(lax.axis_index("layer"), 2) * part, part)
+        copies = [
+            pltpu.make_async_copy(owner_ref, owner, sems.at[0]),
+            pltpu.make_async_copy(sep_ref.at[:wide, pl.ds(start, part)], held, sems.at[1]),
+        ]
+        for copy in copies:
+            copy.start()
+        for copy in copies:
+            copy.wait()
         for i, n in enumerate(inner):
-            mine = owner_ref[n[0]] == lax.axis_index("grid")
+            mine = owner[n[0]] == lax.axis_index("grid")
             out_ref[i] = jnp.where(mine, held[...], jnp.zeros(held.shape, held.dtype))
 
     return kernel_call(
         body,
         jax.ShapeDtypeStruct((len(inner), wide, part, WS), jnp.bfloat16),
-        [SMEM, HBM],
-        scratch=[pltpu.VMEM((wide, part, WS), jnp.bfloat16), pltpu.SemaphoreType.DMA],
+        [HBM, HBM],
+        scratch=[
+            pltpu.VMEM((wide, part, WS), jnp.bfloat16),
+            pltpu.SMEM(sep_owner.shape, jnp.int32),
+            pltpu.SemaphoreType.DMA((2,)),
+        ],
         nbytes=4 * wide * part * WS,
         limit=EARLY_LIMIT,
     )(sep_owner, sep_panels)
@@ -240,9 +249,9 @@
     def body(own_ref, other_ref, p_ref, sep_ref, *refs):
         below_refs = refs[: len(below)]
         out_ref, all_p, all_below = refs[len(below) :]
-        layer = lax.axis_index("layer")
+        core = lax.rem(lax.axis_index("layer"), 2)
         for k, ref in enumerate(below_refs):
-            at = pl.multiple_of((layer ^ k) * part, part)
+            at = pl.multiple_of((core ^ k) * part, part)
             for i in range(len(inner)):
                 for m in inner[i][3]:
                     all_below[i, m, pl.ds(at, part), :] = ref[i, m]
@@ -291,28 +300,25 @@
     beside = apart(u_panels, "grid", near)
     for hop in hops[:-1]:
         for k, piece in list(pieces.items()):
-            if k == far:
-                piece, below = together(piece, below)
             pieces[k ^ hop] = apart(piece, "grid", hop)
     blocks = [k * u_panels.shape[2] // BLOCK for k in pieces]
     order = list(dict.fromkeys(blocks))
     masked = mask_panels(l_panels, jnp.swapaxes(panel_fill, 2, 3), order)
-    beside, below = together(beside, below)
     below = below + apart(below, "grid", far)
     last = list(pieces)[-1]
     pieces[near] = beside
     for k in list(pieces)[1:-1]:
-        if k == far:
-            pieces[k], masked = together(pieces[k], masked)
+        if k == hops[1]:
+            pieces[k], beside = together(pieces[k], beside)
         if k == last:
-            pieces[k], below = together(pieces[k], below)
+            pieces[k], below, masked = together(pieces[k], below, masked)
         pieces[k ^ near] = apart(pieces[k], "grid", near)
     for hop in hops[1:-1]:
         below = below + apart(below, "grid", hop)
     last ^= near
     pieces[last], below = together(pieces[last], below)
 
-    half = len(order) // 2
+    half = len(order) - 1
     early = {k: piece for k, piece in pieces.items() if k * piece.shape[2] // BLOCK in order[:half]}
     late = {k: piece for k, piece in pieces.items() if k not in early}
     begun = first_part(masked, early, order)
@@ -321,8 +327,7 @@
     candidates = lax.all_to_all(candidates.reshape((layers * grids,) + shape[2:]), BOTH, 0, 0).reshape(shape)
 
     below = [below + apart(below, "grid", hops[-1])]
-    while len(below) < layers:
-        below += [apart(part, "layer", len(below)) for part in below]
+    below.append(apart(below[0], "layer", 1))
     other = apart(send, "layer", 1)
     pivots = None
     bit = 1
@@ -335,7 +340,7 @@
         keep = lax.dynamic_index_in_dim(total, side, 1, keepdims=False)
         send = lax.dynamic_index_in_dim(total, 1 - side, 1, keepdims=False).astype(jnp.bfloat16)
         if pivots is None:
-            pivots = lax.all_to_all(pick_pivots(candidates, sep_owner, grids, [send] + below), "grid", 0, 0)
+            pivots = lax.all_to_all(pick_pivots(candidates, sep_owner, grids, [send, below[0]]), "grid", 0, 0)
         other = apart(send, "layer", bit)
     return eliminate(keep[0], other[0], pivots, below, sep_panels)
 

time: 60.3 us -> 57 us (0.945)
  starting transfers between devices: 28.2 us -> 23.8 us
  local copies, waits for them, and re-layouts: 1.83 us -> 3.6 us
  waiting for transfers between devices: 17.7 us -> 16.3 us
  other arithmetic: 0.14 us -> 1.37 us
    ppermute x15 -> x13, waiting for transfers between devices: 15.2 us -> 10.2 us  [apart(): lax.ppermute(x, axis, [(i, i ^ distance) for i in range(lax.axis_size(axi...]
    ppermute x15 -> x13, starting transfers between devices: 21.3 us -> 17.5 us  [apart(): lax.ppermute(x, axis, [(i, i ^ distance) for i in range(lax.axis_size(axi...]
    all_to_all x1, waiting for transfers between devices: 2.43 us -> 6.05 us  [local(): lax.all_to_all(candidates.reshape((layers * grids,) + shape[2:]), BOTH, 0...]
    unnamed x14 -> x16, local copies, waits for them, and re-layouts: 0.72 us -> 2.49 us
    add x1, other arithmetic: 0.09 us -> 1.27 us  [local(): total = keep + other.astype(jnp.float32)]
    pallas_call x1, Pallas kernels: 3.17 us -> 2.46 us  [layer_copy(): kernel_call(body, (jax.ShapeDtypeStruct((layers // 2, rows, width), jnp.f...]
    pallas_call x1, Pallas kernels: 1.48 us -> 2.17 us  [first_part(): kernel_call(body, jax.ShapeDtypeStruct((rows, columns), jnp.float32), [VM...]
  transfers between devices with their start and end apart: 17 -> 15, of which waited for: 10 -> 9; matrix products, arithmetic and copies ran while one was open for 2% -> 4% of each run, Pallas kernels for 10% -> 11%
where the time goes in v4:
time: 57 us; the launch traced here: 56.6 us
  starting transfers between devices  23.8 us (42%)
  waiting for transfers between devices  16.3 us (29%)
  Pallas kernels  11.3 us (20%)
  local copies, waits for them, and re-layouts  3.6 us (6%)
  other arithmetic  1.37 us (2%)
    ppermute x13, starting transfers between devices, apart(): lax.ppermute(x, axis, [(i, i ^ distance) for i in range(lax.axis_size(axi...  17.5 us
    ppermute x13, waiting for transfers between devices, apart(): lax.ppermute(x, axis, [(i, i ^ distance) for i in range(lax.axis_size(axi...  10.2 us
    all_to_all x1, waiting for transfers between devices, local(): lax.all_to_all(candidates.reshape((layers * grids,) + shape[2:]), BOTH, 0...  6.05 us
    all_to_all x1, starting transfers between devices, local(): lax.all_to_all(pick_pivots(candidates, sep_owner, grids, [send, below[0]]...  3.39 us
    all_to_all x1, starting transfers between devices, local(): lax.all_to_all(candidates.reshape((layers * grids,) + shape[2:]), BOTH, 0...  2.91 us
    unnamed x16, local copies, waits for them, and re-layouts  2.49 us
    pallas_call x1, Pallas kernels, layer_copy(): kernel_call(body, (jax.ShapeDtypeStruct((layers // 2, rows, width), jnp.f...  2.46 us
    pallas_call x1, Pallas kernels, mask_panels(): kernel_call(body, jax.ShapeDtypeStruct((rows, panels * width), jnp.bfloat...  2.33 us
  transfers between devices with their start and end apart: 15, of which 9 were waited for; matrix products, arithmetic and copies ran while one was open for 4% of the time, Pallas kernels for 11%

profile of v4, /device:TPU:0, one launch (start us, length us, event | category | flops | bytes accessed | tf_op | source)
XLA Modules:
  0.0 56.6 jit_solution(13222797992667416704)
XLA Ops:
  0.0 5.0 %collective-permute-start = (bf16[1,2,64,512]{3,2,1,0:T(8,128)(2,1)}, bf16[1,2,64,512]{3,2,1,0:T(8,128)(2,1)S(1)}, u32[]{:S(2)}, u32[]{:S(2)}) collective-permute-start(bf16[1,2,64,512]{3,2,1,0:T(8,128)(2,1)} %refs_0_.1), channel_id=1, source_target_pairs={{0,6},{1,7},{2,4},{3,5},{4,2},{5,3},{6,0},{7,1},{8,14},{9,15},{10,... | collective-permute-start | bytes 393224 | tf_op jit(solution)/shard_map/ppermute | solution.py:33
  5.0 0.0 collective-permute-start.3
  5.1 1.5 %collective-permute-start.4 = (bf16[1,2,64,512]{3,2,1,0:T(8,128)(2,1)}, bf16[1,2,64,512]{3,2,1,0:T(8,128)(2,1)S(1)}, u32[]{:S(2)}, u32[]{:S(2)}) collective-permute-start(bf16[1,2,64,512]{3,2,1,0:T(8,128)(2,1)} %refs_0_.1), channel_id=1, source_target_pairs={{0,1},{1,0},{2,3},{3,2},{4,5},{5,4},{6,7},{7,6},{8,9},{9,8},{10,11... | collective-permute-start | bytes 393224 | tf_op jit(solution)/shard_map/ppermute | solution.py:33
  6.5 1.6 %shard_map.64 = bf16[1,2,128,256]{3,2,1,0:T(8,128)(2,1)} custom-call(s32[3]{0:T(128)} %owner_ref.3, bf16[3,1024,256]{2,1,0:T(8,128)(2,1)} %sep_ref.3), custom_call_target="tpu_custom_call" | custom-call | bytes 262144 | tf_op jit(solution)/shard_map/pallas_call | solution.py:64
  8.1 1.0 %collective-permute-start.2 = (bf16[1,2,128,256]{3,2,1,0:T(8,128)(2,1)}, bf16[1,2,128,256]{3,2,1,0:T(8,128)(2,1)S(1)}, u32[]{:S(2)}, u32[]{:S(2)}) collective-permute-start(bf16[1,2,128,256]{3,2,1,0:T(8,128)(2,1)} %shard_map.64), channel_id=1, source_target_pairs={{0,6},{1,7},{2,4},{3,5},{4,2},{5,3},{6,0},{7,1},{8,14},{9,15},{10,... | collective-permute-start | bytes 393224 | tf_op jit(solution)/shard_map/ppermute | solution.py:33
  9.1 0.5 collective-permute-done.refs_1_
  9.6 1.6 %collective-permute-start.1 = (bf16[1,2,64,512]{3,2,1,0:T(8,128)(2,1)S(1)}, bf16[1,2,64,512]{3,2,1,0:T(8,128)(2,1)S(1)}, u32[]{:S(2)}, u32[]{:S(2)}) collective-permute-start(bf16[1,2,64,512]{3,2,1,0:T(8,128)(2,1)S(1)} %collective-permute-done.refs_1_), channel_id=1, source_target_pairs={{0,2},{1,3},{2,0},{3,1},{4,6},{5,7},{6,4},{7,5},{8,10},{9,11},{10,... | collective-permute-start | bytes 393224 | tf_op jit(solution)/shard_map/ppermute | solution.py:33
  11.3 0.8 %collective-permute-done.3.refs_2_ = bf16[1,2,64,512]{3,2,1,0:T(8,128)(2,1)S(1)} collective-permute-done((bf16[1,2,64,512]{3,2,1,0:T(8,128)(2,1)}, bf16[1,2,64,512]{3,2,1,0:T(8,128)(2,1)S(1)}, u32[]{:S(2)}, u32[]{:S(2)}) %collective-permute-start.3) | collective-permute-done | bytes 131104 | tf_op jit(solution)/shard_map/ppermute | solution.py:33
  12.1 0.0 collective-permute-done.4.refs_3_
  12.1 3.4 %collective-permute-start.5 = (bf16[1,2,64,512]{3,2,1,0:T(8,128)(2,1)S(1)}, bf16[1,2,64,512]{3,2,1,0:T(8,128)(2,1)S(1)}, u32[]{:S(2)}, u32[]{:S(2)}) collective-permute-start(bf16[1,2,64,512]{3,2,1,0:T(8,128)(2,1)S(1)} %collective-permute-done.refs_1_), channel_id=1, source_target_pairs={{0,1},{1,0},{2,3},{3,2},{4,5},{5,4},{6,7},{7,6},{8,9},{9,8},{10,11... | collective-permute-start | bytes 393224 | tf_op jit(solution)/shard_map/ppermute | solution.py:33
  15.5 0.0 collective-permute-start.6
  15.6 0.7 %copy-done.2 = s32[1,2,8,4]{2,3,1,0:T(4,128)S(1)} copy-done((s32[1,2,8,4]{2,3,1,0:T(4,128)S(1)}, s32[1,2,8,4]{2,3,1,0:T(4,128)}, u32[]{:S(2)}) %copy-start.2) | copy-done | bytes 280
  16.2 2.3 %shard_map.65.l_ref = bf16[1024,1024]{1,0:T(8,128)(2,1)S(1)} custom-call(s32[1,2,4,8]{3,2,1,0:T(4,128)S(1)} %bitcast.9, bf16[1,2,1024,512]{3,2,1,0:T(8,128)(2,1)} %l_ref.1), custom_call_target="tpu_custom_call" | custom-call | bytes 4194304 | tf_op jit(solution)/shard_map/pallas_call | solution.py:102
  18.6 0.0 collective-permute-done.2
  18.6 0.0 copy-done.7
  18.6 0.0 copy-start.4
  18.7 0.0 collective-permute-done.1.refs_0_
  18.7 1.0 %collective-permute-start.8 = (bf16[1,2,128,256]{3,2,1,0:T(8,128)(2,1)S(1)}, bf16[1,2,128,256]{3,2,1,0:T(8,128)(2,1)S(1)}, u32[]{:S(2)}, u32[]{:S(2)}) collective-permute-start(bf16[1,2,128,256]{3,2,1,0:T(8,128)(2,1)S(1)} %add.25), channel_id=1, source_target_pairs={{0,2},{1,3},{2,0},{3,1},{4,6},{5,7},{6,4},{7,5},{8,10},{9,11},{10,... | collective-permute-start | bytes 393224 | tf_op jit(solution)/shard_map/ppermute | solution.py:33
  19.7 1.5 %collective-permute-start.7 = (bf16[1,2,64,512]{3,2,1,0:T(8,128)(2,1)S(1)}, bf16[1,2,64,512]{3,2,1,0:T(8,128)(2,1)S(1)}, u32[]{:S(2)}, u32[]{:S(2)}) collective-permute-start(bf16[1,2,64,512]{3,2,1,0:T(8,128)(2,1)S(1)} %collective-permute-done.1.refs_0_), channel_id=1, source_target_pairs={{0,1},{1,0},{2,3},{3,2},{4,5},{5,4},{6,7},{7,6},{8,9},{9,8},{10,11... | collective-permute-start | bytes 393224 | tf_op jit(solution)/shard_map/ppermute | solution.py:33
  21.2 0.0 collective-permute-done.5.refs_4_
  21.2 0.0 collective-permute-done.6.refs_5_
  21.2 0.0 copy-done.1
  21.2 2.2 %shard_map.66.begun_ref = f32[1024,512]{1,0:T(8,128)S(1)} custom-call(bf16[1024,1024]{1,0:T(8,128)(2,1)S(1)} %shard_map.65.l_ref, bf16[1,2,64,512]{3,2,1,0:T(8,128)(2,1)S(1)} %copy-done.1, bf16[1,2,64,512]{3,2,1,0:T(8,128)(2,1)S(1)} %collective-permute-done.refs_1_, bf16[1,2,64,512]{3,2,1,0:T(8,128)(2,1)S(1)} %collective-permute-done.3.refs_2_, ...), custom_call_target="tpu_custom_call" | custom-call | flops 805306368 | bytes 4456448 | tf_op jit(solution)/shard_map/pallas_call | solution.py:137
  23.4 0.3 collective-permute-done.8
  23.7 0.9 %collective-permute-done.7.refs_1_ = bf16[1,2,64,512]{3,2,1,0:T(8,128)(2,1)S(1)} collective-permute-done((bf16[1,2,64,512]{3,2,1,0:T(8,128)(2,1)S(1)}, bf16[1,2,64,512]{3,2,1,0:T(8,128)(2,1)S(1)}, u32[]{:S(2)}, u32[]{:S(2)}) %collective-permute-start.7) | collective-permute-done | bytes 131104 | tf_op jit(solution)/shard_map/ppermute | solution.py:33
  24.6 0.0 copy-done.4
  24.6 2.5 %shard_map.67 = (f32[2,1024,128]{2,1,0:T(8,128)S(1)}, bf16[2,1024,128]{2,1,0:T(8,128)(2,1)S(1)}, bf16[4,8,32,128]{3,2,1,0:T(8,128)(2,1)}) custom-call(s32[1,4,8]{2,1,0:T(4,128)S(1)} %bitcast.10, f32[1024,512]{1,0:T(8,128)S(1)} %shard_map.66.begun_ref, bf16[1024,1024]{1,0:T(8,128)(2,1)S(1)} %shard_map.65.l_ref, ...), custom_call_target="tpu_custom_call" | custom-call | flops 268435456 | bytes 4980736 | tf_op jit(solution)/shard_map/pallas_call | solution.py:188
  27.1 0.0 copy-start.3
  27.1 0.1 collective-permute-start.9
  27.2 1.6 %collective-permute-start.11 = (bf16[1,2,128,256]{3,2,1,0:T(8,128)(2,1)S(1)}, bf16[1,2,128,256]{3,2,1,0:T(8,128)(2,1)S(1)}, u32[]{:S(2)}, u32[]{:S(2)}) collective-permute-start(bf16[1,2,128,256]{3,2,1,0:T(8,128)(2,1)S(1)} %add.26), channel_id=1, source_target_pairs={{0,1},{1,0},{2,3},{3,2},{4,5},{5,4},{6,7},{7,6},{8,9},{9,8},{10,11... | collective-permute-start | bytes 393224 | tf_op jit(solution)/shard_map/ppermute | solution.py:33
  28.8 2.9 %all-to-all-start = ((bf16[32,32,128]{2,1,0:T(8,128)(2,1)}), bf16[32,32,128]{2,1,0:T(8,128)(2,1)S(1)}, u32[]{:S(2)}, u32[]{:S(2)}) async-start(bf16[32,32,128]{2,1,0:T(8,128)(2,1)} %bitcast.4), calls=%async_computation | async-start | bytes 524288 | tf_op jit(solution)/shard_map/all_to_all | solution.py:327
  31.7 1.4 %collective-permute-done.11 = bf16[1,2,128,256]{3,2,1,0:T(8,128)(2,1)S(1)} collective-permute-done((bf16[1,2,128,256]{3,2,1,0:T(8,128)(2,1)S(1)}, bf16[1,2,128,256]{3,2,1,0:T(8,128)(2,1)S(1)}, u32[]{:S(2)}, u32[]{:S(2)}) %collective-permute-start.11) | collective-permute-done | bytes 131104 | tf_op jit(solution)/shard_map/ppermute | solution.py:33
  33.2 0.0 collective-permute-done.9
  33.2 0.0 copy-start.6
  33.2 0.8 %copy-done.6 = bf16[2,1024,128]{2,1,0:T(8,128)(2,1)} copy-done((bf16[2,1024,128]{2,1,0:T(8,128)(2,1)}, bf16[2,1024,128]{2,1,0:T(8,128)(2,1)S(1)}, u32[]{:S(2)}) %copy-start.6) | copy-done | bytes 524312
  34.0 1.3 %convert_add_fusion = f32[2,1024,128]{2,1,0:T(8,128)S(1)} fusion(f32[2,1024,128]{2,1,0:T(8,128)S(1)} %get-tuple-element.19, bf16[2,1024,128]{2,1,0:T(8,128)(2,1)} %copy-done.6), kind=kLoop, calls=%fused_computation | loop fusion | flops 524288 | bytes 2621440 | tf_op jit(solution)/shard_map/add | solution.py:337
  35.2 0.0 copy-start.5
  35.2 1.0 %copy-done.5 = f32[2,1024,128]{2,1,0:T(8,128)} copy-done((f32[2,1024,128]{2,1,0:T(8,128)}, f32[2,1024,128]{2,1,0:T(8,128)S(1)}, u32[]{:S(2)}) %copy-start.5) | copy-done | bytes 1048600
  36.3 6.1 %all-to-all-done = bf16[32,32,128]{2,1,0:T(8,128)(2,1)S(1)} async-done(((bf16[32,32,128]{2,1,0:T(8,128)(2,1)}), bf16[32,32,128]{2,1,0:T(8,128)(2,1)S(1)}, u32[]{:S(2)}, u32[]{:S(2)}) %all-to-all-start) | async-done | bytes 262176 | tf_op jit(solution)/shard_map/all_to_all | solution.py:327
  42.3 1.2 %shard_map.68 = bf16[8,3,32,128]{3,2,1,0:T(8,128)(2,1)} custom-call(s32[3]{0:T(128)S(1)} %copy-done.3, bf16[4,8,32,128]{3,2,1,0:T(8,128)(2,1)S(1)} %bitcast.7, bf16[1,1024,128]{2,1,0:T(8,128)(2,1)S(1)} %dynamic-slice_convert_fusion.refs_0_, bf16[1,2,128,256]{3,2,1,0:T(8,128)(2,1)S(1)} %add.31.refs_1_.refs_0_), custom_call_target="tpu_custom_call" | custom-call | bytes 524288 | tf_op jit(solution)/shard_map/pallas_call | solution.py:233
  43.6 3.4 %all-to-all-start.1 = ((bf16[8,3,32,128]{3,2,1,0:T(8,128)(2,1)}), bf16[8,3,32,128]{3,2,1,0:T(8,128)(2,1)S(1)}, u32[]{:S(2)}, u32[]{:S(2)}) async-start(bf16[8,3,32,128]{3,2,1,0:T(8,128)(2,1)} %shard_map.68), calls=%async_computation.1 | async-start | bytes 393216 | tf_op jit(solution)/shard_map/all_to_all | solution.py:343
  47.0 0.6 %collective-permute-start.10 = (bf16[1,1024,128]{2,1,0:T(8,128)(2,1)S(1)}, bf16[1,1024,128]{2,1,0:T(8,128)(2,1)S(1)}, u32[]{:S(2)}, u32[]{:S(2)}) collective-permute-start(bf16[1,1024,128]{2,1,0:T(8,128)(2,1)S(1)} %dynamic-slice_convert_fusion.refs_0_), channel_id=1, source_target_pairs={{0,16},{8,24},{16,0},{24,8},{1,17},{9,25},{17,1},{25,9},{2,18},{10... | collective-permute-start | bytes 786440 | tf_op jit(solution)/shard_map/ppermute | solution.py:33
  47.6 0.1 collective-permute-start.12
  47.7 1.1 %dynamic-slice_bitcast_fusion.own_ref = f32[1024,128]{1,0:T(8,128)S(1)} fusion(f32[2,1024,128]{2,1,0:T(8,128)} %copy-done.5, s32[]{:T(128)S(6)} %select_n.20), kind=kLoop, calls=%fused_computation.2 | loop fusion | bytes 1048580 | tf_op jit(solution)/shard_map/squeeze | solution.py:345
  48.8 0.1 collective-permute-done.12.refs_1_
  48.9 6.1 %collective-permute-done.10 = bf16[1,1024,128]{2,1,0:T(8,128)(2,1)S(1)} collective-permute-done((bf16[1,1024,128]{2,1,0:T(8,128)(2,1)S(1)}, bf16[1,1024,128]{2,1,0:T(8,128)(2,1)S(1)}, u32[]{:S(2)}, u32[]{:S(2)}) %collective-permute-start.10) | collective-permute-done | bytes 262176 | tf_op jit(solution)/shard_map/ppermute | solution.py:33
  55.0 0.1 all-to-all-done.1.p_ref
  55.1 1.5 %shard_map.69 = f32[1024,128]{1,0:T(8,128)} custom-call(f32[1024,128]{1,0:T(8,128)S(1)} %dynamic-slice_bitcast_fusion.own_ref, bf16[1024,128]{1,0:T(8,128)(2,1)S(1)} %bitcast.8, bf16[8,3,32,128]{3,2,1,0:T(8,128)(2,1)S(1)} %all-to-all-done.1.p_ref, bf16[3,1024,256]{2,1,0:T(8,128)(2,1)S(1)} %copy-done, bf16[1,2,128,256]{3,2,1,0:T(8,128)(2,1)S(1)} %add.31.refs_1_.refs_0_, ...), custom_call_target="tpu_custom_call" | custom-call | flops 201326592 | bytes 2883584 | tf_op jit(solution)/shard_map/pallas_call | solution.py:279
  (10 shorter events, 0.1 us)
Async XLA Ops:
  0.0 9.6 %collective-permute-start = (bf16[1,2,64,512]{3,2,1,0:T(8,128)(2,1)}, bf16[1,2,64,512]{3,2,1,0:T(8,128)(2,1)S(1)}, u32[]{:S(2)}, u32[]{:S(2)}) collective-permute-start(bf16[1,2,64,512]{3,2,1,0:T(8,128)(2,1)} %refs_0_.1), channel_id=1, source_target_pairs={{0,6},{1,7},{2,4},{3,5},{4,2},{5,3},{6,0},{7,1},{8,14},{9,15},{10,... | collective-permute-start | bytes 393224 | tf_op jit(solution)/shard_map/ppermute | solution.py:33
  5.0 7.0 %collective-permute-start.3 = (bf16[1,2,64,512]{3,2,1,0:T(8,128)(2,1)}, bf16[1,2,64,512]{3,2,1,0:T(8,128)(2,1)S(1)}, u32[]{:S(2)}, u32[]{:S(2)}) collective-permute-start(bf16[1,2,64,512]{3,2,1,0:T(8,128)(2,1)} %refs_0_.1), channel_id=1, source_target_pairs={{0,2},{1,3},{2,0},{3,1},{4,6},{5,7},{6,4},{7,5},{8,10},{9,11},{10,... | collective-permute-start | bytes 393224 | tf_op jit(solution)/shard_map/ppermute | solution.py:33
  5.1 7.0 %collective-permute-start.4 = (bf16[1,2,64,512]{3,2,1,0:T(8,128)(2,1)}, bf16[1,2,64,512]{3,2,1,0:T(8,128)(2,1)S(1)}, u32[]{:S(2)}, u32[]{:S(2)}) collective-permute-start(bf16[1,2,64,512]{3,2,1,0:T(8,128)(2,1)} %refs_0_.1), channel_id=1, source_target_pairs={{0,1},{1,0},{2,3},{3,2},{4,5},{5,4},{6,7},{7,6},{8,9},{9,8},{10,11... | collective-permute-start | bytes 393224 | tf_op jit(solution)/shard_map/ppermute | solution.py:33
  8.1 10.4 %collective-permute-start.2 = (bf16[1,2,128,256]{3,2,1,0:T(8,128)(2,1)}, bf16[1,2,128,256]{3,2,1,0:T(8,128)(2,1)S(1)}, u32[]{:S(2)}, u32[]{:S(2)}) collective-permute-start(bf16[1,2,128,256]{3,2,1,0:T(8,128)(2,1)} %shard_map.64), channel_id=1, source_target_pairs={{0,6},{1,7},{2,4},{3,5},{4,2},{5,3},{6,0},{7,1},{8,14},{9,15},{10,... | collective-permute-start | bytes 393224 | tf_op jit(solution)/shard_map/ppermute | solution.py:33
  9.6 9.0 %collective-permute-start.1 = (bf16[1,2,64,512]{3,2,1,0:T(8,128)(2,1)S(1)}, bf16[1,2,64,512]{3,2,1,0:T(8,128)(2,1)S(1)}, u32[]{:S(2)}, u32[]{:S(2)}) collective-permute-start(bf16[1,2,64,512]{3,2,1,0:T(8,128)(2,1)S(1)} %collective-permute-done.refs_1_), channel_id=1, source_target_pairs={{0,2},{1,3},{2,0},{3,1},{4,6},{5,7},{6,4},{7,5},{8,10},{9,11},{10,... | collective-permute-start | bytes 393224 | tf_op jit(solution)/shard_map/ppermute | solution.py:33
  12.1 9.1 %collective-permute-start.5 = (bf16[1,2,64,512]{3,2,1,0:T(8,128)(2,1)S(1)}, bf16[1,2,64,512]{3,2,1,0:T(8,128)(2,1)S(1)}, u32[]{:S(2)}, u32[]{:S(2)}) collective-permute-start(bf16[1,2,64,512]{3,2,1,0:T(8,128)(2,1)S(1)} %collective-permute-done.refs_1_), channel_id=1, source_target_pairs={{0,1},{1,0},{2,3},{3,2},{4,5},{5,4},{6,7},{7,6},{8,9},{9,8},{10,11... | collective-permute-start | bytes 393224 | tf_op jit(solution)/shard_map/ppermute | solution.py:33
  15.5 5.7 %collective-permute-start.6 = (bf16[1,2,64,512]{3,2,1,0:T(8,128)(2,1)S(1)}, bf16[1,2,64,512]{3,2,1,0:T(8,128)(2,1)S(1)}, u32[]{:S(2)}, u32[]{:S(2)}) collective-permute-start(bf16[1,2,64,512]{3,2,1,0:T(8,128)(2,1)S(1)} %collective-permute-done.3.refs_2_), channel_id=1, source_target_pairs={{0,1},{1,0},{2,3},{3,2},{4,5},{5,4},{6,7},{7,6},{8,9},{9,8},{10,11... | collective-permute-start | bytes 393224 | tf_op jit(solution)/shard_map/ppermute | solution.py:33
  15.5 0.7 %copy-start.2 = (s32[1,2,8,4]{2,3,1,0:T(4,128)S(1)}, s32[1,2,8,4]{2,3,1,0:T(4,128)}, u32[]{:S(2)}) copy-start(s32[1,2,8,4]{2,3,1,0:T(4,128)} %param.8) | copy-start | bytes 772
  16.2 2.4 %copy-start.7 = (bf16[1,2,128,256]{3,2,1,0:T(8,128)(2,1)S(1)}, bf16[1,2,128,256]{3,2,1,0:T(8,128)(2,1)}, u32[]{:S(2)}) copy-start(bf16[1,2,128,256]{3,2,1,0:T(8,128)(2,1)} %shard_map.64) | copy-start | bytes 393220
  16.2 4.9 %copy-start.1 = (bf16[1,2,64,512]{3,2,1,0:T(8,128)(2,1)S(1)}, bf16[1,2,64,512]{3,2,1,0:T(8,128)(2,1)}, u32[]{:S(2)}) copy-start(bf16[1,2,64,512]{3,2,1,0:T(8,128)(2,1)} %refs_0_.1) | copy-start | bytes 393220
  18.6 6.0 %copy-start.4 = (s32[1,8,4]{1,2,0:T(4,128)S(1)}, s32[1,8,4]{1,2,0:T(4,128)}, u32[]{:S(2)}) copy-start(s32[1,8,4]{1,2,0:T(4,128)} %param.9) | copy-start | bytes 388
  18.7 5.0 %collective-permute-start.8 = (bf16[1,2,128,256]{3,2,1,0:T(8,128)(2,1)S(1)}, bf16[1,2,128,256]{3,2,1,0:T(8,128)(2,1)S(1)}, u32[]{:S(2)}, u32[]{:S(2)}) collective-permute-start(bf16[1,2,128,256]{3,2,1,0:T(8,128)(2,1)S(1)} %add.25), channel_id=1, source_target_pairs={{0,2},{1,3},{2,0},{3,1},{4,6},{5,7},{6,4},{7,5},{8,10},{9,11},{10,... | collective-permute-start | bytes 393224 | tf_op jit(solution)/shard_map/ppermute | solution.py:33
  19.7 5.0 %collective-permute-start.7 = (bf16[1,2,64,512]{3,2,1,0:T(8,128)(2,1)S(1)}, bf16[1,2,64,512]{3,2,1,0:T(8,128)(2,1)S(1)}, u32[]{:S(2)}, u32[]{:S(2)}) collective-permute-start(bf16[1,2,64,512]{3,2,1,0:T(8,128)(2,1)S(1)} %collective-permute-done.1.refs_0_), channel_id=1, source_target_pairs={{0,1},{1,0},{2,3},{3,2},{4,5},{5,4},{6,7},{7,6},{8,9},{9,8},{10,11... | collective-permute-start | bytes 393224 | tf_op jit(solution)/shard_map/ppermute | solution.py:33
  27.1 15.2 %copy-start.3 = (s32[3]{0:T(128)S(1)}, s32[3]{0:T(128)}, u32[]{:S(2)}) copy-start(s32[3]{0:T(128)} %owner_ref.3) | copy-start | bytes 40
  27.1 6.0 %collective-permute-start.9 = (bf16[2,1024,128]{2,1,0:T(8,128)(2,1)S(1)}, bf16[2,1024,128]{2,1,0:T(8,128)(2,1)S(1)}, u32[]{:S(2)}, u32[]{:S(2)}) collective-permute-start(bf16[2,1024,128]{2,1,0:T(8,128)(2,1)S(1)} %get-tuple-element.20), channel_id=1, source_target_pairs={{0,8},{8,0},{16,24},{24,16},{1,9},{9,1},{17,25},{25,17},{2,10},{10... | collective-permute-start | bytes 1572872 | tf_op jit(solution)/shard_map/ppermute | solution.py:33
  27.2 5.9 %collective-permute-start.11 = (bf16[1,2,128,256]{3,2,1,0:T(8,128)(2,1)S(1)}, bf16[1,2,128,256]{3,2,1,0:T(8,128)(2,1)S(1)}, u32[]{:S(2)}, u32[]{:S(2)}) collective-permute-start(bf16[1,2,128,256]{3,2,1,0:T(8,128)(2,1)S(1)} %add.26), channel_id=1, source_target_pairs={{0,1},{1,0},{2,3},{3,2},{4,5},{5,4},{6,7},{7,6},{8,9},{9,8},{10,11... | collective-permute-start | bytes 393224 | tf_op jit(solution)/shard_map/ppermute | solution.py:33
  28.8 13.6 %all-to-all-start = ((bf16[32,32,128]{2,1,0:T(8,128)(2,1)}), bf16[32,32,128]{2,1,0:T(8,128)(2,1)S(1)}, u32[]{:S(2)}, u32[]{:S(2)}) async-start(bf16[32,32,128]{2,1,0:T(8,128)(2,1)} %bitcast.4), calls=%async_computation | async-start | bytes 524288 | tf_op jit(solution)/shard_map/all_to_all | solution.py:327
  33.2 0.8 %copy-start.6 = (bf16[2,1024,128]{2,1,0:T(8,128)(2,1)}, bf16[2,1024,128]{2,1,0:T(8,128)(2,1)S(1)}, u32[]{:S(2)}) copy-start(bf16[2,1024,128]{2,1,0:T(8,128)(2,1)S(1)} %collective-permute-done.9) | copy-start | bytes 1572868
  34.0 21.1 %copy-start = (bf16[3,1024,256]{2,1,0:T(8,128)(2,1)S(1)}, bf16[3,1024,256]{2,1,0:T(8,128)(2,1)}, u32[]{:S(2)}) copy-start(bf16[3,1024,256]{2,1,0:T(8,128)(2,1)} %sep_ref.3) | copy-start | bytes 4718596
  35.2 1.0 %copy-start.5 = (f32[2,1024,128]{2,1,0:T(8,128)}, f32[2,1024,128]{2,1,0:T(8,128)S(1)}, u32[]{:S(2)}) copy-start(f32[2,1024,128]{2,1,0:T(8,128)S(1)} %convert_add_fusion) | copy-start | bytes 3145732
  43.6 11.5 %all-to-all-start.1 = ((bf16[8,3,32,128]{3,2,1,0:T(8,128)(2,1)}), bf16[8,3,32,128]{3,2,1,0:T(8,128)(2,1)S(1)}, u32[]{:S(2)}, u32[]{:S(2)}) async-start(bf16[8,3,32,128]{3,2,1,0:T(8,128)(2,1)} %shard_map.68), calls=%async_computation.1 | async-start | bytes 393216 | tf_op jit(solution)/shard_map/all_to_all | solution.py:343
  47.0 8.0 %collective-permute-start.10 = (bf16[1,1024,128]{2,1,0:T(8,128)(2,1)S(1)}, bf16[1,1024,128]{2,1,0:T(8,128)(2,1)S(1)}, u32[]{:S(2)}, u32[]{:S(2)}) collective-permute-start(bf16[1,1024,128]{2,1,0:T(8,128)(2,1)S(1)} %dynamic-slice_convert_fusion.refs_0_), channel_id=1, source_target_pairs={{0,16},{8,24},{16,0},{24,8},{1,17},{9,25},{17,1},{25,9},{2,18},{10... | collective-permute-start | bytes 786440 | tf_op jit(solution)/shard_map/ppermute | solution.py:33
  47.6 1.3 %collective-permute-start.12 = (bf16[1,2,128,256]{3,2,1,0:T(8,128)(2,1)S(1)}, bf16[1,2,128,256]{3,2,1,0:T(8,128)(2,1)S(1)}, u32[]{:S(2)}, u32[]{:S(2)}) collective-permute-start(bf16[1,2,128,256]{3,2,1,0:T(8,128)(2,1)S(1)} %add.31.refs_1_.refs_0_), channel_id=1, source_target_pairs={{0,8},{8,0},{16,24},{24,16},{1,9},{9,1},{17,25},{25,17},{2,10},{10... | collective-permute-start | bytes 393224 | tf_op jit(solution)/shard_map/ppermute | solution.py:33

commit v5 on v4

--- a/solution.py
+++ b/solution.py
@@ -16,13 +16,13 @@
 SMEM = pl.BlockSpec(memory_space=pltpu.SMEM)
 
 
-def kernel_call(body, out_shape, in_specs, scratch=(), flops=0, nbytes=0, limit=VMEM_LIMIT):
+def kernel_call(body, out_shape, in_specs, scratch=(), flops=0, nbytes=0, limit=VMEM_LIMIT, out_specs=None):
     many = isinstance(out_shape, (tuple, list))
     return pl.pallas_call(
         body,
         out_shape=out_shape,
         in_specs=in_specs,
-        out_specs=[VMEM] * len(out_shape) if many else VMEM,
+        out_specs=out_specs or ([VMEM] * len(out_shape) if many else VMEM),
         scratch_shapes=list(scratch),
         compiler_params=pltpu.CompilerParams(vmem_limit_bytes=limit),
         cost_estimate=pl.CostEstimate(flops=flops, bytes_accessed=nbytes, transcendentals=0),
@@ -80,14 +80,17 @@
     share = width // lax.axis_size("grid")
     step = min(rows, 256)
 
-    def body(fill_ref, l_ref, out_ref, l_all, sems):
+    def body(panel_ref, l_ref, out_ref, l_all, fill_ref, sems, sem):
         first = lax.axis_index("grid") * share // BLOCK
         copies = [
             pltpu.make_async_copy(l_ref.at[0, :, r : r + step], l_all.at[:, r : r + step], sems.at[r // step])
             for r in range(0, rows, step)
         ]
+        fill_copy = pltpu.make_async_copy(panel_ref, fill_ref, sem)
+        fill_copy.start()
         for copy in copies:
             copy.start()
+        fill_copy.wait()
         for r in range(0, rows, step):
             copies[r // step].wait()
             for i, block in enumerate(order):
@@ -102,10 +105,15 @@
     return kernel_call(
         body,
         jax.ShapeDtypeStruct((rows, panels * width), jnp.bfloat16),
-        [SMEM, HBM],
-        scratch=[pltpu.VMEM((panels, rows, width), jnp.bfloat16), pltpu.SemaphoreType.DMA((rows // step,))],
+        [HBM, HBM],
+        scratch=[
+            pltpu.VMEM((panels, rows, width), jnp.bfloat16),
+            pltpu.SMEM(panel_fill.shape, jnp.int32),
+            pltpu.SemaphoreType.DMA((rows // step,)),
+            pltpu.SemaphoreType.DMA,
+        ],
         nbytes=4 * panels * rows * width,
-    )(panel_fill, pltpu.with_memory_space_constraint(l_panels, pltpu.HBM))
+    )(*(pltpu.with_memory_space_constraint(x, pltpu.HBM) for x in (panel_fill, l_panels)))
 
 
 def load_panels(u_refs, pieces, order, u_all, sems, me):
@@ -155,22 +163,28 @@
     done = masked.shape[1] - depth
 
     def body(fill_ref, begun_ref, l_ref, *refs):
-        u_refs, (keep_ref, send_ref, pivot_ref, u_all, sums, sems) = refs[: len(pieces)], refs[len(pieces) :]
+        u_refs = refs[: len(pieces)]
+        keep_ref, send_ref, pivot_ref, u_all, sums, fills, pivots, sems, sem = refs[len(pieces) :]
         core = lax.rem(lax.axis_index("layer"), 2)
-        for copy in load_panels(u_refs, list(pieces), order[-(depth // panels // BLOCK) :], u_all, sems, lax.axis_index("grid")):
+        copies = load_panels(
+            u_refs, list(pieces), order[-(depth // panels // BLOCK) :], u_all, sems, lax.axis_index("grid")
+        )
+        for b in range(rows // BLOCK):
+            for c in range(columns // BLOCK):
+                fill = -fill_ref[0, c, b].astype(jnp.float32)
+                fills[b : b + 1, c * BLOCK : (c + 1) * BLOCK] = jnp.full((1, BLOCK), fill, jnp.float32)
+        for copy in copies:
             copy.wait()
 
         def filled(slot, j, row, count):
-            start = pl.multiple_of(j * width, width)
-            lines = []
-            for b in range(row, row + count, BLOCK):
-                tiles = []
-                for c in range(0, width, BLOCK):
-                    fill = fill_ref[0, j * (width // BLOCK) + c // BLOCK, b // BLOCK].astype(jnp.float32)
-                    tiles.append(sums[slot, b - row : b - row + BLOCK, pl.ds(start + c, BLOCK)] * -fill)
-                lines.append(tiles[0] if len(tiles) == 1 else jnp.concatenate(tiles, 1))
+            at = pl.ds(pl.multiple_of(j * width, width), width)
+            lines = [
+                sums[slot, b - row : b - row + BLOCK, at] * fills[b // BLOCK : b // BLOCK + 1, at]
+                for b in range(row, row + count, BLOCK)
+            ]
             return lines[0] if len(lines) == 1 else jnp.concatenate(lines, 0)
 
+        out = pltpu.make_async_copy(pivots, pivot_ref, sem)
         for r in range(0, rows, step):
             here, slot = slice(r, r + step), r // step % 2
             sums[slot] = begun_ref[here, :] + jnp.dot(
@@ -180,10 +194,13 @@
                 for j in range(layers):
                     low = filled(slot, j, r, step).astype(jnp.bfloat16)
                     for g in range(step // piece_rows):
-                        pivot_ref[j, r // piece_rows + g] = low[g * piece_rows : (g + 1) * piece_rows]
+                        pivots[j, r // piece_rows + g] = low[g * piece_rows : (g + 1) * piece_rows]
+            if r + step == WS:
+                out.start()
             for i in range(layers // 2):
                 keep_ref[i, here, :] = filled(slot, 2 * i + core, r, step)
                 send_ref[i, here, :] = filled(slot, 2 * i + 1 - core, r, step).astype(jnp.bfloat16)
+        out.wait()
 
     return kernel_call(
         body,
@@ -193,10 +210,14 @@
             jax.ShapeDtypeStruct((layers, grids, piece_rows, width), jnp.bfloat16),
         ),
         [SMEM, VMEM, VMEM] + [HBM] * len(pieces),
+        out_specs=[VMEM, VMEM, HBM],
         scratch=[
             pltpu.VMEM((depth, columns), jnp.bfloat16),
             pltpu.VMEM((2, step, columns), jnp.float32),
+            pltpu.VMEM((rows // BLOCK, columns), jnp.float32),
+            pltpu.VMEM((layers, grids, piece_rows, width), jnp.bfloat16),
             pltpu.SemaphoreType.DMA((len(pieces), panels)),
+            pltpu.SemaphoreType.DMA,
         ],
         flops=2 * rows * depth * columns,
         nbytes=2 * rows * depth + 2 * depth * columns + 8 * rows * columns,
@@ -248,7 +269,7 @@
 
     def body(own_ref, other_ref, p_ref, sep_ref, *refs):
         below_refs = refs[: len(below)]
-        out_ref, all_p, all_below = refs[len(below) :]
+        out_ref, all_p, all_below, result, sems = refs[len(below) :]
         core = lax.rem(lax.axis_index("layer"), 2)
         for k, ref in enumerate(below_refs):
             at = pl.multiple_of((core ^ k) * part, part)
@@ -267,6 +288,7 @@
                         all_below[which, m], all_p[m * WS : (m + 1) * WS, :], preferred_element_type=jnp.float32
                     )
                 all_p[at : at + WS, :] = pivot.astype(jnp.bfloat16)
+        copies = []
         for r in range(0, rows, step):
             here = slice(r, r + step)
             total = own_ref[here, :] + other_ref[here, :].astype(jnp.float32)
@@ -274,7 +296,11 @@
                 total = total - jnp.dot(
                     sep_ref[node, here, :], all_p[node * WS : (node + 1) * WS, :], preferred_element_type=jnp.float32
                 )
-            out_ref[here, :] = total
+            result[here, :] = total
+            copies.append(pltpu.make_async_copy(result.at[here], out_ref.at[here], sems.at[r // step]))
+            copies[-1].start()
+        for copy in copies:
+            copy.wait()
 
     return kernel_call(
         body,
@@ -283,7 +309,10 @@
         scratch=[
             pltpu.VMEM((count * WS, width), jnp.bfloat16),
             pltpu.VMEM((len(inner), wide, WS, WS), jnp.bfloat16),
+            pltpu.VMEM((rows, width), jnp.float32),
+            pltpu.SemaphoreType.DMA((rows // step,)),
         ],
+        out_specs=HBM,
         flops=2 * rows * count * WS * width,
         nbytes=10 * rows * width + 2 * sep_panels.size,
     )(own, other, pivots, sep_panels, *below)

time: 57 us -> 55.5 us (0.974)
  Pallas kernels: 11.3 us -> 10.2 us
  local copies, waits for them, and re-layouts: 3.6 us -> 2.9 us
    unnamed x16 -> x14, local copies, waits for them, and re-layouts: 2.49 us -> 1.79 us
  transfers between devices with their start and end apart: 15 -> 15, of which waited for: 9 -> 9; matrix products, arithmetic and copies ran while one was open for 4% -> 4% of each run, Pallas kernels for 11% -> 10%
where the time goes in v5:
time: 55.5 us; the launch traced here: 55.1 us
  starting transfers between devices  24 us (43%)
  waiting for transfers between devices  16.3 us (29%)
  Pallas kernels  10.2 us (18%)
  local copies, waits for them, and re-layouts  2.9 us (5%)
  other arithmetic  1.38 us (2%)
    ppermute x13, starting transfers between devices, apart(): lax.ppermute(x, axis, [(i, i ^ distance) for i in range(lax.axis_size(axi...  18 us
    ppermute x13, waiting for transfers between devices, apart(): lax.ppermute(x, axis, [(i, i ^ distance) for i in range(lax.axis_size(axi...  10.5 us
    all_to_all x1, waiting for transfers between devices, local(): lax.all_to_all(candidates.reshape((layers * grids,) + shape[2:]), BOTH, 0...  5.74 us
    all_to_all x1, starting transfers between devices, local(): lax.all_to_all(pick_pivots(candidates, sep_owner, grids, [send, below[0]]...  3.39 us
    all_to_all x1, starting transfers between devices, local(): lax.all_to_all(candidates.reshape((layers * grids,) + shape[2:]), BOTH, 0...  2.58 us
    pallas_call x1, Pallas kernels, first_part(): kernel_call(body, jax.ShapeDtypeStruct((rows, columns), jnp.float32), [VM...  2.13 us
    pallas_call x1, Pallas kernels, layer_copy(): kernel_call(body, (jax.ShapeDtypeStruct((layers // 2, rows, width), jnp.f...  2.08 us
    unnamed x14, local copies, waits for them, and re-layouts  1.79 us
  transfers between devices with their start and end apart: 15, of which 9 were waited for; matrix products, arithmetic and copies ran while one was open for 4% of the time, Pallas kernels for 10%

profile of v5, /device:TPU:0, one launch (start us, length us, event | category | flops | bytes accessed | tf_op | source)
XLA Modules:
  0.0 55.1 jit_solution(8939772030647099821)
XLA Ops:
  0.0 5.0 %collective-permute-start = (bf16[1,2,64,512]{3,2,1,0:T(8,128)(2,1)}, bf16[1,2,64,512]{3,2,1,0:T(8,128)(2,1)S(1)}, u32[]{:S(2)}, u32[]{:S(2)}) collective-permute-start(bf16[1,2,64,512]{3,2,1,0:T(8,128)(2,1)} %refs_0_.1), channel_id=1, source_target_pairs={{0,6},{1,7},{2,4},{3,5},{4,2},{5,3},{6,0},{7,1},{8,14},{9,15},{10,... | collective-permute-start | bytes 393224 | tf_op jit(solution)/shard_map/ppermute | solution.py:33
  5.0 0.0 collective-permute-start.3
  5.1 1.5 %collective-permute-start.4 = (bf16[1,2,64,512]{3,2,1,0:T(8,128)(2,1)}, bf16[1,2,64,512]{3,2,1,0:T(8,128)(2,1)S(1)}, u32[]{:S(2)}, u32[]{:S(2)}) collective-permute-start(bf16[1,2,64,512]{3,2,1,0:T(8,128)(2,1)} %refs_0_.1), channel_id=1, source_target_pairs={{0,1},{1,0},{2,3},{3,2},{4,5},{5,4},{6,7},{7,6},{8,9},{9,8},{10,11... | collective-permute-start | bytes 393224 | tf_op jit(solution)/shard_map/ppermute | solution.py:33
  6.5 1.6 %shard_map.64 = bf16[1,2,128,256]{3,2,1,0:T(8,128)(2,1)} custom-call(s32[3]{0:T(128)} %owner_ref.3, bf16[3,1024,256]{2,1,0:T(8,128)(2,1)} %sep_ref.3), custom_call_target="tpu_custom_call" | custom-call | bytes 262144 | tf_op jit(solution)/shard_map/pallas_call | solution.py:64
  8.1 1.0 %collective-permute-start.2 = (bf16[1,2,128,256]{3,2,1,0:T(8,128)(2,1)}, bf16[1,2,128,256]{3,2,1,0:T(8,128)(2,1)S(1)}, u32[]{:S(2)}, u32[]{:S(2)}) collective-permute-start(bf16[1,2,128,256]{3,2,1,0:T(8,128)(2,1)} %shard_map.64), channel_id=1, source_target_pairs={{0,6},{1,7},{2,4},{3,5},{4,2},{5,3},{6,0},{7,1},{8,14},{9,15},{10,... | collective-permute-start | bytes 393224 | tf_op jit(solution)/shard_map/ppermute | solution.py:33
  9.1 0.5 collective-permute-done.refs_1_
  9.6 1.6 %collective-permute-start.1 = (bf16[1,2,64,512]{3,2,1,0:T(8,128)(2,1)S(1)}, bf16[1,2,64,512]{3,2,1,0:T(8,128)(2,1)S(1)}, u32[]{:S(2)}, u32[]{:S(2)}) collective-permute-start(bf16[1,2,64,512]{3,2,1,0:T(8,128)(2,1)S(1)} %collective-permute-done.refs_1_), channel_id=1, source_target_pairs={{0,2},{1,3},{2,0},{3,1},{4,6},{5,7},{6,4},{7,5},{8,10},{9,11},{10,... | collective-permute-start | bytes 393224 | tf_op jit(solution)/shard_map/ppermute | solution.py:33
  11.3 0.8 %collective-permute-done.3.refs_2_ = bf16[1,2,64,512]{3,2,1,0:T(8,128)(2,1)S(1)} collective-permute-done((bf16[1,2,64,512]{3,2,1,0:T(8,128)(2,1)}, bf16[1,2,64,512]{3,2,1,0:T(8,128)(2,1)S(1)}, u32[]{:S(2)}, u32[]{:S(2)}) %collective-permute-start.3) | collective-permute-done | bytes 131104 | tf_op jit(solution)/shard_map/ppermute | solution.py:33
  12.1 0.0 collective-permute-done.4.refs_3_
  12.1 3.4 %collective-permute-start.5 = (bf16[1,2,64,512]{3,2,1,0:T(8,128)(2,1)S(1)}, bf16[1,2,64,512]{3,2,1,0:T(8,128)(2,1)S(1)}, u32[]{:S(2)}, u32[]{:S(2)}) collective-permute-start(bf16[1,2,64,512]{3,2,1,0:T(8,128)(2,1)S(1)} %collective-permute-done.refs_1_), channel_id=1, source_target_pairs={{0,1},{1,0},{2,3},{3,2},{4,5},{5,4},{6,7},{7,6},{8,9},{9,8},{10,11... | collective-permute-start | bytes 393224 | tf_op jit(solution)/shard_map/ppermute | solution.py:33
  15.5 0.0 collective-permute-start.6
  15.6 1.8 %shard_map.65.l_ref = bf16[1024,1024]{1,0:T(8,128)(2,1)S(1)} custom-call(s32[1,2,4,8]{3,2,1,0:T(4,128)} %bitcast.10, bf16[1,2,1024,512]{3,2,1,0:T(8,128)(2,1)} %l_ref.1), custom_call_target="tpu_custom_call" | custom-call | bytes 4194304 | tf_op jit(solution)/shard_map/pallas_call | solution.py:105
  17.3 0.0 collective-permute-done.2
  17.4 0.0 copy-done.6
  17.4 0.0 copy-start.3
  17.4 0.0 collective-permute-done.1.refs_0_
  17.4 1.5 %collective-permute-start.8 = (bf16[1,2,128,256]{3,2,1,0:T(8,128)(2,1)S(1)}, bf16[1,2,128,256]{3,2,1,0:T(8,128)(2,1)S(1)}, u32[]{:S(2)}, u32[]{:S(2)}) collective-permute-start(bf16[1,2,128,256]{3,2,1,0:T(8,128)(2,1)S(1)} %add.25), channel_id=1, source_target_pairs={{0,2},{1,3},{2,0},{3,1},{4,6},{5,7},{6,4},{7,5},{8,10},{9,11},{10,... | collective-permute-start | bytes 393224 | tf_op jit(solution)/shard_map/ppermute | solution.py:33
  19.0 1.5 %collective-permute-start.7 = (bf16[1,2,64,512]{3,2,1,0:T(8,128)(2,1)S(1)}, bf16[1,2,64,512]{3,2,1,0:T(8,128)(2,1)S(1)}, u32[]{:S(2)}, u32[]{:S(2)}) collective-permute-start(bf16[1,2,64,512]{3,2,1,0:T(8,128)(2,1)S(1)} %collective-permute-done.1.refs_0_), channel_id=1, source_target_pairs={{0,1},{1,0},{2,3},{3,2},{4,5},{5,4},{6,7},{7,6},{8,9},{9,8},{10,11... | collective-permute-start | bytes 393224 | tf_op jit(solution)/shard_map/ppermute | solution.py:33
  20.5 0.0 collective-permute-done.5.refs_4_
  20.5 0.2 collective-permute-done.6.refs_5_
  20.6 0.0 copy-done.1
  20.7 2.1 %shard_map.66.begun_ref = f32[1024,512]{1,0:T(8,128)S(1)} custom-call(bf16[1024,1024]{1,0:T(8,128)(2,1)S(1)} %shard_map.65.l_ref, bf16[1,2,64,512]{3,2,1,0:T(8,128)(2,1)S(1)} %copy-done.1, bf16[1,2,64,512]{3,2,1,0:T(8,128)(2,1)S(1)} %collective-permute-done.refs_1_, bf16[1,2,64,512]{3,2,1,0:T(8,128)(2,1)S(1)} %collective-permute-done.3.refs_2_, ...), custom_call_target="tpu_custom_call" | custom-call | flops 805306368 | bytes 4456448 | tf_op jit(solution)/shard_map/pallas_call | solution.py:145
  22.8 0.0 collective-permute-done.8
  22.8 1.1 %collective-permute-done.7.refs_1_ = bf16[1,2,64,512]{3,2,1,0:T(8,128)(2,1)S(1)} collective-permute-done((bf16[1,2,64,512]{3,2,1,0:T(8,128)(2,1)S(1)}, bf16[1,2,64,512]{3,2,1,0:T(8,128)(2,1)S(1)}, u32[]{:S(2)}, u32[]{:S(2)}) %collective-permute-start.7) | collective-permute-done | bytes 131104 | tf_op jit(solution)/shard_map/ppermute | solution.py:33
  23.9 0.0 copy-done.3
  23.9 2.1 %shard_map.67 = (f32[2,1024,128]{2,1,0:T(8,128)S(1)}, bf16[2,1024,128]{2,1,0:T(8,128)(2,1)S(1)}, bf16[4,8,32,128]{3,2,1,0:T(8,128)(2,1)}) custom-call(s32[1,4,8]{2,1,0:T(4,128)S(1)} %bitcast.9, f32[1024,512]{1,0:T(8,128)S(1)} %shard_map.66.begun_ref, bf16[1024,1024]{1,0:T(8,128)(2,1)S(1)} %shard_map.65.l_ref, ...), custom_call_target="tpu_custom_call" | custom-call | flops 268435456 | bytes 4980736 | tf_op jit(solution)/shard_map/pallas_call | solution.py:205
  26.0 0.0 copy-start.2
  26.0 0.1 collective-permute-start.9
  26.1 1.6 %collective-permute-start.11 = (bf16[1,2,128,256]{3,2,1,0:T(8,128)(2,1)S(1)}, bf16[1,2,128,256]{3,2,1,0:T(8,128)(2,1)S(1)}, u32[]{:S(2)}, u32[]{:S(2)}) collective-permute-start(bf16[1,2,128,256]{3,2,1,0:T(8,128)(2,1)S(1)} %add.26), channel_id=1, source_target_pairs={{0,1},{1,0},{2,3},{3,2},{4,5},{5,4},{6,7},{7,6},{8,9},{9,8},{10,11... | collective-permute-start | bytes 393224 | tf_op jit(solution)/shard_map/ppermute | solution.py:33
  27.7 2.6 %all-to-all-start = ((bf16[32,32,128]{2,1,0:T(8,128)(2,1)}), bf16[32,32,128]{2,1,0:T(8,128)(2,1)S(1)}, u32[]{:S(2)}, u32[]{:S(2)}) async-start(bf16[32,32,128]{2,1,0:T(8,128)(2,1)} %bitcast.4), calls=%async_computation | async-start | bytes 524288 | tf_op jit(solution)/shard_map/all_to_all | solution.py:356
  30.3 1.7 %collective-permute-done.11 = bf16[1,2,128,256]{3,2,1,0:T(8,128)(2,1)S(1)} collective-permute-done((bf16[1,2,128,256]{3,2,1,0:T(8,128)(2,1)S(1)}, bf16[1,2,128,256]{3,2,1,0:T(8,128)(2,1)S(1)}, u32[]{:S(2)}, u32[]{:S(2)}) %collective-permute-start.11) | collective-permute-done | bytes 131104 | tf_op jit(solution)/shard_map/ppermute | solution.py:33
  32.1 0.0 collective-permute-done.9
  32.1 0.0 copy-start.5
  32.1 0.8 %copy-done.5 = bf16[2,1024,128]{2,1,0:T(8,128)(2,1)} copy-done((bf16[2,1024,128]{2,1,0:T(8,128)(2,1)}, bf16[2,1024,128]{2,1,0:T(8,128)(2,1)S(1)}, u32[]{:S(2)}) %copy-start.5) | copy-done | bytes 524312
  32.9 1.3 %convert_add_fusion = f32[2,1024,128]{2,1,0:T(8,128)S(1)} fusion(f32[2,1024,128]{2,1,0:T(8,128)S(1)} %get-tuple-element.19, bf16[2,1024,128]{2,1,0:T(8,128)(2,1)} %copy-done.5), kind=kLoop, calls=%fused_computation | loop fusion | flops 524288 | bytes 2621440 | tf_op jit(solution)/shard_map/add | solution.py:366
  34.2 0.0 copy-start.4
  34.2 1.0 %copy-done.4 = f32[2,1024,128]{2,1,0:T(8,128)} copy-done((f32[2,1024,128]{2,1,0:T(8,128)}, f32[2,1024,128]{2,1,0:T(8,128)S(1)}, u32[]{:S(2)}) %copy-start.4) | copy-done | bytes 1048600
  35.2 5.7 %all-to-all-done = bf16[32,32,128]{2,1,0:T(8,128)(2,1)S(1)} async-done(((bf16[32,32,128]{2,1,0:T(8,128)(2,1)}), bf16[32,32,128]{2,1,0:T(8,128)(2,1)S(1)}, u32[]{:S(2)}, u32[]{:S(2)}) %all-to-all-start) | async-done | bytes 262176 | tf_op jit(solution)/shard_map/all_to_all | solution.py:356
  40.9 0.0 copy-done.2
  40.9 1.2 %shard_map.68 = bf16[8,3,32,128]{3,2,1,0:T(8,128)(2,1)} custom-call(s32[3]{0:T(128)S(1)} %copy-done.2, bf16[4,8,32,128]{3,2,1,0:T(8,128)(2,1)S(1)} %bitcast.7, bf16[1,1024,128]{2,1,0:T(8,128)(2,1)S(1)} %dynamic-slice_convert_fusion.refs_0_, bf16[1,2,128,256]{3,2,1,0:T(8,128)(2,1)S(1)} %add.31.refs_1_.refs_0_), custom_call_target="tpu_custom_call" | custom-call | bytes 524288 | tf_op jit(solution)/shard_map/pallas_call | solution.py:254
  42.2 3.4 %all-to-all-start.1 = ((bf16[8,3,32,128]{3,2,1,0:T(8,128)(2,1)}), bf16[8,3,32,128]{3,2,1,0:T(8,128)(2,1)S(1)}, u32[]{:S(2)}, u32[]{:S(2)}) async-start(bf16[8,3,32,128]{3,2,1,0:T(8,128)(2,1)} %shard_map.68), calls=%async_computation.1 | async-start | bytes 393216 | tf_op jit(solution)/shard_map/all_to_all | solution.py:372
  45.6 0.6 %collective-permute-start.10 = (bf16[1,1024,128]{2,1,0:T(8,128)(2,1)S(1)}, bf16[1,1024,128]{2,1,0:T(8,128)(2,1)S(1)}, u32[]{:S(2)}, u32[]{:S(2)}) collective-permute-start(bf16[1,1024,128]{2,1,0:T(8,128)(2,1)S(1)} %dynamic-slice_convert_fusion.refs_0_), channel_id=1, source_target_pairs={{0,16},{8,24},{16,0},{24,8},{1,17},{9,25},{17,1},{25,9},{2,18},{10... | collective-permute-start | bytes 786440 | tf_op jit(solution)/shard_map/ppermute | solution.py:33
  46.2 0.2 collective-permute-start.12
  46.3 1.1 %dynamic-slice_bitcast_fusion.own_ref = f32[1024,128]{1,0:T(8,128)S(1)} fusion(f32[2,1024,128]{2,1,0:T(8,128)} %copy-done.4, s32[]{:T(128)S(6)} %select_n.20), kind=kLoop, calls=%fused_computation.2 | loop fusion | bytes 1048580 | tf_op jit(solution)/shard_map/squeeze | solution.py:374
  47.4 0.1 collective-permute-done.12.refs_1_
  47.5 6.1 %collective-permute-done.10 = bf16[1,1024,128]{2,1,0:T(8,128)(2,1)S(1)} collective-permute-done((bf16[1,1024,128]{2,1,0:T(8,128)(2,1)S(1)}, bf16[1,1024,128]{2,1,0:T(8,128)(2,1)S(1)}, u32[]{:S(2)}, u32[]{:S(2)}) %collective-permute-start.10) | collective-permute-done | bytes 262176 | tf_op jit(solution)/shard_map/ppermute | solution.py:33
  53.6 0.1 all-to-all-done.1.p_ref
  53.6 1.4 %shard_map.69 = f32[1024,128]{1,0:T(8,128)} custom-call(f32[1024,128]{1,0:T(8,128)S(1)} %dynamic-slice_bitcast_fusion.own_ref, bf16[1024,128]{1,0:T(8,128)(2,1)S(1)} %bitcast.8, bf16[8,3,32,128]{3,2,1,0:T(8,128)(2,1)S(1)} %all-to-all-done.1.p_ref, bf16[3,1024,256]{2,1,0:T(8,128)(2,1)S(1)} %copy-done, bf16[1,2,128,256]{3,2,1,0:T(8,128)(2,1)S(1)} %add.31.refs_1_.refs_0_, ...), custom_call_target="tpu_custom_call" | custom-call | flops 201326592 | bytes 2883584 | tf_op jit(solution)/shard_map/pallas_call | solution.py:305
  (8 shorter events, 0.1 us)
Async XLA Ops:
  0.0 9.6 %collective-permute-start = (bf16[1,2,64,512]{3,2,1,0:T(8,128)(2,1)}, bf16[1,2,64,512]{3,2,1,0:T(8,128)(2,1)S(1)}, u32[]{:S(2)}, u32[]{:S(2)}) collective-permute-start(bf16[1,2,64,512]{3,2,1,0:T(8,128)(2,1)} %refs_0_.1), channel_id=1, source_target_pairs={{0,6},{1,7},{2,4},{3,5},{4,2},{5,3},{6,0},{7,1},{8,14},{9,15},{10,... | collective-permute-start | bytes 393224 | tf_op jit(solution)/shard_map/ppermute | solution.py:33
  5.0 7.0 %collective-permute-start.3 = (bf16[1,2,64,512]{3,2,1,0:T(8,128)(2,1)}, bf16[1,2,64,512]{3,2,1,0:T(8,128)(2,1)S(1)}, u32[]{:S(2)}, u32[]{:S(2)}) collective-permute-start(bf16[1,2,64,512]{3,2,1,0:T(8,128)(2,1)} %refs_0_.1), channel_id=1, source_target_pairs={{0,2},{1,3},{2,0},{3,1},{4,6},{5,7},{6,4},{7,5},{8,10},{9,11},{10,... | collective-permute-start | bytes 393224 | tf_op jit(solution)/shard_map/ppermute | solution.py:33
  5.1 7.0 %collective-permute-start.4 = (bf16[1,2,64,512]{3,2,1,0:T(8,128)(2,1)}, bf16[1,2,64,512]{3,2,1,0:T(8,128)(2,1)S(1)}, u32[]{:S(2)}, u32[]{:S(2)}) collective-permute-start(bf16[1,2,64,512]{3,2,1,0:T(8,128)(2,1)} %refs_0_.1), channel_id=1, source_target_pairs={{0,1},{1,0},{2,3},{3,2},{4,5},{5,4},{6,7},{7,6},{8,9},{9,8},{10,11... | collective-permute-start | bytes 393224 | tf_op jit(solution)/shard_map/ppermute | solution.py:33
  8.1 9.2 %collective-permute-start.2 = (bf16[1,2,128,256]{3,2,1,0:T(8,128)(2,1)}, bf16[1,2,128,256]{3,2,1,0:T(8,128)(2,1)S(1)}, u32[]{:S(2)}, u32[]{:S(2)}) collective-permute-start(bf16[1,2,128,256]{3,2,1,0:T(8,128)(2,1)} %shard_map.64), channel_id=1, source_target_pairs={{0,6},{1,7},{2,4},{3,5},{4,2},{5,3},{6,0},{7,1},{8,14},{9,15},{10,... | collective-permute-start | bytes 393224 | tf_op jit(solution)/shard_map/ppermute | solution.py:33
  9.6 7.8 %collective-permute-start.1 = (bf16[1,2,64,512]{3,2,1,0:T(8,128)(2,1)S(1)}, bf16[1,2,64,512]{3,2,1,0:T(8,128)(2,1)S(1)}, u32[]{:S(2)}, u32[]{:S(2)}) collective-permute-start(bf16[1,2,64,512]{3,2,1,0:T(8,128)(2,1)S(1)} %collective-permute-done.refs_1_), channel_id=1, source_target_pairs={{0,2},{1,3},{2,0},{3,1},{4,6},{5,7},{6,4},{7,5},{8,10},{9,11},{10,... | collective-permute-start | bytes 393224 | tf_op jit(solution)/shard_map/ppermute | solution.py:33
  12.1 8.4 %collective-permute-start.5 = (bf16[1,2,64,512]{3,2,1,0:T(8,128)(2,1)S(1)}, bf16[1,2,64,512]{3,2,1,0:T(8,128)(2,1)S(1)}, u32[]{:S(2)}, u32[]{:S(2)}) collective-permute-start(bf16[1,2,64,512]{3,2,1,0:T(8,128)(2,1)S(1)} %collective-permute-done.refs_1_), channel_id=1, source_target_pairs={{0,1},{1,0},{2,3},{3,2},{4,5},{5,4},{6,7},{7,6},{8,9},{9,8},{10,11... | collective-permute-start | bytes 393224 | tf_op jit(solution)/shard_map/ppermute | solution.py:33
  15.5 5.1 %collective-permute-start.6 = (bf16[1,2,64,512]{3,2,1,0:T(8,128)(2,1)S(1)}, bf16[1,2,64,512]{3,2,1,0:T(8,128)(2,1)S(1)}, u32[]{:S(2)}, u32[]{:S(2)}) collective-permute-start(bf16[1,2,64,512]{3,2,1,0:T(8,128)(2,1)S(1)} %collective-permute-done.3.refs_2_), channel_id=1, source_target_pairs={{0,1},{1,0},{2,3},{3,2},{4,5},{5,4},{6,7},{7,6},{8,9},{9,8},{10,11... | collective-permute-start | bytes 393224 | tf_op jit(solution)/shard_map/ppermute | solution.py:33
  15.5 1.8 %copy-start.6 = (bf16[1,2,128,256]{3,2,1,0:T(8,128)(2,1)S(1)}, bf16[1,2,128,256]{3,2,1,0:T(8,128)(2,1)}, u32[]{:S(2)}) copy-start(bf16[1,2,128,256]{3,2,1,0:T(8,128)(2,1)} %shard_map.64) | copy-start | bytes 393220
  15.6 5.1 %copy-start.1 = (bf16[1,2,64,512]{3,2,1,0:T(8,128)(2,1)S(1)}, bf16[1,2,64,512]{3,2,1,0:T(8,128)(2,1)}, u32[]{:S(2)}) copy-start(bf16[1,2,64,512]{3,2,1,0:T(8,128)(2,1)} %refs_0_.1) | copy-start | bytes 393220
  17.4 6.5 %copy-start.3 = (s32[1,8,4]{1,2,0:T(4,128)S(1)}, s32[1,8,4]{1,2,0:T(4,128)}, u32[]{:S(2)}) copy-start(s32[1,8,4]{1,2,0:T(4,128)} %param.9) | copy-start | bytes 388
  17.4 5.4 %collective-permute-start.8 = (bf16[1,2,128,256]{3,2,1,0:T(8,128)(2,1)S(1)}, bf16[1,2,128,256]{3,2,1,0:T(8,128)(2,1)S(1)}, u32[]{:S(2)}, u32[]{:S(2)}) collective-permute-start(bf16[1,2,128,256]{3,2,1,0:T(8,128)(2,1)S(1)} %add.25), channel_id=1, source_target_pairs={{0,2},{1,3},{2,0},{3,1},{4,6},{5,7},{6,4},{7,5},{8,10},{9,11},{10,... | collective-permute-start | bytes 393224 | tf_op jit(solution)/shard_map/ppermute | solution.py:33
  19.0 5.0 %collective-permute-start.7 = (bf16[1,2,64,512]{3,2,1,0:T(8,128)(2,1)S(1)}, bf16[1,2,64,512]{3,2,1,0:T(8,128)(2,1)S(1)}, u32[]{:S(2)}, u32[]{:S(2)}) collective-permute-start(bf16[1,2,64,512]{3,2,1,0:T(8,128)(2,1)S(1)} %collective-permute-done.1.refs_0_), channel_id=1, source_target_pairs={{0,1},{1,0},{2,3},{3,2},{4,5},{5,4},{6,7},{7,6},{8,9},{9,8},{10,11... | collective-permute-start | bytes 393224 | tf_op jit(solution)/shard_map/ppermute | solution.py:33
  26.0 14.9 %copy-start.2 = (s32[3]{0:T(128)S(1)}, s32[3]{0:T(128)}, u32[]{:S(2)}) copy-start(s32[3]{0:T(128)} %owner_ref.3) | copy-start | bytes 40
  26.0 6.0 %collective-permute-start.9 = (bf16[2,1024,128]{2,1,0:T(8,128)(2,1)S(1)}, bf16[2,1024,128]{2,1,0:T(8,128)(2,1)S(1)}, u32[]{:S(2)}, u32[]{:S(2)}) collective-permute-start(bf16[2,1024,128]{2,1,0:T(8,128)(2,1)S(1)} %get-tuple-element.20), channel_id=1, source_target_pairs={{0,8},{8,0},{16,24},{24,16},{1,9},{9,1},{17,25},{25,17},{2,10},{10... | collective-permute-start | bytes 1572872 | tf_op jit(solution)/shard_map/ppermute | solution.py:33
  26.1 5.9 %collective-permute-start.11 = (bf16[1,2,128,256]{3,2,1,0:T(8,128)(2,1)S(1)}, bf16[1,2,128,256]{3,2,1,0:T(8,128)(2,1)S(1)}, u32[]{:S(2)}, u32[]{:S(2)}) collective-permute-start(bf16[1,2,128,256]{3,2,1,0:T(8,128)(2,1)S(1)} %add.26), channel_id=1, source_target_pairs={{0,1},{1,0},{2,3},{3,2},{4,5},{5,4},{6,7},{7,6},{8,9},{9,8},{10,11... | collective-permute-start | bytes 393224 | tf_op jit(solution)/shard_map/ppermute | solution.py:33
  27.7 13.2 %all-to-all-start = ((bf16[32,32,128]{2,1,0:T(8,128)(2,1)}), bf16[32,32,128]{2,1,0:T(8,128)(2,1)S(1)}, u32[]{:S(2)}, u32[]{:S(2)}) async-start(bf16[32,32,128]{2,1,0:T(8,128)(2,1)} %bitcast.4), calls=%async_computation | async-start | bytes 524288 | tf_op jit(solution)/shard_map/all_to_all | solution.py:356
  32.1 0.8 %copy-start.5 = (bf16[2,1024,128]{2,1,0:T(8,128)(2,1)}, bf16[2,1024,128]{2,1,0:T(8,128)(2,1)S(1)}, u32[]{:S(2)}) copy-start(bf16[2,1024,128]{2,1,0:T(8,128)(2,1)S(1)} %collective-permute-done.9) | copy-start | bytes 1572868
  32.9 20.8 %copy-start = (bf16[3,1024,256]{2,1,0:T(8,128)(2,1)S(1)}, bf16[3,1024,256]{2,1,0:T(8,128)(2,1)}, u32[]{:S(2)}) copy-start(bf16[3,1024,256]{2,1,0:T(8,128)(2,1)} %sep_ref.3) | copy-start | bytes 4718596
  34.2 1.0 %copy-start.4 = (f32[2,1024,128]{2,1,0:T(8,128)}, f32[2,1024,128]{2,1,0:T(8,128)S(1)}, u32[]{:S(2)}) copy-start(f32[2,1024,128]{2,1,0:T(8,128)S(1)} %convert_add_fusion) | copy-start | bytes 3145732
  42.2 11.5 %all-to-all-start.1 = ((bf16[8,3,32,128]{3,2,1,0:T(8,128)(2,1)}), bf16[8,3,32,128]{3,2,1,0:T(8,128)(2,1)S(1)}, u32[]{:S(2)}, u32[]{:S(2)}) async-start(bf16[8,3,32,128]{3,2,1,0:T(8,128)(2,1)} %shard_map.68), calls=%async_computation.1 | async-start | bytes 393216 | tf_op jit(solution)/shard_map/all_to_all | solution.py:372
  45.6 8.0 %collective-permute-start.10 = (bf16[1,1024,128]{2,1,0:T(8,128)(2,1)S(1)}, bf16[1,1024,128]{2,1,0:T(8,128)(2,1)S(1)}, u32[]{:S(2)}, u32[]{:S(2)}) collective-permute-start(bf16[1,1024,128]{2,1,0:T(8,128)(2,1)S(1)} %dynamic-slice_convert_fusion.refs_0_), channel_id=1, source_target_pairs={{0,16},{8,24},{16,0},{24,8},{1,17},{9,25},{17,1},{25,9},{2,18},{10... | collective-permute-start | bytes 786440 | tf_op jit(solution)/shard_map/ppermute | solution.py:33
  46.2 1.3 %collective-permute-start.12 = (bf16[1,2,128,256]{3,2,1,0:T(8,128)(2,1)S(1)}, bf16[1,2,128,256]{3,2,1,0:T(8,128)(2,1)S(1)}, u32[]{:S(2)}, u32[]{:S(2)}) collective-permute-start(bf16[1,2,128,256]{3,2,1,0:T(8,128)(2,1)S(1)} %add.31.refs_1_.refs_0_), channel_id=1, source_target_pairs={{0,8},{8,0},{16,24},{24,16},{1,9},{9,1},{17,25},{25,17},{2,10},{10... | collective-permute-start | bytes 393224 | tf_op jit(solution)/shard_map/ppermute | solution.py:33

commit v6 on v5

--- a/solution.py
+++ b/solution.py
@@ -152,19 +152,18 @@
     )(masked, *pieces.values())
 
 
-def layer_copy(begun, masked, pieces, order, grids, copy_fill):
+def layer_copy(begun, masked, pieces, order, copy_fill):
     rows, columns = begun.shape
     panels, share = next(iter(pieces.values())).shape[1:3]
     layers = lax.axis_size("layer")
     width = columns // layers
-    piece_rows = WS // grids
     step = min(rows, 256)
     depth = panels * share * len(pieces)
     done = masked.shape[1] - depth
 
     def body(fill_ref, begun_ref, l_ref, *refs):
         u_refs = refs[: len(pieces)]
-        keep_ref, send_ref, pivot_ref, u_all, sums, fills, pivots, sems, sem = refs[len(pieces) :]
+        keep_ref, send_ref, top_ref, u_all, sums, fills, sems = refs[len(pieces) :]
         core = lax.rem(lax.axis_index("layer"), 2)
         copies = load_panels(
             u_refs, list(pieces), order[-(depth // panels // BLOCK) :], u_all, sems, lax.axis_index("grid")
@@ -184,40 +183,31 @@
             ]
             return lines[0] if len(lines) == 1 else jnp.concatenate(lines, 0)
 
-        out = pltpu.make_async_copy(pivots, pivot_ref, sem)
         for r in range(0, rows, step):
             here, slot = slice(r, r + step), r // step % 2
             sums[slot] = begun_ref[here, :] + jnp.dot(
                 l_ref[here, done:], u_all[...], preferred_element_type=jnp.float32
             )
-            if r < WS:
-                for j in range(layers):
-                    low = filled(slot, j, r, step).astype(jnp.bfloat16)
-                    for g in range(step // piece_rows):
-                        pivots[j, r // piece_rows + g] = low[g * piece_rows : (g + 1) * piece_rows]
-            if r + step == WS:
-                out.start()
             for i in range(layers // 2):
                 keep_ref[i, here, :] = filled(slot, 2 * i + core, r, step)
-                send_ref[i, here, :] = filled(slot, 2 * i + 1 - core, r, step).astype(jnp.bfloat16)
-        out.wait()
+                other = filled(slot, 2 * i + 1 - core, r, step)
+                send_ref[i, here, :] = other.astype(jnp.bfloat16)
+                if r < WS:
+                    top_ref[i, here, :] = other
 
     return kernel_call(
         body,
         (
             jax.ShapeDtypeStruct((layers // 2, rows, width), jnp.float32),
             jax.ShapeDtypeStruct((layers // 2, rows, width), jnp.bfloat16),
-            jax.ShapeDtypeStruct((layers, grids, piece_rows, width), jnp.bfloat16),
+            jax.ShapeDtypeStruct((layers // 2, WS, width), jnp.float32),
         ),
         [SMEM, VMEM, VMEM] + [HBM] * len(pieces),
-        out_specs=[VMEM, VMEM, HBM],
         scratch=[
             pltpu.VMEM((depth, columns), jnp.bfloat16),
             pltpu.VMEM((2, step, columns), jnp.float32),
             pltpu.VMEM((rows // BLOCK, columns), jnp.float32),
-            pltpu.VMEM((layers, grids, piece_rows, width), jnp.bfloat16),
             pltpu.SemaphoreType.DMA((len(pieces), panels)),
-            pltpu.SemaphoreType.DMA,
         ],
         flops=2 * rows * depth * columns,
         nbytes=2 * rows * depth + 2 * depth * columns + 8 * rows * columns,
@@ -237,15 +227,15 @@
 
 
 def pick_pivots(candidates, sep_owner, grids, after):
-    layers, _, piece_rows, width = candidates.shape
-    nodes = tree(layers)
+    pairs, _, piece_rows, width = candidates.shape
+    nodes = tree(2 * pairs)
 
     def body(owner_ref, c_ref, *refs):
         out_ref = refs[-1]
         for node, low, size, _ in nodes:
             owner = owner_ref[node]
-            total = c_ref[low, owner].astype(jnp.float32)
-            for i in range(low + 1, low + size):
+            total = c_ref[low // 2, owner].astype(jnp.float32)
+            for i in range(low // 2 + 1, (low + size) // 2):
                 total = total + c_ref[i, owner].astype(jnp.float32)
             total = total.astype(jnp.bfloat16)
             for g in range(grids):
@@ -351,9 +341,13 @@
     early = {k: piece for k, piece in pieces.items() if k * piece.shape[2] // BLOCK in order[:half]}
     late = {k: piece for k, piece in pieces.items() if k not in early}
     begun = first_part(masked, early, order)
-    keep, send, candidates = layer_copy(begun, masked, late, order, grids, jnp.swapaxes(copy_fill, 1, 2))
-    shape = candidates.shape
-    candidates = lax.all_to_all(candidates.reshape((layers * grids,) + shape[2:]), BOTH, 0, 0).reshape(shape)
+    keep, send, top = layer_copy(begun, masked, late, order, jnp.swapaxes(copy_fill, 1, 2))
+    candidates = (keep[:, :WS] + apart(top, "layer", 1)).astype(jnp.bfloat16)
+    candidates = candidates.reshape((layers // 2 * grids, WS // grids) + candidates.shape[2:])
+    alike = [[i * grids + g for i in range(core, layers, 2) for g in range(grids)] for core in (0, 1)]
+    candidates, send, below = together(candidates, send, below)
+    candidates = lax.all_to_all(candidates, BOTH, 0, 0, axis_index_groups=alike)
+    candidates = candidates.reshape((layers // 2, grids) + candidates.shape[1:])
 
     below = [below + apart(below, "grid", hops[-1])]
     below.append(apart(below[0], "layer", 1))
@@ -369,7 +363,7 @@
         keep = lax.dynamic_index_in_dim(total, side, 1, keepdims=False)
         send = lax.dynamic_index_in_dim(total, 1 - side, 1, keepdims=False).astype(jnp.bfloat16)
         if pivots is None:
-            pivots = lax.all_to_all(pick_pivots(candidates, sep_owner, grids, [send, below[0]]), "grid", 0, 0)
+            pivots = lax.all_to_all(pick_pivots(candidates, sep_owner, grids, [send]), "grid", 0, 0)
         other = apart(send, "layer", bit)
     return eliminate(keep[0], other[0], pivots, below, sep_panels)
 

time: 55.5 us -> 55.7 us (level)
  waiting for transfers between devices: 16.3 us -> 17.5 us
  local copies, waits for them, and re-layouts: 2.9 us -> 2.11 us
    all_to_all x2, starting transfers between devices: 5.97 us -> 7.82 us  [the longest x1 4.43 us: local(): candidates = lax.all_to_all(candidates, BOTH, 0, 0, axis_index_groups=alike)]
    ppermute x13 -> x14, starting transfers between devices: 18 us -> 16.6 us  [apart(): lax.ppermute(x, axis, [(i, i ^ distance) for i in range(lax.axis_size(axi...]
    add x1, other arithmetic: 1.27 us -> 0.09 us  [local(): total = keep + other.astype(jnp.float32)]
    all_to_all x2, waiting for transfers between devices: 5.8 us -> 6.83 us  [the longest x1 6.83 us: local(): candidates = lax.all_to_all(candidates, BOTH, 0, 0, axis_index_groups=alike)]
    unnamed x14 -> x12, local copies, waits for them, and re-layouts: 1.79 us -> 1.01 us
    convert_element_type x0 -> x1, other arithmetic: none -> 0.69 us  [local(): candidates = (keep[:, :WS] + apart(top, 'layer', 1)).astype(jnp.bfloat16)]
    ppermute x13 -> x14, waiting for transfers between devices: 10.5 us -> 10.7 us  [apart(): lax.ppermute(x, axis, [(i, i ^ distance) for i in range(lax.axis_size(axi...]
  transfers between devices with their start and end apart: 15 -> 16, of which waited for: 9 -> 10; matrix products, arithmetic and copies ran while one was open for 4% -> 2% of each run, Pallas kernels for 10% -> 10%
where the time goes in v6:
time: 55.7 us; the launch traced here: 55.3 us
  starting transfers between devices  24.4 us (44%)
  waiting for transfers between devices  17.5 us (31%)
  Pallas kernels  10.2 us (18%)
  local copies, waits for them, and re-layouts  2.11 us (4%)
  other arithmetic  0.88 us (2%)
    ppermute x14, starting transfers between devices, apart(): lax.ppermute(x, axis, [(i, i ^ distance) for i in range(lax.axis_size(axi...  16.6 us
    ppermute x14, waiting for transfers between devices, apart(): lax.ppermute(x, axis, [(i, i ^ distance) for i in range(lax.axis_size(axi...  10.7 us
    all_to_all x1, waiting for transfers between devices, local(): candidates = lax.all_to_all(candidates, BOTH, 0, 0, axis_index_groups=alike)  6.83 us
    all_to_all x1, starting transfers between devices, local(): candidates = lax.all_to_all(candidates, BOTH, 0, 0, axis_index_groups=alike)  4.43 us
    all_to_all x1, starting transfers between devices, local(): lax.all_to_all(pick_pivots(candidates, sep_owner, grids, [send]), 'grid',...  3.39 us
    pallas_call x1, Pallas kernels, first_part(): kernel_call(body, jax.ShapeDtypeStruct((rows, columns), jnp.float32), [VM...  2.13 us
    pallas_call x1, Pallas kernels, layer_copy(): kernel_call(body, (jax.ShapeDtypeStruct((layers // 2, rows, width), jnp.f...  2.02 us
    pallas_call x1, Pallas kernels, mask_panels(): kernel_call(body, jax.ShapeDtypeStruct((rows, panels * width), jnp.bfloat...  1.79 us
  transfers between devices with their start and end apart: 16, of which 10 were waited for; matrix products, arithmetic and copies ran while one was open for 2% of the time, Pallas kernels for 10%

profile of v6, /device:TPU:0, one launch (start us, length us, event | category | flops | bytes accessed | tf_op | source)
XLA Modules:
  0.0 55.3 jit_solution(3775483028980603219)
XLA Ops:
  0.0 5.0 %collective-permute-start = (bf16[1,2,64,512]{3,2,1,0:T(8,128)(2,1)}, bf16[1,2,64,512]{3,2,1,0:T(8,128)(2,1)S(1)}, u32[]{:S(2)}, u32[]{:S(2)}) collective-permute-start(bf16[1,2,64,512]{3,2,1,0:T(8,128)(2,1)} %refs_0_.1), channel_id=1, source_target_pairs={{0,6},{1,7},{2,4},{3,5},{4,2},{5,3},{6,0},{7,1},{8,14},{9,15},{10,... | collective-permute-start | bytes 393224 | tf_op jit(solution)/shard_map/ppermute | solution.py:33
  5.0 1.5 %collective-permute-start.4 = (bf16[1,2,64,512]{3,2,1,0:T(8,128)(2,1)}, bf16[1,2,64,512]{3,2,1,0:T(8,128)(2,1)S(1)}, u32[]{:S(2)}, u32[]{:S(2)}) collective-permute-start(bf16[1,2,64,512]{3,2,1,0:T(8,128)(2,1)} %refs_0_.1), channel_id=1, source_target_pairs={{0,1},{1,0},{2,3},{3,2},{4,5},{5,4},{6,7},{7,6},{8,9},{9,8},{10,11... | collective-permute-start | bytes 393224 | tf_op jit(solution)/shard_map/ppermute | solution.py:33
  6.5 0.0 collective-permute-start.3
  6.5 1.6 %shard_map.64 = bf16[1,2,128,256]{3,2,1,0:T(8,128)(2,1)} custom-call(s32[3]{0:T(128)} %owner_ref.3, bf16[3,1024,256]{2,1,0:T(8,128)(2,1)} %sep_ref.3), custom_call_target="tpu_custom_call" | custom-call | bytes 262144 | tf_op jit(solution)/shard_map/pallas_call | solution.py:64
  8.1 1.0 %collective-permute-start.2 = (bf16[1,2,128,256]{3,2,1,0:T(8,128)(2,1)}, bf16[1,2,128,256]{3,2,1,0:T(8,128)(2,1)S(1)}, u32[]{:S(2)}, u32[]{:S(2)}) collective-permute-start(bf16[1,2,128,256]{3,2,1,0:T(8,128)(2,1)} %shard_map.64), channel_id=1, source_target_pairs={{0,6},{1,7},{2,4},{3,5},{4,2},{5,3},{6,0},{7,1},{8,14},{9,15},{10,... | collective-permute-start | bytes 393224 | tf_op jit(solution)/shard_map/ppermute | solution.py:33
  9.1 0.5 collective-permute-done.refs_1_
  9.6 1.6 %collective-permute-start.1 = (bf16[1,2,64,512]{3,2,1,0:T(8,128)(2,1)S(1)}, bf16[1,2,64,512]{3,2,1,0:T(8,128)(2,1)S(1)}, u32[]{:S(2)}, u32[]{:S(2)}) collective-permute-start(bf16[1,2,64,512]{3,2,1,0:T(8,128)(2,1)S(1)} %collective-permute-done.refs_1_), channel_id=1, source_target_pairs={{0,2},{1,3},{2,0},{3,1},{4,6},{5,7},{6,4},{7,5},{8,10},{9,11},{10,... | collective-permute-start | bytes 393224 | tf_op jit(solution)/shard_map/ppermute | solution.py:33
  11.3 0.0 collective-permute-done.4.refs_3_
  11.3 2.9 %collective-permute-done.3.refs_2_ = bf16[1,2,64,512]{3,2,1,0:T(8,128)(2,1)S(1)} collective-permute-done((bf16[1,2,64,512]{3,2,1,0:T(8,128)(2,1)}, bf16[1,2,64,512]{3,2,1,0:T(8,128)(2,1)S(1)}, u32[]{:S(2)}, u32[]{:S(2)}) %collective-permute-start.3) | collective-permute-done | bytes 131104 | tf_op jit(solution)/shard_map/ppermute | solution.py:33
  14.2 1.4 %collective-permute-start.6 = (bf16[1,2,64,512]{3,2,1,0:T(8,128)(2,1)S(1)}, bf16[1,2,64,512]{3,2,1,0:T(8,128)(2,1)S(1)}, u32[]{:S(2)}, u32[]{:S(2)}) collective-permute-start(bf16[1,2,64,512]{3,2,1,0:T(8,128)(2,1)S(1)} %collective-permute-done.3.refs_2_), channel_id=1, source_target_pairs={{0,1},{1,0},{2,3},{3,2},{4,5},{5,4},{6,7},{7,6},{8,9},{9,8},{10,11... | collective-permute-start | bytes 393224 | tf_op jit(solution)/shard_map/ppermute | solution.py:33
  15.5 0.7 %collective-permute-start.5 = (bf16[1,2,64,512]{3,2,1,0:T(8,128)(2,1)S(1)}, bf16[1,2,64,512]{3,2,1,0:T(8,128)(2,1)S(1)}, u32[]{:S(2)}, u32[]{:S(2)}) collective-permute-start(bf16[1,2,64,512]{3,2,1,0:T(8,128)(2,1)S(1)} %collective-permute-done.refs_1_), channel_id=1, source_target_pairs={{0,1},{1,0},{2,3},{3,2},{4,5},{5,4},{6,7},{7,6},{8,9},{9,8},{10,11... | collective-permute-start | bytes 393224 | tf_op jit(solution)/shard_map/ppermute | solution.py:33
  16.2 1.8 %shard_map.65.l_ref = bf16[1024,1024]{1,0:T(8,128)(2,1)S(1)} custom-call(s32[1,2,4,8]{3,2,1,0:T(4,128)} %bitcast.10, bf16[1,2,1024,512]{3,2,1,0:T(8,128)(2,1)} %l_ref.1), custom_call_target="tpu_custom_call" | custom-call | bytes 4194304 | tf_op jit(solution)/shard_map/pallas_call | solution.py:105
  18.0 0.0 collective-permute-done.2
  18.0 0.0 copy-done.5
  18.0 0.0 copy-start.3
  18.1 0.0 collective-permute-done.1.refs_0_
  18.1 0.9 %collective-permute-start.8 = (bf16[1,2,128,256]{3,2,1,0:T(8,128)(2,1)S(1)}, bf16[1,2,128,256]{3,2,1,0:T(8,128)(2,1)S(1)}, u32[]{:S(2)}, u32[]{:S(2)}) collective-permute-start(bf16[1,2,128,256]{3,2,1,0:T(8,128)(2,1)S(1)} %add.28), channel_id=1, source_target_pairs={{0,2},{1,3},{2,0},{3,1},{4,6},{5,7},{6,4},{7,5},{8,10},{9,11},{10,... | collective-permute-start | bytes 393224 | tf_op jit(solution)/shard_map/ppermute | solution.py:33
  19.0 1.5 %collective-permute-start.7 = (bf16[1,2,64,512]{3,2,1,0:T(8,128)(2,1)S(1)}, bf16[1,2,64,512]{3,2,1,0:T(8,128)(2,1)S(1)}, u32[]{:S(2)}, u32[]{:S(2)}) collective-permute-start(bf16[1,2,64,512]{3,2,1,0:T(8,128)(2,1)S(1)} %collective-permute-done.1.refs_0_), channel_id=1, source_target_pairs={{0,1},{1,0},{2,3},{3,2},{4,5},{5,4},{6,7},{7,6},{8,9},{9,8},{10,11... | collective-permute-start | bytes 393224 | tf_op jit(solution)/shard_map/ppermute | solution.py:33
  20.5 0.0 collective-permute-done.6.refs_5_
  20.5 0.2 collective-permute-done.5.refs_4_
  20.7 0.0 copy-done.1
  20.7 2.1 %shard_map.66.begun_ref = f32[1024,512]{1,0:T(8,128)S(1)} custom-call(bf16[1024,1024]{1,0:T(8,128)(2,1)S(1)} %shard_map.65.l_ref, bf16[1,2,64,512]{3,2,1,0:T(8,128)(2,1)S(1)} %copy-done.1, bf16[1,2,64,512]{3,2,1,0:T(8,128)(2,1)S(1)} %collective-permute-done.refs_1_, bf16[1,2,64,512]{3,2,1,0:T(8,128)(2,1)S(1)} %collective-permute-done.3.refs_2_, ...), custom_call_target="tpu_custom_call" | custom-call | flops 805306368 | bytes 4456448 | tf_op jit(solution)/shard_map/pallas_call | solution.py:145
  22.8 0.3 collective-permute-done.8
  23.1 0.8 %collective-permute-done.7.refs_1_ = bf16[1,2,64,512]{3,2,1,0:T(8,128)(2,1)S(1)} collective-permute-done((bf16[1,2,64,512]{3,2,1,0:T(8,128)(2,1)S(1)}, bf16[1,2,64,512]{3,2,1,0:T(8,128)(2,1)S(1)}, u32[]{:S(2)}, u32[]{:S(2)}) %collective-permute-start.7) | collective-permute-done | bytes 131104 | tf_op jit(solution)/shard_map/ppermute | solution.py:33
  23.9 0.0 copy-done.3
  23.9 2.0 %shard_map.67 = (f32[2,1024,128]{2,1,0:T(8,128)S(1)}, bf16[2,1024,128]{2,1,0:T(8,128)(2,1)S(1)}, f32[2,256,128]{2,1,0:T(8,128)S(1)}) custom-call(s32[1,4,8]{2,1,0:T(4,128)S(1)} %bitcast.9, f32[1024,512]{1,0:T(8,128)S(1)} %shard_map.66.begun_ref, bf16[1024,1024]{1,0:T(8,128)(2,1)S(1)} %shard_map.65.l_ref, ...), custom_call_target="tpu_custom_call" | custom-call | flops 268435456 | bytes 4980736 | tf_op jit(solution)/shard_map/pallas_call | solution.py:198
  26.0 0.0 copy-start.2
  26.0 0.1 collective-permute-start.9
  26.1 1.5 %collective-permute-done.9 = f32[2,256,128]{2,1,0:T(8,128)S(1)} collective-permute-done((f32[2,256,128]{2,1,0:T(8,128)S(1)}, f32[2,256,128]{2,1,0:T(8,128)S(1)}, u32[]{:S(2)}, u32[]{:S(2)}) %collective-permute-start.9) | collective-permute-done | bytes 262176 | tf_op jit(solution)/shard_map/ppermute | solution.py:33
  27.6 0.7 %add_convert_fusion = bf16[2,256,128]{2,1,0:T(8,128)(2,1)} fusion(f32[2,256,128]{2,1,0:T(8,128)S(1)} %collective-permute-done.9, f32[2,1024,128]{2,1,0:T(8,128)S(1)} %get-tuple-element.22), kind=kLoop, calls=%fused_computation.3 | loop fusion | flops 131072 | bytes 655360 | tf_op jit(solution)/shard_map/convert_element_type | solution.py:345
  28.3 0.1 collective-permute-start.10
  28.4 4.4 %all-to-all-start = ((bf16[16,32,128]{2,1,0:T(8,128)(2,1)}), bf16[16,32,128]{2,1,0:T(8,128)(2,1)S(1)}, u32[]{:S(2)}, u32[]{:S(2)}) async-start(bf16[16,32,128]{2,1,0:T(8,128)(2,1)} %bitcast.2), calls=%async_computation | async-start | bytes 262144 | tf_op jit(solution)/shard_map/all_to_all | solution.py:349
  32.8 0.0 collective-permute-done.10
  32.9 0.1 convert_add_fusion
  32.9 0.0 copy-start.4
  33.0 1.0 %copy-done.4 = f32[2,1024,128]{2,1,0:T(8,128)} copy-done((f32[2,1024,128]{2,1,0:T(8,128)}, f32[2,1024,128]{2,1,0:T(8,128)S(1)}, u32[]{:S(2)}) %copy-start.4) | copy-done | bytes 1048600
  34.0 6.8 %all-to-all-done = bf16[16,32,128]{2,1,0:T(8,128)(2,1)S(1)} async-done(((bf16[16,32,128]{2,1,0:T(8,128)(2,1)}), bf16[16,32,128]{2,1,0:T(8,128)(2,1)S(1)}, u32[]{:S(2)}, u32[]{:S(2)}) %all-to-all-start) | async-done | bytes 131104 | tf_op jit(solution)/shard_map/all_to_all | solution.py:349
  40.8 1.2 %shard_map.68 = bf16[8,3,32,128]{3,2,1,0:T(8,128)(2,1)} custom-call(s32[3]{0:T(128)S(1)} %copy-done.2, bf16[2,8,32,128]{3,2,1,0:T(8,128)(2,1)S(1)} %bitcast.7, bf16[1,1024,128]{2,1,0:T(8,128)(2,1)S(1)} %dynamic-slice_convert_fusion.refs_0_), custom_call_target="tpu_custom_call" | custom-call | bytes 262144 | tf_op jit(solution)/shard_map/pallas_call | solution.py:244
  42.0 3.4 %all-to-all-start.1 = ((bf16[8,3,32,128]{3,2,1,0:T(8,128)(2,1)}), bf16[8,3,32,128]{3,2,1,0:T(8,128)(2,1)S(1)}, u32[]{:S(2)}, u32[]{:S(2)}) async-start(bf16[8,3,32,128]{3,2,1,0:T(8,128)(2,1)} %shard_map.68), calls=%async_computation.1 | async-start | bytes 393216 | tf_op jit(solution)/shard_map/all_to_all | solution.py:366
  45.4 1.9 %collective-permute-start.12 = (bf16[1,2,128,256]{3,2,1,0:T(8,128)(2,1)S(1)}, bf16[1,2,128,256]{3,2,1,0:T(8,128)(2,1)S(1)}, u32[]{:S(2)}, u32[]{:S(2)}) collective-permute-start(bf16[1,2,128,256]{3,2,1,0:T(8,128)(2,1)S(1)} %add.29), channel_id=1, source_target_pairs={{0,1},{1,0},{2,3},{3,2},{4,5},{5,4},{6,7},{7,6},{8,9},{9,8},{10,11... | collective-permute-start | bytes 393224 | tf_op jit(solution)/shard_map/ppermute | solution.py:33
  47.4 0.8 %collective-permute-start.11 = (bf16[1,1024,128]{2,1,0:T(8,128)(2,1)S(1)}, bf16[1,1024,128]{2,1,0:T(8,128)(2,1)S(1)}, u32[]{:S(2)}, u32[]{:S(2)}) collective-permute-start(bf16[1,1024,128]{2,1,0:T(8,128)(2,1)S(1)} %dynamic-slice_convert_fusion.refs_0_), channel_id=1, source_target_pairs={{0,16},{8,24},{16,0},{24,8},{1,17},{9,25},{17,1},{25,9},{2,18},{10... | collective-permute-start | bytes 786440 | tf_op jit(solution)/shard_map/ppermute | solution.py:33
  48.2 3.5 %collective-permute-done.12 = bf16[1,2,128,256]{3,2,1,0:T(8,128)(2,1)S(1)} collective-permute-done((bf16[1,2,128,256]{3,2,1,0:T(8,128)(2,1)S(1)}, bf16[1,2,128,256]{3,2,1,0:T(8,128)(2,1)S(1)}, u32[]{:S(2)}, u32[]{:S(2)}) %collective-permute-start.12) | collective-permute-done | bytes 131104 | tf_op jit(solution)/shard_map/ppermute | solution.py:33
  51.7 0.1 collective-permute-start.13
  51.8 1.1 %dynamic-slice_bitcast_fusion.own_ref = f32[1024,128]{1,0:T(8,128)S(1)} fusion(f32[2,1024,128]{2,1,0:T(8,128)} %copy-done.4, s32[]{:T(128)S(6)} %select_n.20), kind=kLoop, calls=%fused_computation.2 | loop fusion | bytes 1048580 | tf_op jit(solution)/shard_map/squeeze | solution.py:368
  52.9 0.2 collective-permute-done.13.refs_1_
  53.1 0.8 %collective-permute-done.11 = bf16[1,1024,128]{2,1,0:T(8,128)(2,1)S(1)} collective-permute-done((bf16[1,1024,128]{2,1,0:T(8,128)(2,1)S(1)}, bf16[1,1024,128]{2,1,0:T(8,128)(2,1)S(1)}, u32[]{:S(2)}, u32[]{:S(2)}) %collective-permute-start.11) | collective-permute-done | bytes 262176 | tf_op jit(solution)/shard_map/ppermute | solution.py:33
  53.9 0.0 all-to-all-done.1.p_ref
  53.9 1.4 %shard_map.69 = f32[1024,128]{1,0:T(8,128)} custom-call(f32[1024,128]{1,0:T(8,128)S(1)} %dynamic-slice_bitcast_fusion.own_ref, bf16[1024,128]{1,0:T(8,128)(2,1)S(1)} %bitcast.8, bf16[8,3,32,128]{3,2,1,0:T(8,128)(2,1)S(1)} %all-to-all-done.1.p_ref, bf16[3,1024,256]{2,1,0:T(8,128)(2,1)S(1)} %copy-done, bf16[1,2,128,256]{3,2,1,0:T(8,128)(2,1)S(1)} %add.35.refs_0_, ...), custom_call_target="tpu_custom_call" | custom-call | flops 201326592 | bytes 2883584 | tf_op jit(solution)/shard_map/pallas_call | solution.py:295
  (9 shorter events, 0.1 us)
Async XLA Ops:
  0.0 9.6 %collective-permute-start = (bf16[1,2,64,512]{3,2,1,0:T(8,128)(2,1)}, bf16[1,2,64,512]{3,2,1,0:T(8,128)(2,1)S(1)}, u32[]{:S(2)}, u32[]{:S(2)}) collective-permute-start(bf16[1,2,64,512]{3,2,1,0:T(8,128)(2,1)} %refs_0_.1), channel_id=1, source_target_pairs={{0,6},{1,7},{2,4},{3,5},{4,2},{5,3},{6,0},{7,1},{8,14},{9,15},{10,... | collective-permute-start | bytes 393224 | tf_op jit(solution)/shard_map/ppermute | solution.py:33
  5.0 6.2 %collective-permute-start.4 = (bf16[1,2,64,512]{3,2,1,0:T(8,128)(2,1)}, bf16[1,2,64,512]{3,2,1,0:T(8,128)(2,1)S(1)}, u32[]{:S(2)}, u32[]{:S(2)}) collective-permute-start(bf16[1,2,64,512]{3,2,1,0:T(8,128)(2,1)} %refs_0_.1), channel_id=1, source_target_pairs={{0,1},{1,0},{2,3},{3,2},{4,5},{5,4},{6,7},{7,6},{8,9},{9,8},{10,11... | collective-permute-start | bytes 393224 | tf_op jit(solution)/shard_map/ppermute | solution.py:33
  6.5 7.6 %collective-permute-start.3 = (bf16[1,2,64,512]{3,2,1,0:T(8,128)(2,1)}, bf16[1,2,64,512]{3,2,1,0:T(8,128)(2,1)S(1)}, u32[]{:S(2)}, u32[]{:S(2)}) collective-permute-start(bf16[1,2,64,512]{3,2,1,0:T(8,128)(2,1)} %refs_0_.1), channel_id=1, source_target_pairs={{0,2},{1,3},{2,0},{3,1},{4,6},{5,7},{6,4},{7,5},{8,10},{9,11},{10,... | collective-permute-start | bytes 393224 | tf_op jit(solution)/shard_map/ppermute | solution.py:33
  8.1 9.8 %collective-permute-start.2 = (bf16[1,2,128,256]{3,2,1,0:T(8,128)(2,1)}, bf16[1,2,128,256]{3,2,1,0:T(8,128)(2,1)S(1)}, u32[]{:S(2)}, u32[]{:S(2)}) collective-permute-start(bf16[1,2,128,256]{3,2,1,0:T(8,128)(2,1)} %shard_map.64), channel_id=1, source_target_pairs={{0,6},{1,7},{2,4},{3,5},{4,2},{5,3},{6,0},{7,1},{8,14},{9,15},{10,... | collective-permute-start | bytes 393224 | tf_op jit(solution)/shard_map/ppermute | solution.py:33
  9.6 8.4 %collective-permute-start.1 = (bf16[1,2,64,512]{3,2,1,0:T(8,128)(2,1)S(1)}, bf16[1,2,64,512]{3,2,1,0:T(8,128)(2,1)S(1)}, u32[]{:S(2)}, u32[]{:S(2)}) collective-permute-start(bf16[1,2,64,512]{3,2,1,0:T(8,128)(2,1)S(1)} %collective-permute-done.refs_1_), channel_id=1, source_target_pairs={{0,2},{1,3},{2,0},{3,1},{4,6},{5,7},{6,4},{7,5},{8,10},{9,11},{10,... | collective-permute-start | bytes 393224 | tf_op jit(solution)/shard_map/ppermute | solution.py:33
  14.2 6.3 %collective-permute-start.6 = (bf16[1,2,64,512]{3,2,1,0:T(8,128)(2,1)S(1)}, bf16[1,2,64,512]{3,2,1,0:T(8,128)(2,1)S(1)}, u32[]{:S(2)}, u32[]{:S(2)}) collective-permute-start(bf16[1,2,64,512]{3,2,1,0:T(8,128)(2,1)S(1)} %collective-permute-done.3.refs_2_), channel_id=1, source_target_pairs={{0,1},{1,0},{2,3},{3,2},{4,5},{5,4},{6,7},{7,6},{8,9},{9,8},{10,11... | collective-permute-start | bytes 393224 | tf_op jit(solution)/shard_map/ppermute | solution.py:33
  15.5 5.2 %collective-permute-start.5 = (bf16[1,2,64,512]{3,2,1,0:T(8,128)(2,1)S(1)}, bf16[1,2,64,512]{3,2,1,0:T(8,128)(2,1)S(1)}, u32[]{:S(2)}, u32[]{:S(2)}) collective-permute-start(bf16[1,2,64,512]{3,2,1,0:T(8,128)(2,1)S(1)} %collective-permute-done.refs_1_), channel_id=1, source_target_pairs={{0,1},{1,0},{2,3},{3,2},{4,5},{5,4},{6,7},{7,6},{8,9},{9,8},{10,11... | collective-permute-start | bytes 393224 | tf_op jit(solution)/shard_map/ppermute | solution.py:33
  16.2 1.8 %copy-start.5 = (bf16[1,2,128,256]{3,2,1,0:T(8,128)(2,1)S(1)}, bf16[1,2,128,256]{3,2,1,0:T(8,128)(2,1)}, u32[]{:S(2)}) copy-start(bf16[1,2,128,256]{3,2,1,0:T(8,128)(2,1)} %shard_map.64) | copy-start | bytes 393220
  16.2 4.5 %copy-start.1 = (bf16[1,2,64,512]{3,2,1,0:T(8,128)(2,1)S(1)}, bf16[1,2,64,512]{3,2,1,0:T(8,128)(2,1)}, u32[]{:S(2)}) copy-start(bf16[1,2,64,512]{3,2,1,0:T(8,128)(2,1)} %refs_0_.1) | copy-start | bytes 393220
  18.0 5.9 %copy-start.3 = (s32[1,8,4]{1,2,0:T(4,128)S(1)}, s32[1,8,4]{1,2,0:T(4,128)}, u32[]{:S(2)}) copy-start(s32[1,8,4]{1,2,0:T(4,128)} %param.9) | copy-start | bytes 388
  18.1 5.0 %collective-permute-start.8 = (bf16[1,2,128,256]{3,2,1,0:T(8,128)(2,1)S(1)}, bf16[1,2,128,256]{3,2,1,0:T(8,128)(2,1)S(1)}, u32[]{:S(2)}, u32[]{:S(2)}) collective-permute-start(bf16[1,2,128,256]{3,2,1,0:T(8,128)(2,1)S(1)} %add.28), channel_id=1, source_target_pairs={{0,2},{1,3},{2,0},{3,1},{4,6},{5,7},{6,4},{7,5},{8,10},{9,11},{10,... | collective-permute-start | bytes 393224 | tf_op jit(solution)/shard_map/ppermute | solution.py:33
  19.0 5.0 %collective-permute-start.7 = (bf16[1,2,64,512]{3,2,1,0:T(8,128)(2,1)S(1)}, bf16[1,2,64,512]{3,2,1,0:T(8,128)(2,1)S(1)}, u32[]{:S(2)}, u32[]{:S(2)}) collective-permute-start(bf16[1,2,64,512]{3,2,1,0:T(8,128)(2,1)S(1)} %collective-permute-done.1.refs_0_), channel_id=1, source_target_pairs={{0,1},{1,0},{2,3},{3,2},{4,5},{5,4},{6,7},{7,6},{8,9},{9,8},{10,11... | collective-permute-start | bytes 393224 | tf_op jit(solution)/shard_map/ppermute | solution.py:33
  26.0 14.8 %copy-start.2 = (s32[3]{0:T(128)S(1)}, s32[3]{0:T(128)}, u32[]{:S(2)}) copy-start(s32[3]{0:T(128)} %owner_ref.3) | copy-start | bytes 40
  26.0 1.6 %collective-permute-start.9 = (f32[2,256,128]{2,1,0:T(8,128)S(1)}, f32[2,256,128]{2,1,0:T(8,128)S(1)}, u32[]{:S(2)}, u32[]{:S(2)}) collective-permute-start(f32[2,256,128]{2,1,0:T(8,128)S(1)} %get-tuple-element.23), channel_id=1, source_target_pairs={{0,8},{8,0},{16,24},{24,16},{1,9},{9,1},{17,25},{25,17},{2,10},{10... | collective-permute-start | bytes 786440 | tf_op jit(solution)/shard_map/ppermute | solution.py:33
  28.3 4.6 %collective-permute-start.10 = (bf16[2,1024,128]{2,1,0:T(8,128)(2,1)S(1)}, bf16[2,1024,128]{2,1,0:T(8,128)(2,1)S(1)}, u32[]{:S(2)}, u32[]{:S(2)}) collective-permute-start(bf16[2,1024,128]{2,1,0:T(8,128)(2,1)S(1)} %get-tuple-element.26), channel_id=1, source_target_pairs={{0,8},{8,0},{16,24},{24,16},{1,9},{9,1},{17,25},{25,17},{2,10},{10... | collective-permute-start | bytes 1572872 | tf_op jit(solution)/shard_map/ppermute | solution.py:33
  28.4 12.4 %all-to-all-start = ((bf16[16,32,128]{2,1,0:T(8,128)(2,1)}), bf16[16,32,128]{2,1,0:T(8,128)(2,1)S(1)}, u32[]{:S(2)}, u32[]{:S(2)}) async-start(bf16[16,32,128]{2,1,0:T(8,128)(2,1)} %bitcast.2), calls=%async_computation | async-start | bytes 262144 | tf_op jit(solution)/shard_map/all_to_all | solution.py:349
  32.9 1.0 %copy-start.4 = (f32[2,1024,128]{2,1,0:T(8,128)}, f32[2,1024,128]{2,1,0:T(8,128)S(1)}, u32[]{:S(2)}) copy-start(f32[2,1024,128]{2,1,0:T(8,128)S(1)} %convert_add_fusion) | copy-start | bytes 3145732
  33.9 20.0 %copy-start = (bf16[3,1024,256]{2,1,0:T(8,128)(2,1)S(1)}, bf16[3,1024,256]{2,1,0:T(8,128)(2,1)}, u32[]{:S(2)}) copy-start(bf16[3,1024,256]{2,1,0:T(8,128)(2,1)} %sep_ref.3) | copy-start | bytes 4718596
  42.0 11.8 %all-to-all-start.1 = ((bf16[8,3,32,128]{3,2,1,0:T(8,128)(2,1)}), bf16[8,3,32,128]{3,2,1,0:T(8,128)(2,1)S(1)}, u32[]{:S(2)}, u32[]{:S(2)}) async-start(bf16[8,3,32,128]{3,2,1,0:T(8,128)(2,1)} %shard_map.68), calls=%async_computation.1 | async-start | bytes 393216 | tf_op jit(solution)/shard_map/all_to_all | solution.py:366
  45.4 6.2 %collective-permute-start.12 = (bf16[1,2,128,256]{3,2,1,0:T(8,128)(2,1)S(1)}, bf16[1,2,128,256]{3,2,1,0:T(8,128)(2,1)S(1)}, u32[]{:S(2)}, u32[]{:S(2)}) collective-permute-start(bf16[1,2,128,256]{3,2,1,0:T(8,128)(2,1)S(1)} %add.29), channel_id=1, source_target_pairs={{0,1},{1,0},{2,3},{3,2},{4,5},{5,4},{6,7},{7,6},{8,9},{9,8},{10,11... | collective-permute-start | bytes 393224 | tf_op jit(solution)/shard_map/ppermute | solution.py:33
  47.4 6.5 %collective-permute-start.11 = (bf16[1,1024,128]{2,1,0:T(8,128)(2,1)S(1)}, bf16[1,1024,128]{2,1,0:T(8,128)(2,1)S(1)}, u32[]{:S(2)}, u32[]{:S(2)}) collective-permute-start(bf16[1,1024,128]{2,1,0:T(8,128)(2,1)S(1)} %dynamic-slice_convert_fusion.refs_0_), channel_id=1, source_target_pairs={{0,16},{8,24},{16,0},{24,8},{1,17},{9,25},{17,1},{25,9},{2,18},{10... | collective-permute-start | bytes 786440 | tf_op jit(solution)/shard_map/ppermute | solution.py:33
  51.7 1.4 %collective-permute-start.13 = (bf16[1,2,128,256]{3,2,1,0:T(8,128)(2,1)S(1)}, bf16[1,2,128,256]{3,2,1,0:T(8,128)(2,1)S(1)}, u32[]{:S(2)}, u32[]{:S(2)}) collective-permute-start(bf16[1,2,128,256]{3,2,1,0:T(8,128)(2,1)S(1)} %add.35.refs_0_), channel_id=1, source_target_pairs={{0,8},{8,0},{16,24},{24,16},{1,9},{9,1},{17,25},{25,17},{2,10},{10... | collective-permute-start | bytes 393224 | tf_op jit(solution)/shard_map/ppermute | solution.py:33

commit v7 on v6

--- a/solution.py
+++ b/solution.py
@@ -273,20 +273,22 @@
             if under:
                 which = [n[0] for n in inner].index(node)
                 pivot = all_p[at : at + WS, :].astype(jnp.float32)
+                taken = jnp.zeros_like(pivot)
                 for m in under:
-                    pivot = pivot - jnp.dot(
+                    taken = taken + jnp.dot(
                         all_below[which, m], all_p[m * WS : (m + 1) * WS, :], preferred_element_type=jnp.float32
                     )
-                all_p[at : at + WS, :] = pivot.astype(jnp.bfloat16)
+                all_p[at : at + WS, :] = (pivot - taken).astype(jnp.bfloat16)
         copies = []
         for r in range(0, rows, step):
             here = slice(r, r + step)
             total = own_ref[here, :] + other_ref[here, :].astype(jnp.float32)
+            taken = jnp.zeros_like(total)
             for node in range(count):
-                total = total - jnp.dot(
+                taken = taken + jnp.dot(
                     sep_ref[node, here, :], all_p[node * WS : (node + 1) * WS, :], preferred_element_type=jnp.float32
                 )
-            result[here, :] = total
+            result[here, :] = total - taken
             copies.append(pltpu.make_async_copy(result.at[here], out_ref.at[here], sems.at[r // step]))
             copies[-1].start()
         for copy in copies:
@@ -319,6 +321,8 @@
     beside = apart(u_panels, "grid", near)
     for hop in hops[:-1]:
         for k, piece in list(pieces.items()):
+            if k == far:
+                piece, _ = together(piece, below)
             pieces[k ^ hop] = apart(piece, "grid", hop)
     blocks = [k * u_panels.shape[2] // BLOCK for k in pieces]
     order = list(dict.fromkeys(blocks))

time: 55.7 us -> 55.7 us (level)
  no operation moved by 1% of the time
where the time goes in v7:
time: 55.7 us; the launch traced here: 55.3 us
  starting transfers between devices  24.4 us (44%)
  waiting for transfers between devices  17.5 us (31%)
  Pallas kernels  10.2 us (18%)
  local copies, waits for them, and re-layouts  2.11 us (4%)
  other arithmetic  0.88 us (2%)
    ppermute x14, starting transfers between devices, apart(): lax.ppermute(x, axis, [(i, i ^ distance) for i in range(lax.axis_size(axi...  16.6 us
    ppermute x14, waiting for transfers between devices, apart(): lax.ppermute(x, axis, [(i, i ^ distance) for i in range(lax.axis_size(axi...  10.7 us
    all_to_all x1, waiting for transfers between devices, local(): candidates = lax.all_to_all(candidates, BOTH, 0, 0, axis_index_groups=alike)  6.83 us
    all_to_all x1, starting transfers between devices, local(): candidates = lax.all_to_all(candidates, BOTH, 0, 0, axis_index_groups=alike)  4.43 us
    all_to_all x1, starting transfers between devices, local(): lax.all_to_all(pick_pivots(candidates, sep_owner, grids, [send]), 'grid',...  3.39 us
    pallas_call x1, Pallas kernels, first_part(): kernel_call(body, jax.ShapeDtypeStruct((rows, columns), jnp.float32), [VM...  2.13 us
    pallas_call x1, Pallas kernels, layer_copy(): kernel_call(body, (jax.ShapeDtypeStruct((layers // 2, rows, width), jnp.f...  2.02 us
    pallas_call x1, Pallas kernels, mask_panels(): kernel_call(body, jax.ShapeDtypeStruct((rows, panels * width), jnp.bfloat...  1.79 us
  transfers between devices with their start and end apart: 16, of which 10 were waited for; matrix products, arithmetic and copies ran while one was open for 2% of the time, Pallas kernels for 10%

profile of v7, /device:TPU:0, one launch (start us, length us, event | category | flops | bytes accessed | tf_op | source)
XLA Modules:
  0.0 55.3 jit_solution(16786663350279166225)
XLA Ops:
  0.0 5.0 %collective-permute-start = (bf16[1,2,64,512]{3,2,1,0:T(8,128)(2,1)}, bf16[1,2,64,512]{3,2,1,0:T(8,128)(2,1)S(1)}, u32[]{:S(2)}, u32[]{:S(2)}) collective-permute-start(bf16[1,2,64,512]{3,2,1,0:T(8,128)(2,1)} %refs_0_.1), channel_id=1, source_target_pairs={{0,6},{1,7},{2,4},{3,5},{4,2},{5,3},{6,0},{7,1},{8,14},{9,15},{10,... | collective-permute-start | bytes 393224 | tf_op jit(solution)/shard_map/ppermute | solution.py:33
  5.0 1.5 %collective-permute-start.4 = (bf16[1,2,64,512]{3,2,1,0:T(8,128)(2,1)}, bf16[1,2,64,512]{3,2,1,0:T(8,128)(2,1)S(1)}, u32[]{:S(2)}, u32[]{:S(2)}) collective-permute-start(bf16[1,2,64,512]{3,2,1,0:T(8,128)(2,1)} %refs_0_.1), channel_id=1, source_target_pairs={{0,1},{1,0},{2,3},{3,2},{4,5},{5,4},{6,7},{7,6},{8,9},{9,8},{10,11... | collective-permute-start | bytes 393224 | tf_op jit(solution)/shard_map/ppermute | solution.py:33
  6.5 0.0 collective-permute-start.3
  6.5 1.6 %shard_map.64 = bf16[1,2,128,256]{3,2,1,0:T(8,128)(2,1)} custom-call(s32[3]{0:T(128)} %owner_ref.3, bf16[3,1024,256]{2,1,0:T(8,128)(2,1)} %sep_ref.3), custom_call_target="tpu_custom_call" | custom-call | bytes 262144 | tf_op jit(solution)/shard_map/pallas_call | solution.py:64
  8.1 1.0 %collective-permute-start.2 = (bf16[1,2,128,256]{3,2,1,0:T(8,128)(2,1)}, bf16[1,2,128,256]{3,2,1,0:T(8,128)(2,1)S(1)}, u32[]{:S(2)}, u32[]{:S(2)}) collective-permute-start(bf16[1,2,128,256]{3,2,1,0:T(8,128)(2,1)} %shard_map.64), channel_id=1, source_target_pairs={{0,6},{1,7},{2,4},{3,5},{4,2},{5,3},{6,0},{7,1},{8,14},{9,15},{10,... | collective-permute-start | bytes 393224 | tf_op jit(solution)/shard_map/ppermute | solution.py:33
  9.1 0.5 collective-permute-done.refs_1_
  9.6 1.6 %collective-permute-start.1 = (bf16[1,2,64,512]{3,2,1,0:T(8,128)(2,1)S(1)}, bf16[1,2,64,512]{3,2,1,0:T(8,128)(2,1)S(1)}, u32[]{:S(2)}, u32[]{:S(2)}) collective-permute-start(bf16[1,2,64,512]{3,2,1,0:T(8,128)(2,1)S(1)} %collective-permute-done.refs_1_), channel_id=1, source_target_pairs={{0,2},{1,3},{2,0},{3,1},{4,6},{5,7},{6,4},{7,5},{8,10},{9,11},{10,... | collective-permute-start | bytes 393224 | tf_op jit(solution)/shard_map/ppermute | solution.py:33
  11.3 0.0 collective-permute-done.4.refs_3_
  11.3 2.9 %collective-permute-done.3.refs_2_ = bf16[1,2,64,512]{3,2,1,0:T(8,128)(2,1)S(1)} collective-permute-done((bf16[1,2,64,512]{3,2,1,0:T(8,128)(2,1)}, bf16[1,2,64,512]{3,2,1,0:T(8,128)(2,1)S(1)}, u32[]{:S(2)}, u32[]{:S(2)}) %collective-permute-start.3) | collective-permute-done | bytes 131104 | tf_op jit(solution)/shard_map/ppermute | solution.py:33
  14.2 1.4 %collective-permute-start.6 = (bf16[1,2,64,512]{3,2,1,0:T(8,128)(2,1)S(1)}, bf16[1,2,64,512]{3,2,1,0:T(8,128)(2,1)S(1)}, u32[]{:S(2)}, u32[]{:S(2)}) collective-permute-start(bf16[1,2,64,512]{3,2,1,0:T(8,128)(2,1)S(1)} %collective-permute-done.3.refs_2_), channel_id=1, source_target_pairs={{0,1},{1,0},{2,3},{3,2},{4,5},{5,4},{6,7},{7,6},{8,9},{9,8},{10,11... | collective-permute-start | bytes 393224 | tf_op jit(solution)/shard_map/ppermute | solution.py:33
  15.5 0.7 %collective-permute-start.5 = (bf16[1,2,64,512]{3,2,1,0:T(8,128)(2,1)S(1)}, bf16[1,2,64,512]{3,2,1,0:T(8,128)(2,1)S(1)}, u32[]{:S(2)}, u32[]{:S(2)}) collective-permute-start(bf16[1,2,64,512]{3,2,1,0:T(8,128)(2,1)S(1)} %collective-permute-done.refs_1_), channel_id=1, source_target_pairs={{0,1},{1,0},{2,3},{3,2},{4,5},{5,4},{6,7},{7,6},{8,9},{9,8},{10,11... | collective-permute-start | bytes 393224 | tf_op jit(solution)/shard_map/ppermute | solution.py:33
  16.2 1.8 %shard_map.65.l_ref = bf16[1024,1024]{1,0:T(8,128)(2,1)S(1)} custom-call(s32[1,2,4,8]{3,2,1,0:T(4,128)} %bitcast.10, bf16[1,2,1024,512]{3,2,1,0:T(8,128)(2,1)} %l_ref.1), custom_call_target="tpu_custom_call" | custom-call | bytes 4194304 | tf_op jit(solution)/shard_map/pallas_call | solution.py:105
  18.0 0.0 collective-permute-done.2
  18.0 0.0 copy-done.5
  18.0 0.0 copy-start.3
  18.1 0.0 collective-permute-done.1.refs_0_
  18.1 0.9 %collective-permute-start.8 = (bf16[1,2,128,256]{3,2,1,0:T(8,128)(2,1)S(1)}, bf16[1,2,128,256]{3,2,1,0:T(8,128)(2,1)S(1)}, u32[]{:S(2)}, u32[]{:S(2)}) collective-permute-start(bf16[1,2,128,256]{3,2,1,0:T(8,128)(2,1)S(1)} %add.28), channel_id=1, source_target_pairs={{0,2},{1,3},{2,0},{3,1},{4,6},{5,7},{6,4},{7,5},{8,10},{9,11},{10,... | collective-permute-start | bytes 393224 | tf_op jit(solution)/shard_map/ppermute | solution.py:33
  19.0 1.5 %collective-permute-start.7 = (bf16[1,2,64,512]{3,2,1,0:T(8,128)(2,1)S(1)}, bf16[1,2,64,512]{3,2,1,0:T(8,128)(2,1)S(1)}, u32[]{:S(2)}, u32[]{:S(2)}) collective-permute-start(bf16[1,2,64,512]{3,2,1,0:T(8,128)(2,1)S(1)} %collective-permute-done.1.refs_0_), channel_id=1, source_target_pairs={{0,1},{1,0},{2,3},{3,2},{4,5},{5,4},{6,7},{7,6},{8,9},{9,8},{10,11... | collective-permute-start | bytes 393224 | tf_op jit(solution)/shard_map/ppermute | solution.py:33
  20.5 0.0 collective-permute-done.6.refs_5_
  20.5 0.2 collective-permute-done.5.refs_4_
  20.7 0.0 copy-done.1
  20.7 2.1 %shard_map.66.begun_ref = f32[1024,512]{1,0:T(8,128)S(1)} custom-call(bf16[1024,1024]{1,0:T(8,128)(2,1)S(1)} %shard_map.65.l_ref, bf16[1,2,64,512]{3,2,1,0:T(8,128)(2,1)S(1)} %copy-done.1, bf16[1,2,64,512]{3,2,1,0:T(8,128)(2,1)S(1)} %collective-permute-done.refs_1_, bf16[1,2,64,512]{3,2,1,0:T(8,128)(2,1)S(1)} %collective-permute-done.3.refs_2_, ...), custom_call_target="tpu_custom_call" | custom-call | flops 805306368 | bytes 4456448 | tf_op jit(solution)/shard_map/pallas_call | solution.py:145
  22.8 0.3 collective-permute-done.8
  23.1 0.8 %collective-permute-done.7.refs_1_ = bf16[1,2,64,512]{3,2,1,0:T(8,128)(2,1)S(1)} collective-permute-done((bf16[1,2,64,512]{3,2,1,0:T(8,128)(2,1)S(1)}, bf16[1,2,64,512]{3,2,1,0:T(8,128)(2,1)S(1)}, u32[]{:S(2)}, u32[]{:S(2)}) %collective-permute-start.7) | collective-permute-done | bytes 131104 | tf_op jit(solution)/shard_map/ppermute | solution.py:33
  23.9 0.0 copy-done.3
  23.9 2.0 %shard_map.67 = (f32[2,1024,128]{2,1,0:T(8,128)S(1)}, bf16[2,1024,128]{2,1,0:T(8,128)(2,1)S(1)}, f32[2,256,128]{2,1,0:T(8,128)S(1)}) custom-call(s32[1,4,8]{2,1,0:T(4,128)S(1)} %bitcast.9, f32[1024,512]{1,0:T(8,128)S(1)} %shard_map.66.begun_ref, bf16[1024,1024]{1,0:T(8,128)(2,1)S(1)} %shard_map.65.l_ref, ...), custom_call_target="tpu_custom_call" | custom-call | flops 268435456 | bytes 4980736 | tf_op jit(solution)/shard_map/pallas_call | solution.py:198
  26.0 0.0 copy-start.2
  26.0 0.1 collective-permute-start.9
  26.1 1.5 %collective-permute-done.9 = f32[2,256,128]{2,1,0:T(8,128)S(1)} collective-permute-done((f32[2,256,128]{2,1,0:T(8,128)S(1)}, f32[2,256,128]{2,1,0:T(8,128)S(1)}, u32[]{:S(2)}, u32[]{:S(2)}) %collective-permute-start.9) | collective-permute-done | bytes 262176 | tf_op jit(solution)/shard_map/ppermute | solution.py:33
  27.6 0.7 %add_convert_fusion = bf16[2,256,128]{2,1,0:T(8,128)(2,1)} fusion(f32[2,256,128]{2,1,0:T(8,128)S(1)} %collective-permute-done.9, f32[2,1024,128]{2,1,0:T(8,128)S(1)} %get-tuple-element.24), kind=kLoop, calls=%fused_computation.3 | loop fusion | flops 131072 | bytes 655360 | tf_op jit(solution)/shard_map/convert_element_type | solution.py:349
  28.3 0.1 collective-permute-start.10
  28.4 4.4 %all-to-all-start = ((bf16[16,32,128]{2,1,0:T(8,128)(2,1)}), bf16[16,32,128]{2,1,0:T(8,128)(2,1)S(1)}, u32[]{:S(2)}, u32[]{:S(2)}) async-start(bf16[16,32,128]{2,1,0:T(8,128)(2,1)} %bitcast.2), calls=%async_computation | async-start | bytes 262144 | tf_op jit(solution)/shard_map/all_to_all | solution.py:353
  32.8 0.0 collective-permute-done.10
  32.9 0.1 convert_add_fusion
  32.9 0.0 copy-start.4
  33.0 1.0 %copy-done.4 = f32[2,1024,128]{2,1,0:T(8,128)} copy-done((f32[2,1024,128]{2,1,0:T(8,128)}, f32[2,1024,128]{2,1,0:T(8,128)S(1)}, u32[]{:S(2)}) %copy-start.4) | copy-done | bytes 1048600
  34.0 6.8 %all-to-all-done = bf16[16,32,128]{2,1,0:T(8,128)(2,1)S(1)} async-done(((bf16[16,32,128]{2,1,0:T(8,128)(2,1)}), bf16[16,32,128]{2,1,0:T(8,128)(2,1)S(1)}, u32[]{:S(2)}, u32[]{:S(2)}) %all-to-all-start) | async-done | bytes 131104 | tf_op jit(solution)/shard_map/all_to_all | solution.py:353
  40.8 1.2 %shard_map.68 = bf16[8,3,32,128]{3,2,1,0:T(8,128)(2,1)} custom-call(s32[3]{0:T(128)S(1)} %copy-done.2, bf16[2,8,32,128]{3,2,1,0:T(8,128)(2,1)S(1)} %bitcast.7, bf16[1,1024,128]{2,1,0:T(8,128)(2,1)S(1)} %dynamic-slice_convert_fusion.refs_0_), custom_call_target="tpu_custom_call" | custom-call | bytes 262144 | tf_op jit(solution)/shard_map/pallas_call | solution.py:244
  42.0 3.4 %all-to-all-start.1 = ((bf16[8,3,32,128]{3,2,1,0:T(8,128)(2,1)}), bf16[8,3,32,128]{3,2,1,0:T(8,128)(2,1)S(1)}, u32[]{:S(2)}, u32[]{:S(2)}) async-start(bf16[8,3,32,128]{3,2,1,0:T(8,128)(2,1)} %shard_map.68), calls=%async_computation.1 | async-start | bytes 393216 | tf_op jit(solution)/shard_map/all_to_all | solution.py:370
  45.4 1.9 %collective-permute-start.12 = (bf16[1,2,128,256]{3,2,1,0:T(8,128)(2,1)S(1)}, bf16[1,2,128,256]{3,2,1,0:T(8,128)(2,1)S(1)}, u32[]{:S(2)}, u32[]{:S(2)}) collective-permute-start(bf16[1,2,128,256]{3,2,1,0:T(8,128)(2,1)S(1)} %add.29), channel_id=1, source_target_pairs={{0,1},{1,0},{2,3},{3,2},{4,5},{5,4},{6,7},{7,6},{8,9},{9,8},{10,11... | collective-permute-start | bytes 393224 | tf_op jit(solution)/shard_map/ppermute | solution.py:33
  47.4 0.8 %collective-permute-start.11 = (bf16[1,1024,128]{2,1,0:T(8,128)(2,1)S(1)}, bf16[1,1024,128]{2,1,0:T(8,128)(2,1)S(1)}, u32[]{:S(2)}, u32[]{:S(2)}) collective-permute-start(bf16[1,1024,128]{2,1,0:T(8,128)(2,1)S(1)} %dynamic-slice_convert_fusion.refs_0_), channel_id=1, source_target_pairs={{0,16},{8,24},{16,0},{24,8},{1,17},{9,25},{17,1},{25,9},{2,18},{10... | collective-permute-start | bytes 786440 | tf_op jit(solution)/shard_map/ppermute | solution.py:33
  48.2 3.5 %collective-permute-done.12 = bf16[1,2,128,256]{3,2,1,0:T(8,128)(2,1)S(1)} collective-permute-done((bf16[1,2,128,256]{3,2,1,0:T(8,128)(2,1)S(1)}, bf16[1,2,128,256]{3,2,1,0:T(8,128)(2,1)S(1)}, u32[]{:S(2)}, u32[]{:S(2)}) %collective-permute-start.12) | collective-permute-done | bytes 131104 | tf_op jit(solution)/shard_map/ppermute | solution.py:33
  51.7 0.1 collective-permute-start.13
  51.8 1.1 %dynamic-slice_bitcast_fusion.own_ref = f32[1024,128]{1,0:T(8,128)S(1)} fusion(f32[2,1024,128]{2,1,0:T(8,128)} %copy-done.4, s32[]{:T(128)S(6)} %select_n.20), kind=kLoop, calls=%fused_computation.2 | loop fusion | bytes 1048580 | tf_op jit(solution)/shard_map/squeeze | solution.py:372
  52.9 0.2 collective-permute-done.13.refs_1_
  53.1 0.8 %collective-permute-done.11 = bf16[1,1024,128]{2,1,0:T(8,128)(2,1)S(1)} collective-permute-done((bf16[1,1024,128]{2,1,0:T(8,128)(2,1)S(1)}, bf16[1,1024,128]{2,1,0:T(8,128)(2,1)S(1)}, u32[]{:S(2)}, u32[]{:S(2)}) %collective-permute-start.11) | collective-permute-done | bytes 262176 | tf_op jit(solution)/shard_map/ppermute | solution.py:33
  53.9 0.0 all-to-all-done.1.p_ref
  53.9 1.4 %shard_map.69 = f32[1024,128]{1,0:T(8,128)} custom-call(f32[1024,128]{1,0:T(8,128)S(1)} %dynamic-slice_bitcast_fusion.own_ref, bf16[1024,128]{1,0:T(8,128)(2,1)S(1)} %bitcast.8, bf16[8,3,32,128]{3,2,1,0:T(8,128)(2,1)S(1)} %all-to-all-done.1.p_ref, bf16[3,1024,256]{2,1,0:T(8,128)(2,1)S(1)} %copy-done, bf16[1,2,128,256]{3,2,1,0:T(8,128)(2,1)S(1)} %add.35.refs_0_, ...), custom_call_target="tpu_custom_call" | custom-call | flops 201326592 | bytes 2883584 | tf_op jit(solution)/shard_map/pallas_call | solution.py:297
  (9 shorter events, 0.1 us)
Async XLA Ops:
  0.0 9.6 %collective-permute-start = (bf16[1,2,64,512]{3,2,1,0:T(8,128)(2,1)}, bf16[1,2,64,512]{3,2,1,0:T(8,128)(2,1)S(1)}, u32[]{:S(2)}, u32[]{:S(2)}) collective-permute-start(bf16[1,2,64,512]{3,2,1,0:T(8,128)(2,1)} %refs_0_.1), channel_id=1, source_target_pairs={{0,6},{1,7},{2,4},{3,5},{4,2},{5,3},{6,0},{7,1},{8,14},{9,15},{10,... | collective-permute-start | bytes 393224 | tf_op jit(solution)/shard_map/ppermute | solution.py:33
  5.0 6.2 %collective-permute-start.4 = (bf16[1,2,64,512]{3,2,1,0:T(8,128)(2,1)}, bf16[1,2,64,512]{3,2,1,0:T(8,128)(2,1)S(1)}, u32[]{:S(2)}, u32[]{:S(2)}) collective-permute-start(bf16[1,2,64,512]{3,2,1,0:T(8,128)(2,1)} %refs_0_.1), channel_id=1, source_target_pairs={{0,1},{1,0},{2,3},{3,2},{4,5},{5,4},{6,7},{7,6},{8,9},{9,8},{10,11... | collective-permute-start | bytes 393224 | tf_op jit(solution)/shard_map/ppermute | solution.py:33
  6.5 7.6 %collective-permute-start.3 = (bf16[1,2,64,512]{3,2,1,0:T(8,128)(2,1)}, bf16[1,2,64,512]{3,2,1,0:T(8,128)(2,1)S(1)}, u32[]{:S(2)}, u32[]{:S(2)}) collective-permute-start(bf16[1,2,64,512]{3,2,1,0:T(8,128)(2,1)} %refs_0_.1), channel_id=1, source_target_pairs={{0,2},{1,3},{2,0},{3,1},{4,6},{5,7},{6,4},{7,5},{8,10},{9,11},{10,... | collective-permute-start | bytes 393224 | tf_op jit(solution)/shard_map/ppermute | solution.py:33
  8.1 9.8 %collective-permute-start.2 = (bf16[1,2,128,256]{3,2,1,0:T(8,128)(2,1)}, bf16[1,2,128,256]{3,2,1,0:T(8,128)(2,1)S(1)}, u32[]{:S(2)}, u32[]{:S(2)}) collective-permute-start(bf16[1,2,128,256]{3,2,1,0:T(8,128)(2,1)} %shard_map.64), channel_id=1, source_target_pairs={{0,6},{1,7},{2,4},{3,5},{4,2},{5,3},{6,0},{7,1},{8,14},{9,15},{10,... | collective-permute-start | bytes 393224 | tf_op jit(solution)/shard_map/ppermute | solution.py:33
  9.6 8.4 %collective-permute-start.1 = (bf16[1,2,64,512]{3,2,1,0:T(8,128)(2,1)S(1)}, bf16[1,2,64,512]{3,2,1,0:T(8,128)(2,1)S(1)}, u32[]{:S(2)}, u32[]{:S(2)}) collective-permute-start(bf16[1,2,64,512]{3,2,1,0:T(8,128)(2,1)S(1)} %collective-permute-done.refs_1_), channel_id=1, source_target_pairs={{0,2},{1,3},{2,0},{3,1},{4,6},{5,7},{6,4},{7,5},{8,10},{9,11},{10,... | collective-permute-start | bytes 393224 | tf_op jit(solution)/shard_map/ppermute | solution.py:33
  14.2 6.3 %collective-permute-start.6 = (bf16[1,2,64,512]{3,2,1,0:T(8,128)(2,1)S(1)}, bf16[1,2,64,512]{3,2,1,0:T(8,128)(2,1)S(1)}, u32[]{:S(2)}, u32[]{:S(2)}) collective-permute-start(bf16[1,2,64,512]{3,2,1,0:T(8,128)(2,1)S(1)} %collective-permute-done.3.refs_2_), channel_id=1, source_target_pairs={{0,1},{1,0},{2,3},{3,2},{4,5},{5,4},{6,7},{7,6},{8,9},{9,8},{10,11... | collective-permute-start | bytes 393224 | tf_op jit(solution)/shard_map/ppermute | solution.py:33
  15.5 5.2 %collective-permute-start.5 = (bf16[1,2,64,512]{3,2,1,0:T(8,128)(2,1)S(1)}, bf16[1,2,64,512]{3,2,1,0:T(8,128)(2,1)S(1)}, u32[]{:S(2)}, u32[]{:S(2)}) collective-permute-start(bf16[1,2,64,512]{3,2,1,0:T(8,128)(2,1)S(1)} %collective-permute-done.refs_1_), channel_id=1, source_target_pairs={{0,1},{1,0},{2,3},{3,2},{4,5},{5,4},{6,7},{7,6},{8,9},{9,8},{10,11... | collective-permute-start | bytes 393224 | tf_op jit(solution)/shard_map/ppermute | solution.py:33
  16.2 1.8 %copy-start.5 = (bf16[1,2,128,256]{3,2,1,0:T(8,128)(2,1)S(1)}, bf16[1,2,128,256]{3,2,1,0:T(8,128)(2,1)}, u32[]{:S(2)}) copy-start(bf16[1,2,128,256]{3,2,1,0:T(8,128)(2,1)} %shard_map.64) | copy-start | bytes 393220
  16.2 4.5 %copy-start.1 = (bf16[1,2,64,512]{3,2,1,0:T(8,128)(2,1)S(1)}, bf16[1,2,64,512]{3,2,1,0:T(8,128)(2,1)}, u32[]{:S(2)}) copy-start(bf16[1,2,64,512]{3,2,1,0:T(8,128)(2,1)} %refs_0_.1) | copy-start | bytes 393220
  18.0 5.9 %copy-start.3 = (s32[1,8,4]{1,2,0:T(4,128)S(1)}, s32[1,8,4]{1,2,0:T(4,128)}, u32[]{:S(2)}) copy-start(s32[1,8,4]{1,2,0:T(4,128)} %param.9) | copy-start | bytes 388
  18.1 5.0 %collective-permute-start.8 = (bf16[1,2,128,256]{3,2,1,0:T(8,128)(2,1)S(1)}, bf16[1,2,128,256]{3,2,1,0:T(8,128)(2,1)S(1)}, u32[]{:S(2)}, u32[]{:S(2)}) collective-permute-start(bf16[1,2,128,256]{3,2,1,0:T(8,128)(2,1)S(1)} %add.28), channel_id=1, source_target_pairs={{0,2},{1,3},{2,0},{3,1},{4,6},{5,7},{6,4},{7,5},{8,10},{9,11},{10,... | collective-permute-start | bytes 393224 | tf_op jit(solution)/shard_map/ppermute | solution.py:33
  19.0 5.0 %collective-permute-start.7 = (bf16[1,2,64,512]{3,2,1,0:T(8,128)(2,1)S(1)}, bf16[1,2,64,512]{3,2,1,0:T(8,128)(2,1)S(1)}, u32[]{:S(2)}, u32[]{:S(2)}) collective-permute-start(bf16[1,2,64,512]{3,2,1,0:T(8,128)(2,1)S(1)} %collective-permute-done.1.refs_0_), channel_id=1, source_target_pairs={{0,1},{1,0},{2,3},{3,2},{4,5},{5,4},{6,7},{7,6},{8,9},{9,8},{10,11... | collective-permute-start | bytes 393224 | tf_op jit(solution)/shard_map/ppermute | solution.py:33
  26.0 14.8 %copy-start.2 = (s32[3]{0:T(128)S(1)}, s32[3]{0:T(128)}, u32[]{:S(2)}) copy-start(s32[3]{0:T(128)} %owner_ref.3) | copy-start | bytes 40
  26.0 1.6 %collective-permute-start.9 = (f32[2,256,128]{2,1,0:T(8,128)S(1)}, f32[2,256,128]{2,1,0:T(8,128)S(1)}, u32[]{:S(2)}, u32[]{:S(2)}) collective-permute-start(f32[2,256,128]{2,1,0:T(8,128)S(1)} %get-tuple-element.25), channel_id=1, source_target_pairs={{0,8},{8,0},{16,24},{24,16},{1,9},{9,1},{17,25},{25,17},{2,10},{10... | collective-permute-start | bytes 786440 | tf_op jit(solution)/shard_map/ppermute | solution.py:33
  28.3 4.6 %collective-permute-start.10 = (bf16[2,1024,128]{2,1,0:T(8,128)(2,1)S(1)}, bf16[2,1024,128]{2,1,0:T(8,128)(2,1)S(1)}, u32[]{:S(2)}, u32[]{:S(2)}) collective-permute-start(bf16[2,1024,128]{2,1,0:T(8,128)(2,1)S(1)} %get-tuple-element.28), channel_id=1, source_target_pairs={{0,8},{8,0},{16,24},{24,16},{1,9},{9,1},{17,25},{25,17},{2,10},{10... | collective-permute-start | bytes 1572872 | tf_op jit(solution)/shard_map/ppermute | solution.py:33
  28.4 12.4 %all-to-all-start = ((bf16[16,32,128]{2,1,0:T(8,128)(2,1)}), bf16[16,32,128]{2,1,0:T(8,128)(2,1)S(1)}, u32[]{:S(2)}, u32[]{:S(2)}) async-start(bf16[16,32,128]{2,1,0:T(8,128)(2,1)} %bitcast.2), calls=%async_computation | async-start | bytes 262144 | tf_op jit(solution)/shard_map/all_to_all | solution.py:353
  32.9 1.0 %copy-start.4 = (f32[2,1024,128]{2,1,0:T(8,128)}, f32[2,1024,128]{2,1,0:T(8,128)S(1)}, u32[]{:S(2)}) copy-start(f32[2,1024,128]{2,1,0:T(8,128)S(1)} %convert_add_fusion) | copy-start | bytes 3145732
  33.9 20.0 %copy-start = (bf16[3,1024,256]{2,1,0:T(8,128)(2,1)S(1)}, bf16[3,1024,256]{2,1,0:T(8,128)(2,1)}, u32[]{:S(2)}) copy-start(bf16[3,1024,256]{2,1,0:T(8,128)(2,1)} %sep_ref.3) | copy-start | bytes 4718596
  42.0 11.8 %all-to-all-start.1 = ((bf16[8,3,32,128]{3,2,1,0:T(8,128)(2,1)}), bf16[8,3,32,128]{3,2,1,0:T(8,128)(2,1)S(1)}, u32[]{:S(2)}, u32[]{:S(2)}) async-start(bf16[8,3,32,128]{3,2,1,0:T(8,128)(2,1)} %shard_map.68), calls=%async_computation.1 | async-start | bytes 393216 | tf_op jit(solution)/shard_map/all_to_all | solution.py:370
  45.4 6.2 %collective-permute-start.12 = (bf16[1,2,128,256]{3,2,1,0:T(8,128)(2,1)S(1)}, bf16[1,2,128,256]{3,2,1,0:T(8,128)(2,1)S(1)}, u32[]{:S(2)}, u32[]{:S(2)}) collective-permute-start(bf16[1,2,128,256]{3,2,1,0:T(8,128)(2,1)S(1)} %add.29), channel_id=1, source_target_pairs={{0,1},{1,0},{2,3},{3,2},{4,5},{5,4},{6,7},{7,6},{8,9},{9,8},{10,11... | collective-permute-start | bytes 393224 | tf_op jit(solution)/shard_map/ppermute | solution.py:33
  47.4 6.5 %collective-permute-start.11 = (bf16[1,1024,128]{2,1,0:T(8,128)(2,1)S(1)}, bf16[1,1024,128]{2,1,0:T(8,128)(2,1)S(1)}, u32[]{:S(2)}, u32[]{:S(2)}) collective-permute-start(bf16[1,1024,128]{2,1,0:T(8,128)(2,1)S(1)} %dynamic-slice_convert_fusion.refs_0_), channel_id=1, source_target_pairs={{0,16},{8,24},{16,0},{24,8},{1,17},{9,25},{17,1},{25,9},{2,18},{10... | collective-permute-start | bytes 786440 | tf_op jit(solution)/shard_map/ppermute | solution.py:33
  51.7 1.4 %collective-permute-start.13 = (bf16[1,2,128,256]{3,2,1,0:T(8,128)(2,1)S(1)}, bf16[1,2,128,256]{3,2,1,0:T(8,128)(2,1)S(1)}, u32[]{:S(2)}, u32[]{:S(2)}) collective-permute-start(bf16[1,2,128,256]{3,2,1,0:T(8,128)(2,1)S(1)} %add.35.refs_0_), channel_id=1, source_target_pairs={{0,8},{8,0},{16,24},{24,16},{1,9},{9,1},{17,25},{25,17},{2,10},{10... | collective-permute-start | bytes 393224 | tf_op jit(solution)/shard_map/ppermute | solution.py:33

commit v8 on v6

--- a/solution.py
+++ b/solution.py
@@ -1,3 +1,5 @@
+import functools
+
 import jax
 import jax.numpy as jnp
 from jax import lax
@@ -152,7 +154,7 @@
     )(masked, *pieces.values())
 
 
-def layer_copy(begun, masked, pieces, order, copy_fill):
+def layer_copy(begun, masked, pieces, order, grids, copy_fill):
     rows, columns = begun.shape
     panels, share = next(iter(pieces.values())).shape[1:3]
     layers = lax.axis_size("layer")
@@ -163,8 +165,9 @@
 
     def body(fill_ref, begun_ref, l_ref, *refs):
         u_refs = refs[: len(pieces)]
-        keep_ref, send_ref, top_ref, u_all, sums, fills, sems = refs[len(pieces) :]
-        core = lax.rem(lax.axis_index("layer"), 2)
+        keep_refs, send_refs = refs[len(pieces) :][: layers // 2], refs[len(pieces) :][layers // 2 : layers]
+        top_ref, top_send_ref, u_all, sums, fills, sems = refs[len(pieces) + layers :]
+        pair, core = lax.axis_index("layer") // 2, lax.rem(lax.axis_index("layer"), 2)
         copies = load_panels(
             u_refs, list(pieces), order[-(depth // panels // BLOCK) :], u_all, sems, lax.axis_index("grid")
         )
@@ -188,20 +191,19 @@
             sums[slot] = begun_ref[here, :] + jnp.dot(
                 l_ref[here, done:], u_all[...], preferred_element_type=jnp.float32
             )
+            if r < WS:
+                for i in range(layers // 2):
+                    top_ref[i, here, :] = filled(slot, 2 * i + core, r, step)
+                    top_send_ref[i, here, :] = filled(slot, 2 * i + 1 - core, r, step)
             for i in range(layers // 2):
-                keep_ref[i, here, :] = filled(slot, 2 * i + core, r, step)
-                other = filled(slot, 2 * i + 1 - core, r, step)
-                send_ref[i, here, :] = other.astype(jnp.bfloat16)
-                if r < WS:
-                    top_ref[i, here, :] = other
-
-    return kernel_call(
-        body,
-        (
-            jax.ShapeDtypeStruct((layers // 2, rows, width), jnp.float32),
-            jax.ShapeDtypeStruct((layers // 2, rows, width), jnp.bfloat16),
-            jax.ShapeDtypeStruct((layers // 2, WS, width), jnp.float32),
-        ),
+                keep_refs[i][here, :] = filled(slot, 2 * (pair ^ i) + core, r, step)
+                send_refs[i][here, :] = filled(slot, 2 * (pair ^ i) + 1 - core, r, step).astype(jnp.bfloat16)
+
+    *blocks, top, top_send = kernel_call(
+        body,
+        [jax.ShapeDtypeStruct((rows, width), jnp.float32)] * (layers // 2)
+        + [jax.ShapeDtypeStruct((rows, width), jnp.bfloat16)] * (layers // 2)
+        + [jax.ShapeDtypeStruct((layers // 2, WS, width), jnp.float32)] * 2,
         [SMEM, VMEM, VMEM] + [HBM] * len(pieces),
         scratch=[
             pltpu.VMEM((depth, columns), jnp.bfloat16),
@@ -212,6 +214,7 @@
         flops=2 * rows * depth * columns,
         nbytes=2 * rows * depth + 2 * depth * columns + 8 * rows * columns,
     )(copy_fill, begun, masked, *pieces.values())
+    return blocks[: layers // 2], blocks[layers // 2 :], top, top_send
 
 
 def tree(layers):
@@ -249,17 +252,18 @@
     )(sep_owner, candidates, *after)
 
 
-def eliminate(own, other, pivots, below, sep_panels):
-    rows, width = own.shape
+def eliminate(parts, pivots, below, sep_panels):
+    rows, width = parts[0].shape
     grids, count, piece_rows, _ = pivots.shape
     nodes = tree(count + 1)
     inner = [n for n in nodes if n[3]]
     _, wide, part, _ = below[0].shape
     step = min(rows, 256)
 
-    def body(own_ref, other_ref, p_ref, sep_ref, *refs):
-        below_refs = refs[: len(below)]
-        out_ref, all_p, all_below, result, sems = refs[len(below) :]
+    def body(p_ref, sep_ref, *refs):
+        below_refs, refs = refs[: len(below)], refs[len(below) :]
+        part_refs, refs = refs[: len(parts)], refs[len(parts) :]
+        out_ref, all_p, all_below, result, sems = refs
         core = lax.rem(lax.axis_index("layer"), 2)
         for k, ref in enumerate(below_refs):
             at = pl.multiple_of((core ^ k) * part, part)
@@ -281,7 +285,7 @@
         copies = []
         for r in range(0, rows, step):
             here = slice(r, r + step)
-            total = own_ref[here, :] + other_ref[here, :].astype(jnp.float32)
+            total = functools.reduce(jnp.add, [ref[here, :].astype(jnp.float32) for ref in part_refs])
             for node in range(count):
                 total = total - jnp.dot(
                     sep_ref[node, here, :], all_p[node * WS : (node + 1) * WS, :], preferred_element_type=jnp.float32
@@ -295,7 +299,7 @@
     return kernel_call(
         body,
         jax.ShapeDtypeStruct((rows, width), jnp.float32),
-        [VMEM] * (4 + len(below)),
+        [VMEM] * (2 + len(below) + len(parts)),
         scratch=[
             pltpu.VMEM((count * WS, width), jnp.bfloat16),
             pltpu.VMEM((len(inner), wide, WS, WS), jnp.bfloat16),
@@ -305,7 +309,7 @@
         out_specs=HBM,
         flops=2 * rows * count * WS * width,
         nbytes=10 * rows * width + 2 * sep_panels.size,
-    )(own, other, pivots, sep_panels, *below)
+    )(pivots, sep_panels, *below, *parts)
 
 
 def local(l_panels, u_panels, panel_fill, copy_fill, sep_panels, sep_owner):
@@ -341,31 +345,29 @@
     early = {k: piece for k, piece in pieces.items() if k * piece.shape[2] // BLOCK in order[:half]}
     late = {k: piece for k, piece in pieces.items() if k not in early}
     begun = first_part(masked, early, order)
-    keep, send, top = layer_copy(begun, masked, late, order, jnp.swapaxes(copy_fill, 1, 2))
-    candidates = (keep[:, :WS] + apart(top, "layer", 1)).astype(jnp.bfloat16)
+    keep, send, top, top_send = layer_copy(begun, masked, late, order, grids, jnp.swapaxes(copy_fill, 1, 2))
+    candidates = (top + apart(top_send, "layer", 1)).astype(jnp.bfloat16)
+    candidates, below, *send = together(candidates, below, *send)
     candidates = candidates.reshape((layers // 2 * grids, WS // grids) + candidates.shape[2:])
     alike = [[i * grids + g for i in range(core, layers, 2) for g in range(grids)] for core in (0, 1)]
-    candidates, send, below = together(candidates, send, below)
     candidates = lax.all_to_all(candidates, BOTH, 0, 0, axis_index_groups=alike)
     candidates = candidates.reshape((layers // 2, grids) + candidates.shape[1:])
 
     below = [below + apart(below, "grid", hops[-1])]
     below.append(apart(below[0], "layer", 1))
-    other = apart(send, "layer", 1)
+    parts = [[kept, apart(sent, "layer", 1)] for kept, sent in zip(keep, send)]
     pivots = None
-    bit = 1
-    while keep.shape[0] > 1:
-        bit *= 2
-        half = keep.shape[0] // 2
-        total = keep + other.astype(jnp.float32)
-        total = total.reshape((half, 2) + total.shape[1:])
-        side = (layer // bit) % 2
-        keep = lax.dynamic_index_in_dim(total, side, 1, keepdims=False)
-        send = lax.dynamic_index_in_dim(total, 1 - side, 1, keepdims=False).astype(jnp.bfloat16)
+    while len(parts) > 1:
+        half = len(parts) // 2
+        sums = [functools.reduce(jnp.add, [x.astype(jnp.float32) for x in part]) for part in parts[half:]]
+        sums = [x.astype(jnp.bfloat16) for x in sums]
         if pivots is None:
-            pivots = lax.all_to_all(pick_pivots(candidates, sep_owner, grids, [send]), "grid", 0, 0)
-        other = apart(send, "layer", bit)
-    return eliminate(keep[0], other[0], pivots, below, sep_panels)
+            parts[0] = [functools.reduce(jnp.add, [x.astype(jnp.float32) for x in parts[0]])]
+            pivots = lax.all_to_all(
+                pick_pivots(candidates, sep_owner, grids, [sums[0], parts[0][0]]), "grid", 0, 0
+            )
+        parts = [part + [apart(x, "layer", 2 * half)] for part, x in zip(parts, sums)]
+    return eliminate(parts[0], pivots, below, sep_panels)
 
 
 def solution(mesh):

time: 55.7 us -> 56 us (level)
  waiting for transfers between devices: 17.5 us -> 13.1 us
  other arithmetic: 0.88 us -> 4.51 us
  starting transfers between devices: 24.4 us -> 27.1 us
  local copies, waits for them, and re-layouts: 2.11 us -> 0.72 us
    ppermute x14 -> x15, waiting for transfers between devices: 10.7 us -> 8.14 us  [apart(): lax.ppermute(x, axis, [(i, i ^ distance) for i in range(lax.axis_size(axi...]
    ppermute x14 -> x15, starting transfers between devices: 16.6 us -> 19.2 us  [apart(): lax.ppermute(x, axis, [(i, i ^ distance) for i in range(lax.axis_size(axi...]
    all_to_all x1, waiting for transfers between devices: 6.83 us -> 4.91 us  [local(): candidates = lax.all_to_all(candidates, BOTH, 0, 0, axis_index_groups=alike)]
    squeeze x1 -> x0, local copies, waits for them, and re-layouts: 1.08 us -> none  [local(): return eliminate(keep[0], other[0], pivots, below, sep_panels)]
    add x1, other arithmetic: 0.09 us -> 1.15 us  [local(): functools.reduce(jnp.add, [x.astype(jnp.float32) for x in parts[0]])]
    convert_element_type x1 -> x2, other arithmetic: 0.69 us -> 1.71 us  [the longest x1 1.02 us: local(): sums = [x.astype(jnp.bfloat16) for x in sums]]
    add x1, other arithmetic: 0.03 us -> 0.94 us  [local(): below = [below + apart(below, 'grid', hops[-1])]]
    add x1, other arithmetic: 0.03 us -> 0.68 us  [local(): below = below + apart(below, 'grid', hop)]
  transfers between devices with their start and end apart: 16 -> 17, of which waited for: 10 -> 8; matrix products, arithmetic and copies ran while one was open for 2% -> 7% of each run, Pallas kernels for 10% -> 10%
where the time goes in v8:
time: 56 us; the launch traced here: 55.6 us
  starting transfers between devices  27.1 us (48%)
  waiting for transfers between devices  13.1 us (23%)
  Pallas kernels  10.1 us (18%)
  other arithmetic  4.51 us (8%)
  local copies, waits for them, and re-layouts  0.72 us (1%)
    ppermute x15, starting transfers between devices, apart(): lax.ppermute(x, axis, [(i, i ^ distance) for i in range(lax.axis_size(axi...  19.2 us
    ppermute x15, waiting for transfers between devices, apart(): lax.ppermute(x, axis, [(i, i ^ distance) for i in range(lax.axis_size(axi...  8.14 us
    all_to_all x1, waiting for transfers between devices, local(): candidates = lax.all_to_all(candidates, BOTH, 0, 0, axis_index_groups=alike)  4.91 us
    all_to_all x1, starting transfers between devices, local(): candidates = lax.all_to_all(candidates, BOTH, 0, 0, axis_index_groups=alike)  4.54 us
    all_to_all x1, starting transfers between devices, local(): lax.all_to_all(pick_pivots(candidates, sep_owner, grids, [sums[0], parts[...  3.39 us
    pallas_call x1, Pallas kernels, first_part(): kernel_call(body, jax.ShapeDtypeStruct((rows, columns), jnp.float32), [VM...  2.13 us
    pallas_call x1, Pallas kernels, layer_copy(): kernel_call(body, [jax.ShapeDtypeStruct((rows, width), jnp.float32)] * (l...  1.88 us
    pallas_call x1, Pallas kernels, mask_panels(): kernel_call(body, jax.ShapeDtypeStruct((rows, panels * width), jnp.bfloat...  1.79 us
  transfers between devices with their start and end apart: 17, of which 8 were waited for; matrix products, arithmetic and copies ran while one was open for 7% of the time, Pallas kernels for 10%

profile of v8, /device:TPU:0, one launch (start us, length us, event | category | flops | bytes accessed | tf_op | source)
XLA Modules:
  0.0 55.6 jit_solution(18371895916533036235)
XLA Ops:
  0.0 5.0 %collective-permute-start = (bf16[1,2,64,512]{3,2,1,0:T(8,128)(2,1)}, bf16[1,2,64,512]{3,2,1,0:T(8,128)(2,1)S(1)}, u32[]{:S(2)}, u32[]{:S(2)}) collective-permute-start(bf16[1,2,64,512]{3,2,1,0:T(8,128)(2,1)} %refs_0_.1), channel_id=1, source_target_pairs={{0,6},{1,7},{2,4},{3,5},{4,2},{5,3},{6,0},{7,1},{8,14},{9,15},{10,... | collective-permute-start | bytes 393224 | tf_op jit(solution)/shard_map/ppermute | solution.py:35
  5.0 0.0 collective-permute-start.3
  5.1 1.5 %collective-permute-start.4 = (bf16[1,2,64,512]{3,2,1,0:T(8,128)(2,1)}, bf16[1,2,64,512]{3,2,1,0:T(8,128)(2,1)S(1)}, u32[]{:S(2)}, u32[]{:S(2)}) collective-permute-start(bf16[1,2,64,512]{3,2,1,0:T(8,128)(2,1)} %refs_0_.1), channel_id=1, source_target_pairs={{0,1},{1,0},{2,3},{3,2},{4,5},{5,4},{6,7},{7,6},{8,9},{9,8},{10,11... | collective-permute-start | bytes 393224 | tf_op jit(solution)/shard_map/ppermute | solution.py:35
  6.5 1.6 %shard_map.64 = bf16[1,2,128,256]{3,2,1,0:T(8,128)(2,1)} custom-call(s32[3]{0:T(128)} %owner_ref.3, bf16[3,1024,256]{2,1,0:T(8,128)(2,1)} %sep_ref.3), custom_call_target="tpu_custom_call" | custom-call | bytes 262144 | tf_op jit(solution)/shard_map/pallas_call | solution.py:66
  8.1 1.0 %collective-permute-start.2 = (bf16[1,2,128,256]{3,2,1,0:T(8,128)(2,1)}, bf16[1,2,128,256]{3,2,1,0:T(8,128)(2,1)S(1)}, u32[]{:S(2)}, u32[]{:S(2)}) collective-permute-start(bf16[1,2,128,256]{3,2,1,0:T(8,128)(2,1)} %shard_map.64), channel_id=1, source_target_pairs={{0,6},{1,7},{2,4},{3,5},{4,2},{5,3},{6,0},{7,1},{8,14},{9,15},{10,... | collective-permute-start | bytes 393224 | tf_op jit(solution)/shard_map/ppermute | solution.py:35
  9.1 0.5 collective-permute-done.refs_1_
  9.6 1.6 %collective-permute-start.1 = (bf16[1,2,64,512]{3,2,1,0:T(8,128)(2,1)S(1)}, bf16[1,2,64,512]{3,2,1,0:T(8,128)(2,1)S(1)}, u32[]{:S(2)}, u32[]{:S(2)}) collective-permute-start(bf16[1,2,64,512]{3,2,1,0:T(8,128)(2,1)S(1)} %collective-permute-done.refs_1_), channel_id=1, source_target_pairs={{0,2},{1,3},{2,0},{3,1},{4,6},{5,7},{6,4},{7,5},{8,10},{9,11},{10,... | collective-permute-start | bytes 393224 | tf_op jit(solution)/shard_map/ppermute | solution.py:35
  11.3 0.8 %collective-permute-done.3.refs_2_ = bf16[1,2,64,512]{3,2,1,0:T(8,128)(2,1)S(1)} collective-permute-done((bf16[1,2,64,512]{3,2,1,0:T(8,128)(2,1)}, bf16[1,2,64,512]{3,2,1,0:T(8,128)(2,1)S(1)}, u32[]{:S(2)}, u32[]{:S(2)}) %collective-permute-start.3) | collective-permute-done | bytes 131104 | tf_op jit(solution)/shard_map/ppermute | solution.py:35
  12.1 3.4 %collective-permute-start.5 = (bf16[1,2,64,512]{3,2,1,0:T(8,128)(2,1)S(1)}, bf16[1,2,64,512]{3,2,1,0:T(8,128)(2,1)S(1)}, u32[]{:S(2)}, u32[]{:S(2)}) collective-permute-start(bf16[1,2,64,512]{3,2,1,0:T(8,128)(2,1)S(1)} %collective-permute-done.refs_1_), channel_id=1, source_target_pairs={{0,1},{1,0},{2,3},{3,2},{4,5},{5,4},{6,7},{7,6},{8,9},{9,8},{10,11... | collective-permute-start | bytes 393224 | tf_op jit(solution)/shard_map/ppermute | solution.py:35
  15.5 0.0 collective-permute-start.6
  15.6 1.8 %shard_map.65.l_ref = bf16[1024,1024]{1,0:T(8,128)(2,1)S(1)} custom-call(s32[1,2,4,8]{3,2,1,0:T(4,128)} %bitcast.6, bf16[1,2,1024,512]{3,2,1,0:T(8,128)(2,1)} %l_ref.1), custom_call_target="tpu_custom_call" | custom-call | bytes 4194304 | tf_op jit(solution)/shard_map/pallas_call | solution.py:107
  17.3 0.0 collective-permute-done.2
  17.4 0.0 copy-start.3
  17.4 0.0 collective-permute-done.1.refs_0_
  17.4 1.5 %collective-permute-start.8 = (bf16[1,2,128,256]{3,2,1,0:T(8,128)(2,1)S(1)}, bf16[1,2,128,256]{3,2,1,0:T(8,128)(2,1)S(1)}, u32[]{:S(2)}, u32[]{:S(2)}) collective-permute-start(bf16[1,2,128,256]{3,2,1,0:T(8,128)(2,1)S(1)} %add.18), channel_id=1, source_target_pairs={{0,2},{1,3},{2,0},{3,1},{4,6},{5,7},{6,4},{7,5},{8,10},{9,11},{10,... | collective-permute-start | bytes 393224 | tf_op jit(solution)/shard_map/ppermute | solution.py:35
  19.0 1.5 %collective-permute-start.7 = (bf16[1,2,64,512]{3,2,1,0:T(8,128)(2,1)S(1)}, bf16[1,2,64,512]{3,2,1,0:T(8,128)(2,1)S(1)}, u32[]{:S(2)}, u32[]{:S(2)}) collective-permute-start(bf16[1,2,64,512]{3,2,1,0:T(8,128)(2,1)S(1)} %collective-permute-done.1.refs_0_), channel_id=1, source_target_pairs={{0,1},{1,0},{2,3},{3,2},{4,5},{5,4},{6,7},{7,6},{8,9},{9,8},{10,11... | collective-permute-start | bytes 393224 | tf_op jit(solution)/shard_map/ppermute | solution.py:35
  20.5 0.0 collective-permute-done.5.refs_4_
  20.5 0.2 collective-permute-done.6.refs_5_
  20.7 2.1 %shard_map.66.begun_ref = f32[1024,512]{1,0:T(8,128)S(1)} custom-call(bf16[1024,1024]{1,0:T(8,128)(2,1)S(1)} %shard_map.65.l_ref, bf16[1,2,64,512]{3,2,1,0:T(8,128)(2,1)S(1)} %copy-done.1, bf16[1,2,64,512]{3,2,1,0:T(8,128)(2,1)S(1)} %collective-permute-done.refs_1_, bf16[1,2,64,512]{3,2,1,0:T(8,128)(2,1)S(1)} %collective-permute-done.3.refs_2_, ...), custom_call_target="tpu_custom_call" | custom-call | flops 805306368 | bytes 4456448 | tf_op jit(solution)/shard_map/pallas_call | solution.py:147
  22.8 0.0 collective-permute-done.8
  22.8 0.7 %add.19 = bf16[1,2,128,256]{3,2,1,0:T(8,128)(2,1)} add(bf16[1,2,128,256]{3,2,1,0:T(8,128)(2,1)S(1)} %add.18, bf16[1,2,128,256]{3,2,1,0:T(8,128)(2,1)S(1)} %collective-permute-done.8) | non-fusion elementwise | flops 65536 | bytes 393216 | tf_op jit(solution)/shard_map/add | solution.py:340
  23.5 0.5 collective-permute-done.7.refs_1_
  23.9 1.9 %shard_map.67 = (f32[1024,128]{1,0:T(8,128)S(1)}, f32[1024,128]{1,0:T(8,128)S(1)}, bf16[1024,128]{1,0:T(8,128)(2,1)S(1)}, bf16[1024,128]{1,0:T(8,128)(2,1)S(1)},...) custom-call(s32[1,4,8]{2,1,0:T(4,128)S(1)} %bitcast.5, f32[1024,512]{1,0:T(8,128)S(1)} %shard_map.66.begun_ref, ...), custom_call_target="tpu_custom_call" | custom-call | flops 268435456 | bytes 4980736 | tf_op jit(solution)/shard_map/pallas_call | solution.py:202
  25.8 0.0 copy-start.2
  25.8 0.1 collective-permute-start.9
  25.9 1.5 %collective-permute-done.9 = f32[2,256,128]{2,1,0:T(8,128)S(1)} collective-permute-done((f32[2,256,128]{2,1,0:T(8,128)S(1)}, f32[2,256,128]{2,1,0:T(8,128)S(1)}, u32[]{:S(2)}, u32[]{:S(2)}) %collective-permute-start.9) | collective-permute-done | bytes 262176 | tf_op jit(solution)/shard_map/ppermute | solution.py:35
  27.4 0.7 %add_convert_fusion.1 = bf16[2,256,128]{2,1,0:T(8,128)(2,1)} fusion(f32[2,256,128]{2,1,0:T(8,128)S(1)} %get-tuple-element.26, f32[2,256,128]{2,1,0:T(8,128)S(1)} %collective-permute-done.9), kind=kLoop, calls=%fused_computation.2 | loop fusion | flops 131072 | bytes 655360 | tf_op jit(solution)/shard_map/convert_element_type | solution.py:349
  28.1 0.1 collective-permute-start.11
  28.3 0.4 collective-permute-start.10
  28.6 4.5 %all-to-all-start = ((bf16[16,32,128]{2,1,0:T(8,128)(2,1)}), bf16[16,32,128]{2,1,0:T(8,128)(2,1)S(1)}, u32[]{:S(2)}, u32[]{:S(2)}) async-start(bf16[16,32,128]{2,1,0:T(8,128)(2,1)} %bitcast.2), calls=%async_computation | async-start | bytes 262144 | tf_op jit(solution)/shard_map/all_to_all | solution.py:353
  33.2 0.0 collective-permute-done.11
  33.2 0.0 copy-start.5
  33.2 0.7 %copy-done.5 = bf16[1024,128]{1,0:T(8,128)(2,1)} copy-done((bf16[1024,128]{1,0:T(8,128)(2,1)}, bf16[1024,128]{1,0:T(8,128)(2,1)S(1)}, u32[]{:S(2)}) %copy-start.5) | copy-done | bytes 262168
  33.9 1.1 %convert_add_fusion.refs_1_.refs_2_ = f32[1024,128]{1,0:T(8,128)S(1)} fusion(f32[1024,128]{1,0:T(8,128)S(1)} %get-tuple-element.34, bf16[1024,128]{1,0:T(8,128)(2,1)} %copy-done.5), kind=kLoop, calls=%fused_computation | loop fusion | flops 262144 | bytes 1310720 | tf_op jit(solution)/shard_map/add | solution.py:365
  35.1 0.0 collective-permute-done.10
  35.1 1.0 %add_convert_fusion.refs_0_ = bf16[1024,128]{1,0:T(8,128)(2,1)S(1)} fusion(f32[1024,128]{1,0:T(8,128)S(1)} %get-tuple-element.32, bf16[1024,128]{1,0:T(8,128)(2,1)} %collective-permute-done.10), kind=kLoop, calls=%fused_computation.1 | loop fusion | flops 393216 | bytes 1048576 | tf_op jit(solution)/shard_map/convert_element_type | solution.py:363
  36.1 4.9 %all-to-all-done = bf16[16,32,128]{2,1,0:T(8,128)(2,1)S(1)} async-done(((bf16[16,32,128]{2,1,0:T(8,128)(2,1)}), bf16[16,32,128]{2,1,0:T(8,128)(2,1)S(1)}, u32[]{:S(2)}, u32[]{:S(2)}) %all-to-all-start) | async-done | bytes 131104 | tf_op jit(solution)/shard_map/all_to_all | solution.py:353
  41.0 1.2 %shard_map.68 = bf16[8,3,32,128]{3,2,1,0:T(8,128)(2,1)} custom-call(s32[3]{0:T(128)S(1)} %copy-done.2, bf16[2,8,32,128]{3,2,1,0:T(8,128)(2,1)S(1)} %bitcast.4, bf16[1024,128]{1,0:T(8,128)(2,1)S(1)} %add_convert_fusion.refs_0_, f32[1024,128]{1,0:T(8,128)S(1)} %convert_add_fusion.refs_1_.refs_2_), custom_call_target="tpu_custom_call" | custom-call | bytes 262144 | tf_op jit(solution)/shard_map/pallas_call | solution.py:247
  42.2 3.4 %all-to-all-start.1 = ((bf16[8,3,32,128]{3,2,1,0:T(8,128)(2,1)}), bf16[8,3,32,128]{3,2,1,0:T(8,128)(2,1)S(1)}, u32[]{:S(2)}, u32[]{:S(2)}) async-start(bf16[8,3,32,128]{3,2,1,0:T(8,128)(2,1)} %shard_map.68), calls=%async_computation.1 | async-start | bytes 393216 | tf_op jit(solution)/shard_map/all_to_all | solution.py:366
  45.6 1.9 %collective-permute-start.12 = (bf16[1,2,128,256]{3,2,1,0:T(8,128)(2,1)}, bf16[1,2,128,256]{3,2,1,0:T(8,128)(2,1)S(1)}, u32[]{:S(2)}, u32[]{:S(2)}) collective-permute-start(bf16[1,2,128,256]{3,2,1,0:T(8,128)(2,1)} %add.19), channel_id=1, source_target_pairs={{0,1},{1,0},{2,3},{3,2},{4,5},{5,4},{6,7},{7,6},{8,9},{9,8},{10,11... | collective-permute-start | bytes 393224 | tf_op jit(solution)/shard_map/ppermute | solution.py:35
  47.6 0.9 %collective-permute-start.14 = (bf16[1024,128]{1,0:T(8,128)(2,1)S(1)}, bf16[1024,128]{1,0:T(8,128)(2,1)S(1)}, u32[]{:S(2)}, u32[]{:S(2)}) collective-permute-start(bf16[1024,128]{1,0:T(8,128)(2,1)S(1)} %add_convert_fusion.refs_0_), channel_id=1, source_target_pairs={{0,16},{8,24},{16,0},{24,8},{1,17},{9,25},{17,1},{25,9},{2,18},{10... | collective-permute-start | bytes 786440 | tf_op jit(solution)/shard_map/ppermute | solution.py:35
  48.5 3.3 %collective-permute-done.12 = bf16[1,2,128,256]{3,2,1,0:T(8,128)(2,1)S(1)} collective-permute-done((bf16[1,2,128,256]{3,2,1,0:T(8,128)(2,1)}, bf16[1,2,128,256]{3,2,1,0:T(8,128)(2,1)S(1)}, u32[]{:S(2)}, u32[]{:S(2)}) %collective-permute-start.12) | collective-permute-done | bytes 131104 | tf_op jit(solution)/shard_map/ppermute | solution.py:35
  51.8 0.9 %add.23.refs_0_ = bf16[1,2,128,256]{3,2,1,0:T(8,128)(2,1)S(1)} add(bf16[1,2,128,256]{3,2,1,0:T(8,128)(2,1)} %add.19, bf16[1,2,128,256]{3,2,1,0:T(8,128)(2,1)S(1)} %collective-permute-done.12) | non-fusion elementwise | flops 65536 | bytes 393216 | tf_op jit(solution)/shard_map/add | solution.py:356
  52.7 0.1 collective-permute-start.13
  52.8 1.3 %collective-permute-done.13.refs_1_ = bf16[1,2,128,256]{3,2,1,0:T(8,128)(2,1)S(1)} collective-permute-done((bf16[1,2,128,256]{3,2,1,0:T(8,128)(2,1)S(1)}, bf16[1,2,128,256]{3,2,1,0:T(8,128)(2,1)S(1)}, u32[]{:S(2)}, u32[]{:S(2)}) %collective-permute-start.13) | collective-permute-done | bytes 131104 | tf_op jit(solution)/shard_map/ppermute | solution.py:35
  54.2 0.0 collective-permute-done.14.refs_3_
  54.2 0.0 all-to-all-done.1.p_ref
  54.2 1.4 %shard_map.69 = f32[1024,128]{1,0:T(8,128)} custom-call(bf16[8,3,32,128]{3,2,1,0:T(8,128)(2,1)S(1)} %all-to-all-done.1.p_ref, bf16[3,1024,256]{2,1,0:T(8,128)(2,1)S(1)} %copy-done, bf16[1,2,128,256]{3,2,1,0:T(8,128)(2,1)S(1)} %add.23.refs_0_, bf16[1,2,128,256]{3,2,1,0:T(8,128)(2,1)S(1)} %collective-permute-done.13.refs_1_, ...), custom_call_target="tpu_custom_call" | custom-call | flops 201326592 | bytes 2883584 | tf_op jit(solution)/shard_map/pallas_call | solution.py:299
  (10 shorter events, 0.1 us)
Async XLA Ops:
  0.0 9.6 %collective-permute-start = (bf16[1,2,64,512]{3,2,1,0:T(8,128)(2,1)}, bf16[1,2,64,512]{3,2,1,0:T(8,128)(2,1)S(1)}, u32[]{:S(2)}, u32[]{:S(2)}) collective-permute-start(bf16[1,2,64,512]{3,2,1,0:T(8,128)(2,1)} %refs_0_.1), channel_id=1, source_target_pairs={{0,6},{1,7},{2,4},{3,5},{4,2},{5,3},{6,0},{7,1},{8,14},{9,15},{10,... | collective-permute-start | bytes 393224 | tf_op jit(solution)/shard_map/ppermute | solution.py:35
  5.0 7.0 %collective-permute-start.3 = (bf16[1,2,64,512]{3,2,1,0:T(8,128)(2,1)}, bf16[1,2,64,512]{3,2,1,0:T(8,128)(2,1)S(1)}, u32[]{:S(2)}, u32[]{:S(2)}) collective-permute-start(bf16[1,2,64,512]{3,2,1,0:T(8,128)(2,1)} %refs_0_.1), channel_id=1, source_target_pairs={{0,2},{1,3},{2,0},{3,1},{4,6},{5,7},{6,4},{7,5},{8,10},{9,11},{10,... | collective-permute-start | bytes 393224 | tf_op jit(solution)/shard_map/ppermute | solution.py:35
  5.1 7.0 %collective-permute-start.4 = (bf16[1,2,64,512]{3,2,1,0:T(8,128)(2,1)}, bf16[1,2,64,512]{3,2,1,0:T(8,128)(2,1)S(1)}, u32[]{:S(2)}, u32[]{:S(2)}) collective-permute-start(bf16[1,2,64,512]{3,2,1,0:T(8,128)(2,1)} %refs_0_.1), channel_id=1, source_target_pairs={{0,1},{1,0},{2,3},{3,2},{4,5},{5,4},{6,7},{7,6},{8,9},{9,8},{10,11... | collective-permute-start | bytes 393224 | tf_op jit(solution)/shard_map/ppermute | solution.py:35
  8.1 9.2 %collective-permute-start.2 = (bf16[1,2,128,256]{3,2,1,0:T(8,128)(2,1)}, bf16[1,2,128,256]{3,2,1,0:T(8,128)(2,1)S(1)}, u32[]{:S(2)}, u32[]{:S(2)}) collective-permute-start(bf16[1,2,128,256]{3,2,1,0:T(8,128)(2,1)} %shard_map.64), channel_id=1, source_target_pairs={{0,6},{1,7},{2,4},{3,5},{4,2},{5,3},{6,0},{7,1},{8,14},{9,15},{10,... | collective-permute-start | bytes 393224 | tf_op jit(solution)/shard_map/ppermute | solution.py:35
  9.6 7.8 %collective-permute-start.1 = (bf16[1,2,64,512]{3,2,1,0:T(8,128)(2,1)S(1)}, bf16[1,2,64,512]{3,2,1,0:T(8,128)(2,1)S(1)}, u32[]{:S(2)}, u32[]{:S(2)}) collective-permute-start(bf16[1,2,64,512]{3,2,1,0:T(8,128)(2,1)S(1)} %collective-permute-done.refs_1_), channel_id=1, source_target_pairs={{0,2},{1,3},{2,0},{3,1},{4,6},{5,7},{6,4},{7,5},{8,10},{9,11},{10,... | collective-permute-start | bytes 393224 | tf_op jit(solution)/shard_map/ppermute | solution.py:35
  12.1 8.4 %collective-permute-start.5 = (bf16[1,2,64,512]{3,2,1,0:T(8,128)(2,1)S(1)}, bf16[1,2,64,512]{3,2,1,0:T(8,128)(2,1)S(1)}, u32[]{:S(2)}, u32[]{:S(2)}) collective-permute-start(bf16[1,2,64,512]{3,2,1,0:T(8,128)(2,1)S(1)} %collective-permute-done.refs_1_), channel_id=1, source_target_pairs={{0,1},{1,0},{2,3},{3,2},{4,5},{5,4},{6,7},{7,6},{8,9},{9,8},{10,11... | collective-permute-start | bytes 393224 | tf_op jit(solution)/shard_map/ppermute | solution.py:35
  15.5 5.1 %collective-permute-start.6 = (bf16[1,2,64,512]{3,2,1,0:T(8,128)(2,1)S(1)}, bf16[1,2,64,512]{3,2,1,0:T(8,128)(2,1)S(1)}, u32[]{:S(2)}, u32[]{:S(2)}) collective-permute-start(bf16[1,2,64,512]{3,2,1,0:T(8,128)(2,1)S(1)} %collective-permute-done.3.refs_2_), channel_id=1, source_target_pairs={{0,1},{1,0},{2,3},{3,2},{4,5},{5,4},{6,7},{7,6},{8,9},{9,8},{10,11... | collective-permute-start | bytes 393224 | tf_op jit(solution)/shard_map/ppermute | solution.py:35
  15.5 1.8 %copy-start.4 = (bf16[1,2,128,256]{3,2,1,0:T(8,128)(2,1)S(1)}, bf16[1,2,128,256]{3,2,1,0:T(8,128)(2,1)}, u32[]{:S(2)}) copy-start(bf16[1,2,128,256]{3,2,1,0:T(8,128)(2,1)} %shard_map.64) | copy-start | bytes 393220
  15.6 5.1 %copy-start.1 = (bf16[1,2,64,512]{3,2,1,0:T(8,128)(2,1)S(1)}, bf16[1,2,64,512]{3,2,1,0:T(8,128)(2,1)}, u32[]{:S(2)}) copy-start(bf16[1,2,64,512]{3,2,1,0:T(8,128)(2,1)} %refs_0_.1) | copy-start | bytes 393220
  17.4 6.5 %copy-start.3 = (s32[1,8,4]{1,2,0:T(4,128)S(1)}, s32[1,8,4]{1,2,0:T(4,128)}, u32[]{:S(2)}) copy-start(s32[1,8,4]{1,2,0:T(4,128)} %param.9) | copy-start | bytes 388
  17.4 5.4 %collective-permute-start.8 = (bf16[1,2,128,256]{3,2,1,0:T(8,128)(2,1)S(1)}, bf16[1,2,128,256]{3,2,1,0:T(8,128)(2,1)S(1)}, u32[]{:S(2)}, u32[]{:S(2)}) collective-permute-start(bf16[1,2,128,256]{3,2,1,0:T(8,128)(2,1)S(1)} %add.18), channel_id=1, source_target_pairs={{0,2},{1,3},{2,0},{3,1},{4,6},{5,7},{6,4},{7,5},{8,10},{9,11},{10,... | collective-permute-start | bytes 393224 | tf_op jit(solution)/shard_map/ppermute | solution.py:35
  19.0 5.0 %collective-permute-start.7 = (bf16[1,2,64,512]{3,2,1,0:T(8,128)(2,1)S(1)}, bf16[1,2,64,512]{3,2,1,0:T(8,128)(2,1)S(1)}, u32[]{:S(2)}, u32[]{:S(2)}) collective-permute-start(bf16[1,2,64,512]{3,2,1,0:T(8,128)(2,1)S(1)} %collective-permute-done.1.refs_0_), channel_id=1, source_target_pairs={{0,1},{1,0},{2,3},{3,2},{4,5},{5,4},{6,7},{7,6},{8,9},{9,8},{10,11... | collective-permute-start | bytes 393224 | tf_op jit(solution)/shard_map/ppermute | solution.py:35
  25.8 15.2 %copy-start.2 = (s32[3]{0:T(128)S(1)}, s32[3]{0:T(128)}, u32[]{:S(2)}) copy-start(s32[3]{0:T(128)} %owner_ref.3) | copy-start | bytes 40
  25.8 1.6 %collective-permute-start.9 = (f32[2,256,128]{2,1,0:T(8,128)S(1)}, f32[2,256,128]{2,1,0:T(8,128)S(1)}, u32[]{:S(2)}, u32[]{:S(2)}) collective-permute-start(f32[2,256,128]{2,1,0:T(8,128)S(1)} %get-tuple-element.27), channel_id=1, source_target_pairs={{0,8},{8,0},{16,24},{24,16},{1,9},{9,1},{17,25},{25,17},{2,10},{10... | collective-permute-start | bytes 786440 | tf_op jit(solution)/shard_map/ppermute | solution.py:35
  28.1 5.1 %collective-permute-start.11 = (bf16[1024,128]{1,0:T(8,128)(2,1)S(1)}, bf16[1024,128]{1,0:T(8,128)(2,1)S(1)}, u32[]{:S(2)}, u32[]{:S(2)}) collective-permute-start(bf16[1024,128]{1,0:T(8,128)(2,1)S(1)} %get-tuple-element.35), channel_id=1, source_target_pairs={{0,8},{8,0},{16,24},{24,16},{1,9},{9,1},{17,25},{25,17},{2,10},{10... | collective-permute-start | bytes 786440 | tf_op jit(solution)/shard_map/ppermute | solution.py:35
  28.3 6.8 %collective-permute-start.10 = (bf16[1024,128]{1,0:T(8,128)(2,1)S(1)}, bf16[1024,128]{1,0:T(8,128)(2,1)}, u32[]{:S(2)}, u32[]{:S(2)}) collective-permute-start(bf16[1024,128]{1,0:T(8,128)(2,1)S(1)} %get-tuple-element.33), channel_id=1, source_target_pairs={{0,8},{8,0},{16,24},{24,16},{1,9},{9,1},{17,25},{25,17},{2,10},{10... | collective-permute-start | bytes 786440 | tf_op jit(solution)/shard_map/ppermute | solution.py:35
  28.6 12.3 %all-to-all-start = ((bf16[16,32,128]{2,1,0:T(8,128)(2,1)}), bf16[16,32,128]{2,1,0:T(8,128)(2,1)S(1)}, u32[]{:S(2)}, u32[]{:S(2)}) async-start(bf16[16,32,128]{2,1,0:T(8,128)(2,1)} %bitcast.2), calls=%async_computation | async-start | bytes 262144 | tf_op jit(solution)/shard_map/all_to_all | solution.py:353
  33.2 0.7 %copy-start.5 = (bf16[1024,128]{1,0:T(8,128)(2,1)}, bf16[1024,128]{1,0:T(8,128)(2,1)S(1)}, u32[]{:S(2)}) copy-start(bf16[1024,128]{1,0:T(8,128)(2,1)S(1)} %collective-permute-done.11) | copy-start | bytes 786436
  33.9 20.3 %copy-start = (bf16[3,1024,256]{2,1,0:T(8,128)(2,1)S(1)}, bf16[3,1024,256]{2,1,0:T(8,128)(2,1)}, u32[]{:S(2)}) copy-start(bf16[3,1024,256]{2,1,0:T(8,128)(2,1)} %sep_ref.3) | copy-start | bytes 4718596
  42.2 11.9 %all-to-all-start.1 = ((bf16[8,3,32,128]{3,2,1,0:T(8,128)(2,1)}), bf16[8,3,32,128]{3,2,1,0:T(8,128)(2,1)S(1)}, u32[]{:S(2)}, u32[]{:S(2)}) async-start(bf16[8,3,32,128]{3,2,1,0:T(8,128)(2,1)} %shard_map.68), calls=%async_computation.1 | async-start | bytes 393216 | tf_op jit(solution)/shard_map/all_to_all | solution.py:366
  45.6 6.2 %collective-permute-start.12 = (bf16[1,2,128,256]{3,2,1,0:T(8,128)(2,1)}, bf16[1,2,128,256]{3,2,1,0:T(8,128)(2,1)S(1)}, u32[]{:S(2)}, u32[]{:S(2)}) collective-permute-start(bf16[1,2,128,256]{3,2,1,0:T(8,128)(2,1)} %add.19), channel_id=1, source_target_pairs={{0,1},{1,0},{2,3},{3,2},{4,5},{5,4},{6,7},{7,6},{8,9},{9,8},{10,11... | collective-permute-start | bytes 393224 | tf_op jit(solution)/shard_map/ppermute | solution.py:35
  47.6 6.6 %collective-permute-start.14 = (bf16[1024,128]{1,0:T(8,128)(2,1)S(1)}, bf16[1024,128]{1,0:T(8,128)(2,1)S(1)}, u32[]{:S(2)}, u32[]{:S(2)}) collective-permute-start(bf16[1024,128]{1,0:T(8,128)(2,1)S(1)} %add_convert_fusion.refs_0_), channel_id=1, source_target_pairs={{0,16},{8,24},{16,0},{24,8},{1,17},{9,25},{17,1},{25,9},{2,18},{10... | collective-permute-start | bytes 786440 | tf_op jit(solution)/shard_map/ppermute | solution.py:35
  52.7 1.4 %collective-permute-start.13 = (bf16[1,2,128,256]{3,2,1,0:T(8,128)(2,1)S(1)}, bf16[1,2,128,256]{3,2,1,0:T(8,128)(2,1)S(1)}, u32[]{:S(2)}, u32[]{:S(2)}) collective-permute-start(bf16[1,2,128,256]{3,2,1,0:T(8,128)(2,1)S(1)} %add.23.refs_0_), channel_id=1, source_target_pairs={{0,8},{8,0},{16,24},{24,16},{1,9},{9,1},{17,25},{25,17},{2,10},{10... | collective-permute-start | bytes 393224 | tf_op jit(solution)/shard_map/ppermute | solution.py:35
